TPU v7x, 256 devices: a whole 4x4x8 slice. The times are simulated.
256 devices in a mesh: seq: 32 (over y, z), head: 8 (over x, core).
Axes of the slice: x: 4, y: 4, z: 8, core: 2. Of those that a mesh axis runs over, the one named last changes fastest.
Arguments:
- query_states: bfloat16 [1, 24576, 3072], P(None, 'seq', 'head'), may hold values from -8 to 8
- key_states: bfloat16 [1, 24576, 3072], P(None, 'seq', 'head'), may hold values from -8 to 8
- value_states: bfloat16 [1, 24576, 3072], P(None, 'seq', 'head'), may hold values from -6 to 6
- spatial_mask: int32 [16, 12, 12], replicated, may hold values from 0 to 1, as said below
- temporal_mask: int32 [12, 16, 16], replicated, may hold values from 0 to 1, as said below
- temporal_heads: int32 [8], P('head'), may hold values from 0 to 23, as said below
- out_weight: bfloat16 [3072, 3072], P('head', 'seq'), may hold values from -0.109375 to 0.109375
Outputs:
- projected: bfloat16 [1, 24576, 3072], P(None, 'seq', 'head')
Inputs may be any that keep to these rules, and one draw needn't show every extreme that they name: `temporal_heads`: entries i * 1 to (i + 1) - 1 are distinct heads among i * 3 to (i + 1) * 3 - 1. `spatial_mask`: diagonal blocks are 1. `temporal_mask`: entries whose two frames are at most one apart are 1.
All inputs are finite; a program needn't handle non-finite values.
Results may differ from a plain program's by a relative error of at most 0.0057.
Values may be sent and summed in bfloat16 or wider, within the bound.
No kernel may reach another device: no remote copies, remote signals or barrier semaphores. Data moves between devices by JAX's collectives and lax.ppermute only.
A program may use at most 64 MiB of HBM per device.

v0:
```python
import math

import jax
import jax.numpy as jnp
from jax import lax
from jax.sharding import PartitionSpec as P

HD = 128
BLOCK = 128


def partner(block, axis, apart):
    count = lax.axis_size(axis)
    route = []
    for low in range(count):
        high = low | 1 << apart
        if high != low and high < count:
            route += [(low, high), (high, low)]
    return lax.ppermute(block, axis, route)


def normalize(scores):
    row_max = jnp.max(scores, axis=-1, keepdims=True)
    lifted = jnp.exp(scores - row_max)
    return (lifted / jnp.sum(lifted, axis=-1, keepdims=True)).astype(jnp.bfloat16)


def frame_attention(queries, key_rows, value_rows, allowed):
    score_scale = 1.0 / math.sqrt(HD)
    scores = jnp.dot(queries, key_rows.T, preferred_element_type=jnp.float32) * score_scale
    scores = jnp.where(allowed, scores, -jnp.inf)
    probabilities = normalize(scores)
    return jnp.dot(probabilities, value_rows, preferred_element_type=jnp.float32).astype(
        jnp.bfloat16
    )


def shards(
    query_states, key_states, value_states, spatial_mask, temporal_mask, temporal_heads, out_weight
):
    clip_count, tok_rows, width = query_states.shape
    head_dev = width // HD
    temp_dev = temporal_heads.shape[0]
    spat_dev = head_dev - temp_dev
    seq_count = lax.axis_size("seq")
    seq_index = lax.axis_index("seq")
    head_index = lax.axis_index("head")
    frame_count = spatial_mask.shape[0]
    block_count = spatial_mask.shape[1]
    parity = seq_index % 2
    frame_id = seq_index // 2
    score_scale = 1.0 / math.sqrt(HD)
    slots = jnp.arange(head_dev, dtype=jnp.int32)
    local_temp = temporal_heads - head_index * head_dev
    temp_pick = local_temp[:, None] == slots[None, :]
    is_temp = jnp.any(temp_pick, axis=0)
    spat_rank = jnp.cumsum(1 - is_temp.astype(jnp.int32)) - 1
    spat_pick = jnp.logical_and(
        jnp.logical_not(is_temp)[None, :],
        spat_rank[None, :] == jnp.arange(spat_dev, dtype=jnp.int32)[:, None],
    )
    temp_select = temp_pick.astype(query_states.dtype)
    spat_select = spat_pick.astype(query_states.dtype)

    def select(states, chooser):
        shaped = states.reshape(clip_count, tok_rows, head_dev, HD)
        return jnp.einsum(
            "bthd,sh->btsd", shaped, chooser, preferred_element_type=jnp.float32
        ).astype(query_states.dtype)

    q_spatial = select(query_states, spat_select)
    local_kv = jnp.stack([select(key_states, spat_select), select(value_states, spat_select)])
    partner_kv = partner(local_kv, "seq", 0)
    whole_kv = jnp.where(
        parity == 0,
        jnp.concatenate([local_kv, partner_kv], axis=2),
        jnp.concatenate([partner_kv, local_kv], axis=2),
    )
    q_blocks = tok_rows // BLOCK
    mask_rows = lax.dynamic_slice(
        spatial_mask, (frame_id, parity * q_blocks, jnp.int32(0)), (1, q_blocks, block_count)
    )[0]
    allowed = jnp.repeat(jnp.repeat(mask_rows > 0, BLOCK, axis=0), BLOCK, axis=1)
    flat_q = q_spatial.transpose(0, 2, 1, 3).reshape(clip_count * spat_dev, tok_rows, HD)
    flat_k = whole_kv[0].transpose(0, 2, 1, 3).reshape(clip_count * spat_dev, 2 * tok_rows, HD)
    flat_v = whole_kv[1].transpose(0, 2, 1, 3).reshape(clip_count * spat_dev, 2 * tok_rows, HD)
    spat_out = lax.map(
        lambda members: frame_attention(members[0], members[1], members[2], allowed),
        (flat_q, flat_k, flat_v),
    )
    spat_out = spat_out.reshape(clip_count, spat_dev, tok_rows, HD).transpose(0, 2, 1, 3)
    positions = tok_rows // seq_count
    packed = jnp.stack(
        [
            select(query_states, temp_select),
            select(key_states, temp_select),
            select(value_states, temp_select),
        ]
    )
    packed = packed.reshape(3, clip_count, seq_count, positions, temp_dev * HD)
    owned = lax.all_to_all(packed, "seq", split_axis=2, concat_axis=2, tiled=True)
    owned = owned.reshape(3, clip_count, frame_count, 2, positions, temp_dev, HD)
    spot = (
        jnp.arange(2, dtype=jnp.int32)[:, None] * tok_rows
        + seq_index * positions
        + jnp.arange(positions, dtype=jnp.int32)[None, :]
    ) // BLOCK
    one_hot = (spot[:, :, None] == jnp.arange(block_count, dtype=jnp.int32)[None, None, :]).astype(
        jnp.float32
    )
    time_mask = (
        jnp.einsum(
            "hin,nfg->hifg",
            one_hot,
            temporal_mask.astype(jnp.float32),
            precision=lax.Precision.HIGHEST,
        )
        > 0.5
    )
    time_scores = (
        jnp.einsum("bfhitd,bghitd->bhitfg", owned[0], owned[1], preferred_element_type=jnp.float32)
        * score_scale
    )
    time_scores = jnp.where(time_mask[None, :, :, None, :, :], time_scores, -jnp.inf)
    time_probs = normalize(time_scores)
    time_result = jnp.einsum(
        "bhitfg,bghitd->bfhitd", time_probs, owned[2], preferred_element_type=jnp.float32
    ).astype(jnp.bfloat16)
    time_result = time_result.reshape(clip_count, seq_count, positions, temp_dev * HD)
    returned = lax.all_to_all(time_result, "seq", split_axis=1, concat_axis=1, tiled=True)
    temp_out = returned.reshape(clip_count, tok_rows, temp_dev, HD)
    attended = jnp.einsum(
        "btsd,sh->bthd", spat_out, spat_select, preferred_element_type=jnp.float32
    )
    attended = attended + jnp.einsum(
        "btsd,sh->bthd", temp_out, temp_select, preferred_element_type=jnp.float32
    )
    attended = attended.astype(jnp.bfloat16).reshape(clip_count, tok_rows, width)
    weight_rows = lax.all_gather(out_weight, "seq", axis=1, tiled=True)
    partial_sum = jnp.dot(attended[0], weight_rows, preferred_element_type=jnp.float32)
    pieces = [lax.psum_scatter(partial_sum, "head", scatter_dimension=1, tiled=True)]
    projected = jnp.stack(pieces).astype(jnp.bfloat16)
    return projected


def solution(mesh):
    in_specs = (
        P(None, "seq", "head"),
        P(None, "seq", "head"),
        P(None, "seq", "head"),
        P(),
        P(),
        P("head"),
        P("head", "seq"),
    )
    out_specs = P(None, "seq", "head")
    return jax.shard_map(shards, mesh=mesh, in_specs=in_specs, out_specs=out_specs, check_vma=False)
```

profile of v0, /device:TPU:1, one launch (start us, length us, event | category | flops | bytes accessed | tf_op | source)
XLA Modules:
  0.0 175.4 jit_solution(17428825261752885467)
XLA Ops:
  6.5 0.7 all-gather.2.cloned.1.call-update
  7.9 1.3 copy.38
  9.2 0.6 copy.39
  10.7 0.6 copy.41
  11.3 0.6 fusion.47
  12.2 0.6 copy.43
  12.8 0.6 fusion.45
  13.4 0.9 pad_maximum_fusion.1
  14.2 12.0 %all-to-all-start = ((bf16[3,1,32,24,128]{4,3,1,0,2:T(8,128)(2,1)}), bf16[3,1,32,24,128]{4,3,1,0,2:T(8,128)(2,1)S(1)}, u32[]{:S(2)}, u32[]{:S(2)}) async-start(bf16[3,1,32,24,128]{4,3,1,0,2:T(8,128)(2,1)} %pad_maximum_fusion.1), calls=%async_computation | async-start | bytes 1179648 | tf_op jit(solution)/shard_map/all_to_all | solution.py:101
  27.1 0.6 fusion.19
  27.6 1.1 pad_maximum_fusion
  28.8 1.5 collective-permute-start
  30.7 0.6 convolution_convert_fusion.2
  31.7 28.8 %collective-permute-done = bf16[2,1,768,2,128]{4,3,2,1,0:T(2,128)(2,1)} collective-permute-done((bf16[2,1,768,2,128]{4,3,2,1,0:T(2,128)(2,1)S(1)}, bf16[2,1,768,2,128]{4,3,2,1,0:T(2,128)(2,1)}, u32[]{:S(2)}, u32[]{:S(2)}) %collective-permute-start) | collective-permute-done | bytes 786464 | tf_op jit(solution)/shard_map/ppermute | solution.py:19
  60.6 14.9 %broadcast_select_fusion = bf16[2,1,1536,2,128]{4,3,2,1,0:T(2,128)(2,1)S(1)} fusion(pred[]{:T(512)S(6)} %eq.102, bf16[2,1,768,2,128]{4,3,2,1,0:T(2,128)(2,1)} %collective-permute-done, bf16[1,1,768,2,128]{4,3,2,1,0:T(2,128)(2,1)S(1)} %fusion.19, bf16[1,1,768,2,128]{4,3,2,1,0:T(2,128)(2,1)S(1)} %fusion.18), kind=kLoop, calls=%fused_computation.18 | loop fusion | flops 3932160 | bytes 3145729 | tf_op jit(solution)/shard_map/jit(_where)/select_n | solution.py:74
  75.5 1.1 slice_bitcast_fusion
  78.1 0.7 copy.59
  78.9 8.7 %all-to-all-start.1 = ((bf16[1,32,24,128]{3,2,0,1:T(8,128)(2,1)}), bf16[1,32,24,128]{3,2,0,1:T(8,128)(2,1)S(1)}, u32[]{:S(2)}, u32[]{:S(2)}) async-start(bf16[1,32,24,128]{3,2,0,1:T(8,128)(2,1)} %bitcast.48), calls=%async_computation.1 | async-start | bytes 393216 | tf_op jit(solution)/shard_map/all_to_all | solution.py:130
  87.8 9.0 %while.11 = (s32[]{:T(128)}, bf16[2,768,128]{2,1,0:T(8,128)(2,1)S(1)}, bf16[2,768,128]{2,1,0:T(8,128)(2,1)S(1)}, bf16[2,1536,128]{2,1,0:T(8,128)(2,1)S(1)}, bf16...) while((s32[]{:T(128)}, bf16[2,768,128]{2,1,0:T(8,128)(2,1)S(1)}, ...), condition=%wide.region_4.5_spmd.clone, body=%wide.region_1.4_spmd.clone.sunk | while | flops 613513728 | bytes 20082772 | solution.py:87
  88.1 1.3 copy.83
  89.4 1.0 fusion.76
  90.5 0.8 fusion.77
  91.3 1.1 fusion.78
  92.6 1.3 copy.83
  93.9 1.0 fusion.76
  95.0 0.8 fusion.77
  95.8 1.0 fusion.78
  97.1 1.0 fusion.16
  98.1 0.6 copy.61
  98.7 6.7 %fusion.61 = f32[768,3072]{1,0:T(8,128)} fusion(bf16[768,384]{0,1:T(8,128)(2,1)S(1)} %bitcast.149, bf16[384,3072]{0,1:T(8,128)(2,1)} %all-gather.2.cloned.1.call-done), kind=kOutput, calls=%fused_computation.93 | convolution fusion | flops 1811939328 | bytes 12386304 | tf_op jit(solution)/shard_map/dot_general | solution.py:140
  105.5 61.0 %reduce-scatter.2.cloned.1.call-done = f32[768,384]{1,0:T(8,128)} async-done(((f32[768,3072]{1,0:T(8,128)}), f32[768,384]{1,0:T(8,128)}) %reduce-scatter.2.cloned.1.call-update) | async-done | bytes 1179664 | tf_op jit(solution)/shard_map/reduce_scatter | solution.py:141
  166.4 2.1 %convert_bitcast_fusion = bf16[1,768,384]{2,1,0:T(8,128)(2,1)} fusion(f32[768,384]{1,0:T(8,128)} %reduce-scatter.2.cloned.1.call-done), kind=kLoop, calls=%fused_computation.39 | loop fusion | flops 294912 | bytes 1769472 | tf_op jit(solution)/shard_map/convert_element_type | solution.py:142
  (54 shorter events, 5.3 us)
Async XLA Ops:
  6.5 23.7 %copy-start = (s32[16,12,12]{2,0,1:T(8,128)S(1)}, s32[16,12,12]{2,0,1:T(8,128)}, u32[]{:S(2)}) copy-start(s32[16,12,12]{2,0,1:T(8,128)} %param.12) | copy-start | bytes 27652
  6.5 92.2 %all-gather.2.cloned.1.call-start = ((), (), s32[]{:S(2)}) async-start(), calls=%async_computation.3 | async-start | bytes 2433024 | tf_op jit(solution)/shard_map/all_gather | solution.py:139
  9.2 1.2 copy-start.1
  10.7 1.2 copy-start.2
  14.2 62.6 %all-to-all-start = ((bf16[3,1,32,24,128]{4,3,1,0,2:T(8,128)(2,1)}), bf16[3,1,32,24,128]{4,3,1,0,2:T(8,128)(2,1)S(1)}, u32[]{:S(2)}, u32[]{:S(2)}) async-start(bf16[3,1,32,24,128]{4,3,1,0,2:T(8,128)(2,1)} %pad_maximum_fusion.1), calls=%async_computation | async-start | bytes 1179648 | tf_op jit(solution)/shard_map/all_to_all | solution.py:101
  27.1 3.5 %copy-start.3 = (s32[12,16,16]{2,1,0:T(8,128)S(1)}, s32[12,16,16]{2,1,0:T(8,128)}, u32[]{:S(2)}) copy-start(s32[12,16,16]{2,1,0:T(8,128)} %param.13) | copy-start | bytes 36868
  28.8 31.8 %collective-permute-start = (bf16[2,1,768,2,128]{4,3,2,1,0:T(2,128)(2,1)S(1)}, bf16[2,1,768,2,128]{4,3,2,1,0:T(2,128)(2,1)}, u32[]{:S(2)}, u32[]{:S(2)}) collective-permute-start(bf16[2,1,768,2,128]{4,3,2,1,0:T(2,128)(2,1)S(1)} %pad_maximum_fusion), channel_id=1, source_target_pairs={{0,8},{8,0},{16,24},{24,16},{32,40},{40,32},{48,56},{56,48},{64,72... | collective-permute-start | bytes 2359304 | tf_op jit(solution)/shard_map/ppermute | solution.py:19
  77.6 10.2 %copy-start.4 = (bf16[2,768,128]{2,1,0:T(8,128)(2,1)S(1)}, bf16[2,768,128]{2,1,0:T(8,128)(2,1)}, u32[]{:S(2)}) copy-start(bf16[2,768,128]{2,1,0:T(8,128)(2,1)} %custom-call) | copy-start | bytes 1179652
  78.9 18.2 %all-to-all-start.1 = ((bf16[1,32,24,128]{3,2,0,1:T(8,128)(2,1)}), bf16[1,32,24,128]{3,2,0,1:T(8,128)(2,1)S(1)}, u32[]{:S(2)}, u32[]{:S(2)}) async-start(bf16[1,32,24,128]{3,2,0,1:T(8,128)(2,1)} %bitcast.48), calls=%async_computation.1 | async-start | bytes 393216 | tf_op jit(solution)/shard_map/all_to_all | solution.py:130
  87.5 78.9 %reduce-scatter.2.cloned.1.call-start = ((), (), s32[]{:S(2)}) async-start(), calls=%async_computation.4 | async-start | bytes 10616832 | tf_op jit(solution)/shard_map/reduce_scatter | solution.py:141
Sparse Core Ops, SparseCore 0:
  9.9 79.2 all-gather.1
  105.6 60.7 reduce-scatter.1
where the time goes:
time: 176 us; the launch traced here: 175 us
  waiting for transfers between devices  90.7 us (52%)
  starting transfers between devices  22.5 us (13%)
  other arithmetic  21.2 us (12%)
  matrix products  16 us (9%)
  between operations  14.5 us (8%)
  local copies, waits for them, and re-layouts  10.5 us (6%)
    reduce_scatter x1, waiting for transfers between devices, shards(): lax.psum_scatter(partial_sum, 'head', scatter_dimension=1, tiled=True)  61 us
    ppermute x1, waiting for transfers between devices, partner(): return lax.ppermute(block, axis, route)  28.8 us
    select_n x1, other arithmetic, shards(): jnp.where(parity == 0, jnp.concatenate([local_kv, partner_kv], axis=2), j...  14.9 us
    all_to_all x1, starting transfers between devices, shards(): lax.all_to_all(packed, 'seq', split_axis=2, concat_axis=2, tiled=True)  12 us
    all_to_all x1, starting transfers between devices, shards(): lax.all_to_all(time_result, 'seq', split_axis=1, concat_axis=1, tiled=True)  8.66 us
    dot_general x1, matrix products, shards(): jnp.dot(attended[0], weight_rows, preferred_element_type=jnp.float32)  6.75 us
  transfers between devices with their start and end apart: 5, of which 3 were waited for; matrix products, arithmetic and copies ran while one was open for 22% of the time, Pallas kernels for 0%

commit v1 on v0

v1 whole, which is shorter than its diff:
```python
import functools
import math

import jax
import jax.numpy as jnp
import numpy as np
from jax import lax
from jax.experimental import pallas as pl
from jax.experimental.pallas import tpu as pltpu
from jax.sharding import PartitionSpec as P

HD = 128
BLOCK = 128
VMEM = 56 * 1024 * 1024
BF16 = jnp.bfloat16
F32 = jnp.float32
LOG2E = math.log2(math.e)
SCALE2 = LOG2E / math.sqrt(HD)
NT = (((1,), (1,)), ((), ()))


def dot_nt(a, b):
    return lax.dot_general(a, b, NT, preferred_element_type=F32)


def dot_nn(a, b):
    return jnp.dot(a, b, preferred_element_type=F32)


def params():
    return pltpu.CompilerParams(vmem_limit_bytes=VMEM)


def cost(flops, moved):
    return pl.CostEstimate(flops=flops, bytes_accessed=moved, transcendentals=0)


def pick_columns(order, sources, rows):
    arrays = [a for a, _ in sources]
    total = arrays[0].shape[0]
    count = len(sources)

    def body(order_ref, *refs):
        out = refs[-1]
        for n in range(count):
            out[:, n * HD : (n + 1) * HD] = refs[n][...]

    return pl.pallas_call(
        body,
        out_shape=jax.ShapeDtypeStruct((total, count * HD), BF16),
        grid_spec=pltpu.PrefetchScalarGridSpec(
            num_scalar_prefetch=1,
            grid=(total // rows,),
            in_specs=[
                pl.BlockSpec((rows, HD), functools.partial(lambda i, o, slot: (i, o[slot]), slot=slot))
                for _, slot in sources
            ],
            out_specs=pl.BlockSpec((rows, count * HD), lambda i, o: (i, 0)),
        ),
        compiler_params=params(),
        cost_estimate=cost(0, 4 * total * count * HD),
    )(order, *arrays)


def weight_blocks(order, weight):
    rows, cols = weight.shape

    def body(order_ref, w_ref, out_ref):
        for n in range(rows // HD):
            piece = w_ref[pl.ds(pl.multiple_of(order_ref[n] * HD, HD), HD), :]
            out_ref[:, n * HD : (n + 1) * HD] = piece.astype(F32).T.astype(BF16)

    return pl.pallas_call(
        body,
        out_shape=jax.ShapeDtypeStruct((cols, rows), BF16),
        in_specs=[pl.BlockSpec(memory_space=pltpu.SMEM), pl.BlockSpec(memory_space=pltpu.VMEM)],
        out_specs=pl.BlockSpec(memory_space=pltpu.VMEM),
        compiler_params=params(),
    )(order, weight)


def own_half(order, q, k, v, bias):
    rows = q.shape[0]
    tile = 256
    per = tile // BLOCK

    def body(order_ref, q_ref, k_ref, v_ref, bias_ref, o_ref, m_ref, l_ref):
        keys = k_ref[...]
        values = v_ref[...]
        for n in range(per):
            part = slice(n * BLOCK, (n + 1) * BLOCK)
            s = dot_nt(q_ref[part, :], keys) * SCALE2 + bias_ref[n]
            m = jnp.max(s, axis=1, keepdims=True)
            p = jnp.exp2(s - m)
            l = jnp.sum(p, axis=1, keepdims=True)
            o_ref[part, :] = dot_nn(p.astype(BF16), values)
            m_ref[part, :] = jnp.broadcast_to(m, (BLOCK, HD))
            l_ref[part, :] = jnp.broadcast_to(l, (BLOCK, HD))

    shape = jax.ShapeDtypeStruct((rows, 2 * HD), F32)
    out = pl.BlockSpec((tile, HD), lambda h, i, o: (i, h))
    return pl.pallas_call(
        body,
        out_shape=(shape, shape, shape),
        grid_spec=pltpu.PrefetchScalarGridSpec(
            num_scalar_prefetch=1,
            grid=(2, rows // tile),
            in_specs=[
                pl.BlockSpec((tile, HD), lambda h, i, o: (i, o[h])),
                pl.BlockSpec((rows, HD), lambda h, i, o: (0, o[h])),
                pl.BlockSpec((rows, HD), lambda h, i, o: (0, o[h])),
                pl.BlockSpec((per, 1, rows), lambda h, i, o: (i, 0, 0)),
            ],
            out_specs=(out, out, out),
        ),
        compiler_params=params(),
        cost_estimate=cost(8 * rows * rows * HD, 8 * rows * HD * 8),
    )(order, q, k, v, bias)


def other_half(order, q, kv, bias, o, m, l):
    rows = q.shape[0]
    tile = 256
    per = tile // BLOCK

    def body(order_ref, q_ref, k_ref, v_ref, bias_ref, o_ref, m_ref, l_ref, out_ref):
        keys = k_ref[...]
        values = v_ref[...]
        for n in range(per):
            part = slice(n * BLOCK, (n + 1) * BLOCK)
            s = dot_nt(q_ref[part, :], keys) * SCALE2 + bias_ref[n]
            before = m_ref[part, 0:1]
            m = jnp.maximum(before, jnp.max(s, axis=1, keepdims=True))
            p = jnp.exp2(s - m)
            keep = jnp.exp2(before - m)
            total = l_ref[part, 0:1] * keep + jnp.sum(p, axis=1, keepdims=True)
            mixed = o_ref[part, :] * keep + dot_nn(p.astype(BF16), values)
            out_ref[part, :] = (mixed / total).astype(BF16)

    mid = pl.BlockSpec((tile, HD), lambda h, i, o: (i, h))
    return pl.pallas_call(
        body,
        out_shape=jax.ShapeDtypeStruct((rows, 2 * HD), BF16),
        grid_spec=pltpu.PrefetchScalarGridSpec(
            num_scalar_prefetch=1,
            grid=(2, rows // tile),
            in_specs=[
                pl.BlockSpec((tile, HD), lambda h, i, o: (i, o[h])),
                pl.BlockSpec((rows, HD), lambda h, i, o: (0, h)),
                pl.BlockSpec((rows, HD), lambda h, i, o: (0, 2 + h)),
                pl.BlockSpec((per, 1, rows), lambda h, i, o: (i, 0, 0)),
                mid,
                mid,
                mid,
            ],
            out_specs=mid,
        ),
        compiler_params=params(),
        cost_estimate=cost(8 * rows * rows * HD, 8 * rows * HD * 8),
    )(order, q, kv, kv, bias, o, m, l)


def time_attention(owned, rule, frame_of, key_col, key_row):
    rows = owned.shape[0]
    tile = 256

    def body(all_ref, rule_ref, frame_ref, col_ref, row_ref, out_ref):
        start = pl.multiple_of(pl.program_id(0) * tile, tile)
        q = all_ref[pl.ds(start, tile), 0:HD]
        s = dot_nt(q, all_ref[:, HD : 2 * HD]) * SCALE2
        seen = dot_nn(rule_ref[...], frame_ref[...]) > 0.5
        allowed = jnp.logical_and(seen, col_ref[...] == row_ref[...])
        s = jnp.where(allowed, s, -jnp.inf)
        m = jnp.max(s, axis=1, keepdims=True)
        p = jnp.exp2(s - m)
        l = jnp.sum(p, axis=1, keepdims=True)
        out_ref[...] = (dot_nn(p.astype(BF16), all_ref[:, 2 * HD :]) / l).astype(BF16)

    frames = rule.shape[1]
    return pl.pallas_call(
        body,
        out_shape=jax.ShapeDtypeStruct((rows, HD), BF16),
        grid=(rows // tile,),
        in_specs=[
            pl.BlockSpec((rows, 3 * HD), lambda i: (0, 0)),
            pl.BlockSpec((tile, frames), lambda i: (i, 0)),
            pl.BlockSpec((frames, rows), lambda i: (0, 0)),
            pl.BlockSpec((tile, 1), lambda i: (i, 0)),
            pl.BlockSpec((1, rows), lambda i: (0, 0)),
        ],
        out_specs=pl.BlockSpec((tile, HD), lambda i: (i, 0)),
        compiler_params=params(),
        cost_estimate=cost(4 * rows * rows * HD, 8 * rows * HD),
    )(owned, rule, frame_of, key_col, key_row)


def project_spatial(which, parts, weights):
    rows, width = parts[0].shape
    count, cols, _ = weights.shape
    tile = 256

    def body(which_ref, *refs):
        out_ref = refs[-1]
        w_ref = refs[-2]
        total = None
        for n in range(count):
            term = dot_nt(refs[n][...], w_ref[which_ref[n]])
            total = term if total is None else total + term
        out_ref[...] = total

    return pl.pallas_call(
        body,
        out_shape=jax.ShapeDtypeStruct((rows, cols), F32),
        grid_spec=pltpu.PrefetchScalarGridSpec(
            num_scalar_prefetch=1,
            grid=(rows // tile,),
            in_specs=[pl.BlockSpec((tile, width), lambda i, o: (i, 0))] * count
            + [pl.BlockSpec((count, cols, width), lambda i, o: (0, 0, 0))],
            out_specs=pl.BlockSpec((tile, cols), lambda i, o: (i, 0)),
        ),
        compiler_params=params(),
        cost_estimate=cost(2 * rows * cols * width * count, 6 * rows * cols),
    )(which, *parts, weights)


def project_time(which, side, parts, weights, base, dtype):
    rows, width = parts[0].shape
    count, cols, all_rows = weights.shape
    half = cols // 2
    tile = 256
    last = all_rows // width - 1

    def body(which_ref, side_ref, *refs):
        out_ref = refs[-1]
        base_ref = refs[-2]
        w_ref = refs[-3]
        total = base_ref[...]
        for n in range(count):
            total = total + dot_nt(refs[n][...], w_ref[which_ref[n]])
        out_ref[...] = total.astype(dtype)

    return pl.pallas_call(
        body,
        out_shape=jax.ShapeDtypeStruct((rows, half), dtype),
        grid_spec=pltpu.PrefetchScalarGridSpec(
            num_scalar_prefetch=2,
            grid=(rows // tile,),
            in_specs=[pl.BlockSpec((tile, width), lambda i, o, s: (i, 0))] * count
            + [
                pl.BlockSpec((count, half, width), lambda i, o, s: (0, s[0], last)),
                pl.BlockSpec((tile, half), lambda i, o, s: (i, s[0])),
            ],
            out_specs=pl.BlockSpec((tile, half), lambda i, o, s: (i, 0)),
        ),
        compiler_params=params(),
        cost_estimate=cost(2 * rows * half * width * count, 6 * rows * half),
    )(which, side, *parts, weights, base)


def shards(
    shape_yzx,
    query_states,
    key_states,
    value_states,
    spatial_mask,
    temporal_mask,
    temporal_heads,
    out_weight,
):
    ys, zs, xs, cores = shape_yzx
    _, rows, width = query_states.shape
    heads_here = width // HD
    seq_count = ys * zs
    seq_index = lax.axis_index("seq")
    head_index = lax.axis_index("head")
    frames = spatial_mask.shape[0]
    blocks = spatial_mask.shape[1]
    x_index = head_index // cores
    core = head_index % cores
    q, k, v = query_states[0], key_states[0], value_states[0]

    temp = temporal_heads[0] - head_index * heads_here
    first = jnp.where(temp == 0, 1, 0)
    second = jnp.where(temp == 2, 1, 2)
    order = jnp.stack([first, second, temp]).astype(jnp.int32)

    swap = []
    for y in range(ys):
        for z in range(zs):
            for x in range(xs):
                for c in range(cores):
                    here = (y * zs + z) * xs * cores + x * cores + c
                    there = (x * zs + z) * xs * cores + y * cores + c
                    swap.append((here, there))
    w_own = lax.ppermute(weight_blocks(order, out_weight), ("seq", "head"), swap)
    w_all = lax.all_gather(w_own, "seq", axis=0, tiled=False)
    w_all = w_all.reshape(ys, zs * w_own.shape[0], width)

    kv = pick_columns(order, [(k, 0), (k, 1), (v, 0), (v, 1)], 256)
    kv_other = lax.ppermute(kv, "seq", [(s, s ^ 1) for s in range(seq_count)])

    packed = pick_columns(order, [(q, 2), (k, 2), (v, 2)], 256)
    positions = rows // seq_count
    owned = lax.all_to_all(packed.reshape(seq_count, positions, 3 * HD), "seq", 0, 0, tiled=True)
    owned = owned.reshape(rows, 3 * HD)

    parity = seq_index % 2
    mine = lax.dynamic_slice(
        spatial_mask,
        (seq_index // 2, parity * (blocks // 2), jnp.int32(0)),
        (1, blocks // 2, blocks),
    )[0]
    bias = jnp.where(mine > 0, 0.0, -jnp.inf).astype(F32)
    bias = jnp.where(parity == 0, bias, jnp.roll(bias, blocks // 2, axis=1))
    bias = jnp.repeat(bias, BLOCK, axis=1)[:, None, :]
    o, m, l = own_half(order, q, k, v, bias[:, :, :rows])
    spat = other_half(order, q, kv_other, bias[:, :, rows:], o, m, l)

    spot = np.arange(2)[:, None] * rows + np.arange(positions)[None, :]
    spot = (jnp.asarray(spot.reshape(-1), jnp.int32) + seq_index * positions) // BLOCK
    hot = (spot[:, None] == jnp.arange(blocks, dtype=jnp.int32)[None, :]).astype(BF16)
    rule = jnp.dot(
        hot, (temporal_mask > 0).reshape(blocks, -1).astype(BF16), preferred_element_type=F32
    )
    rule = rule.reshape(2 * positions, frames, frames).transpose(1, 0, 2)
    rule = rule.reshape(rows, frames).astype(BF16)
    index = np.arange(rows)
    frame_of = jnp.asarray(np.arange(frames)[:, None] == index[None, :] // (2 * positions), BF16)
    key = (index % (2 * positions)).astype(np.float32)
    time = time_attention(owned, rule, frame_of, jnp.asarray(key[:, None]), jnp.asarray(key[None]))
    returned = lax.all_to_all(time.reshape(seq_count, positions, HD), "seq", 0, 0, tiled=True)
    returned = returned.reshape(rows, HD)

    def along_x(block):
        got = [block]
        for step in range(1, xs):
            route = [(h, (h + step * cores) % (xs * cores)) for h in range(xs * cores)]
            got.append(lax.ppermute(block, "head", route))
        return got

    which = ((x_index + xs - jnp.arange(xs)) % xs).astype(jnp.int32)
    base = project_spatial(which, along_x(spat), w_all)
    time_parts = along_x(returned)
    mine_side = core.astype(jnp.int32).reshape(1)
    for_twin = project_time(which, 1 - mine_side, time_parts, w_all, base, BF16)
    from_twin = lax.ppermute(for_twin, "head", [(h, h ^ 1) for h in range(xs * cores)])
    own = project_time(which, mine_side, time_parts, w_all, base, F32)
    return (own + from_twin.astype(F32)).astype(BF16)[None]


def solution(mesh):
    in_specs = (
        P(None, "seq", "head"),
        P(None, "seq", "head"),
        P(None, "seq", "head"),
        P(),
        P(),
        P("head"),
        P("head", "seq"),
    )
    out_specs = P(None, "seq", "head")
    return jax.shard_map(
        functools.partial(shards, (4, 8, 4, 2)),
        mesh=mesh,
        in_specs=in_specs,
        out_specs=out_specs,
        check_vma=False,
    )
```

time: 176 us -> 147 us (0.84)
  waiting for transfers between devices: 90.7 us -> 35.9 us
  Pallas kernels: 0 us -> 45.2 us
  other arithmetic: 21.2 us -> 3.52 us
  starting transfers between devices: 22.5 us -> 38.6 us
  matrix products: 16 us -> 0.15 us
  local copies, waits for them, and re-layouts: 10.5 us -> 7.67 us
    reduce_scatter x1 -> x0, waiting for transfers between devices: 61 us -> none  [shards(): lax.psum_scatter(partial_sum, 'head', scatter_dimension=1, tiled=True)]
    pallas_call x0 -> x9, Pallas kernels: none -> 45.2 us  [the longest x2 9.31 us: project_time(): pl.pallas_call(body, out_shape=jax.ShapeDtypeStruct((rows, half), dtype),...]
    dot_general x15 -> x1, matrix products: 16 us -> 0.15 us  [shards(): jnp.dot(hot, (temporal_mask > 0).reshape(blocks, -1).astype(BF16), prefer...]
    select_n x2 -> x4, other arithmetic: 15 us -> 0.71 us  [the longest x1 0.61 us: shards(): which = ((x_index + xs - jnp.arange(xs)) % xs).astype(jnp.int32)]
    all_to_all x2, starting transfers between devices: 20.7 us -> 30.2 us  [the longest x1 21 us: shards(): lax.all_to_all(packed.reshape(seq_count, positions, 3 * HD), 'seq', 0, 0,...]
    all_to_all x2, waiting for transfers between devices: 0.19 us -> 7.92 us  [the longest x1 7.92 us: shards(): lax.all_to_all(time.reshape(seq_count, positions, HD), 'seq', 0, 0, tiled...]
    ppermute x1 -> x9, starting transfers between devices: 1.5 us -> 8.43 us  [the longest x6 4.93 us: along_x(): got.append(lax.ppermute(block, 'head', route))]
    reshape x3 -> x1, local copies, waits for them, and re-layouts: 3.73 us -> 0.11 us  [shards(): (temporal_mask > 0).reshape(blocks, -1).astype(BF16)]
  transfers between devices with their start and end apart: 5 -> 12, of which waited for: 3 -> 4; matrix products, arithmetic and copies ran while one was open for 22% -> 2% of each run, Pallas kernels for 0% -> 27%
where the time goes in v1:
time: 147 us; the launch traced here: 145 us
  Pallas kernels  45.2 us (31%)
  starting transfers between devices  38.6 us (26%)
  waiting for transfers between devices  35.9 us (24%)
  between operations  14.3 us (10%)
  local copies, waits for them, and re-layouts  7.67 us (5%)
  other arithmetic  3.52 us (2%)
    all_to_all x1, starting transfers between devices, shards(): lax.all_to_all(packed.reshape(seq_count, positions, 3 * HD), 'seq', 0, 0,...  21 us
    ppermute x1, waiting for transfers between devices, shards(): kv_other = lax.ppermute(kv, 'seq', [(s, s ^ 1) for s in range(seq_count)])  18.7 us
    pallas_call x2, Pallas kernels, project_time(): pl.pallas_call(body, out_shape=jax.ShapeDtypeStruct((rows, half), dtype),...  9.31 us
    ppermute x6, waiting for transfers between devices, along_x(): got.append(lax.ppermute(block, 'head', route))  9.29 us
    all_to_all x1, starting transfers between devices, shards(): lax.all_to_all(time.reshape(seq_count, positions, HD), 'seq', 0, 0, tiled...  9.2 us
    pallas_call x1, Pallas kernels, other_half(): pl.pallas_call(body, out_shape=jax.ShapeDtypeStruct((rows, 2 * HD), BF16)...  9.09 us
    all_to_all x1, waiting for transfers between devices, shards(): lax.all_to_all(time.reshape(seq_count, positions, HD), 'seq', 0, 0, tiled...  7.92 us
    pallas_call x1, Pallas kernels, own_half(): pl.pallas_call(body, out_shape=(shape, shape, shape), grid_spec=pltpu.Pre...  7.74 us
  transfers between devices with their start and end apart: 12, of which 4 were waited for; matrix products, arithmetic and copies ran while one was open for 2% of the time, Pallas kernels for 27%

profile of v1, /device:TPU:1, one launch (start us, length us, event | category | flops | bytes accessed | tf_op | source)
XLA Modules:
  0.0 145.3 jit_solution(5161879905786585300)
XLA Ops:
  7.2 1.6 %copy.14.w_ref = bf16[384,96]{1,0:T(8,128)(2,1)} copy(bf16[384,96]{0,1:T(8,128)(2,1)} %param.17) | data formatting | bytes 147456 | tf_op args[6]
  8.9 0.6 pad_add_fusion.order_ref
  9.5 1.6 %shard_map.111 = bf16[96,384]{1,0:T(8,128)(2,1)} custom-call(s32[3]{0:T(128)} %pad_add_fusion.order_ref, bf16[384,96]{1,0:T(8,128)(2,1)} %copy.14.w_ref), custom_call_target="tpu_custom_call" | custom-call | tf_op jit(solution)/shard_map/pallas_call | solution.py:73
  11.1 1.5 %collective-permute-start.3 = (bf16[96,384]{1,0:T(8,128)(2,1)}, bf16[96,384]{1,0:T(8,128)(2,1)S(1)}, u32[]{:S(2)}, u32[]{:S(2)}) collective-permute-start(bf16[96,384]{1,0:T(8,128)(2,1)} %shard_map.111), channel_id=1, source_target_pairs={{0,0},{1,1},{2,64},{3,65},{4,128},{5,129},{6,192},{7,193},{8,8},{9... | collective-permute-start | bytes 221192 | tf_op jit(solution)/shard_map/ppermute | solution.py:295
  12.6 0.6 copy-done.12
  13.3 3.4 %shard_map.109 = bf16[768,384]{1,0:T(8,128)(2,1)} custom-call(s32[3]{0:T(128)} %pad_add_fusion.order_ref, bf16[768,384]{1,0:T(8,128)(2,1)} %bitcast.40, bf16[768,384]{1,0:T(8,128)(2,1)} %bitcast.32, bf16[768,384]{1,0:T(8,128)(2,1)} %bitcast.36), custom_call_target="tpu_custom_call" | custom-call | bytes 1179648 | tf_op jit(solution)/shard_map/pallas_call | solution.py:48
  16.7 21.0 %all-to-all-start = ((bf16[32,24,384]{2,1,0:T(8,128)(2,1)}), bf16[32,24,384]{2,1,0:T(8,128)(2,1)S(1)}, u32[]{:S(2)}, u32[]{:S(2)}) async-start(bf16[32,24,384]{2,1,0:T(8,128)(2,1)} %bitcast.43), calls=%async_computation | async-start | bytes 1179648 | tf_op jit(solution)/shard_map/all_to_all | solution.py:304
  37.7 3.7 %shard_map.112 = bf16[768,512]{1,0:T(8,128)(2,1)} custom-call(s32[3]{0:T(128)} %pad_add_fusion.order_ref, bf16[768,384]{1,0:T(8,128)(2,1)} %bitcast.33, bf16[768,384]{1,0:T(8,128)(2,1)} %bitcast.34, bf16[768,384]{1,0:T(8,128)(2,1)} %bitcast.37, bf16[768,384]{1,0:T(8,128)(2,1)} %bitcast.38), custom_call_target="tpu_custom_call" | custom-call | bytes 1572864 | tf_op jit(solution)/shard_map/pallas_call | solution.py:48
  41.5 1.2 collective-permute-start.4
  43.5 0.8 copy.13
  44.3 0.6 fusion.6
  44.9 7.7 %shard_map.113 = (f32[768,256]{1,0:T(8,128)}, f32[768,256]{1,0:T(8,128)}, f32[768,256]{1,0:T(8,128)}) custom-call(s32[3]{0:T(128)} %pad_add_fusion.order_ref, bf16[768,384]{1,0:T(8,128)(2,1)} %bitcast.41, bf16[768,384]{1,0:T(8,128)(2,1)} %bitcast.35, bf16[768,384]{1,0:T(8,128)(2,1)} %bitcast.39, f32[6,1,768]{2,1,0:T(1,128)} %get-tuple-element.11.bias_ref), custom_call_target="tpu_custom_call" | custom-call | flops 603979776 | bytes 6291456 | tf_op jit(solution)/shard_map/pallas_call | solution.py:102
  52.6 18.7 %collective-permute-done.4.k_ref.v_ref = bf16[768,512]{1,0:T(8,128)(2,1)S(1)} collective-permute-done((bf16[768,512]{1,0:T(8,128)(2,1)}, bf16[768,512]{1,0:T(8,128)(2,1)S(1)}, u32[]{:S(2)}, u32[]{:S(2)}) %collective-permute-start.4) | collective-permute-done | bytes 786464 | tf_op jit(solution)/shard_map/ppermute | solution.py:300
  71.3 0.9 copy-done.1
  72.2 9.1 %shard_map.114.refs_0_ = bf16[768,256]{1,0:T(8,128)(2,1)} custom-call(s32[3]{0:T(128)} %pad_add_fusion.order_ref, bf16[768,384]{1,0:T(8,128)(2,1)} %bitcast.42, bf16[768,512]{1,0:T(8,128)(2,1)} %copy-done.1, bf16[768,512]{1,0:T(8,128)(2,1)} %copy-done.1, f32[6,1,768]{2,1,0:T(1,128)} %get-tuple-element.12.bias_ref, f32[768,256]{1,0:T(8,128)} %get-tuple-element.8.o_ref, ...), custom_call_target="tpu_custom_call" | custom-call | flops 603979776 | bytes 6291456 | tf_op jit(solution)/shard_map/pallas_call | solution.py:141
  81.4 0.8 copy-done.2
  82.2 4.3 %shard_map.110 = bf16[768,128]{1,0:T(8,128)(2,1)} custom-call(bf16[768,384]{1,0:T(8,128)(2,1)} %bitcast.44, bf16[768,16]{1,0:T(8,128)(2,1)} %bitcast.51, bf16[16,768]{1,0:T(8,128)(2,1)} %constant.99.clone.frame_ref, f32[768,1]{1,0:T(8,128)} %constant.100.clone.col_ref, f32[1,768]{1,0:T(1,128)} %constant.101.clone.row_ref), custom_call_target="tpu_custom_call" | custom-call | flops 301989888 | bytes 786432 | tf_op jit(solution)/shard_map/pallas_call | solution.py:180
  86.5 9.2 %all-to-all-start.1 = ((bf16[32,24,128]{2,1,0:T(8,128)(2,1)}), bf16[32,24,128]{2,1,0:T(8,128)(2,1)S(1)}, u32[]{:S(2)}, u32[]{:S(2)}) async-start(bf16[32,24,128]{2,1,0:T(8,128)(2,1)} %bitcast.50), calls=%async_computation.1 | async-start | bytes 393216 | tf_op jit(solution)/shard_map/all_to_all | solution.py:331
  95.7 0.8 collective-permute-start.6
  96.5 0.8 collective-permute-start.5
  97.3 7.9 %all-to-all-done.1 = bf16[32,24,128]{2,1,0:T(8,128)(2,1)S(1)} async-done(((bf16[32,24,128]{2,1,0:T(8,128)(2,1)}), bf16[32,24,128]{2,1,0:T(8,128)(2,1)S(1)}, u32[]{:S(2)}, u32[]{:S(2)}) %all-to-all-start.1) | async-done | bytes 196640 | tf_op jit(solution)/shard_map/all_to_all | solution.py:331
  105.2 3.3 %collective-permute-start.1 = (bf16[768,128]{1,0:T(8,128)(2,1)S(1)}, bf16[768,128]{1,0:T(8,128)(2,1)S(1)}, u32[]{:S(2)}, u32[]{:S(2)}) collective-permute-start(bf16[768,128]{1,0:T(8,128)(2,1)S(1)} %bitcast.46), channel_id=1, source_target_pairs={{0,4},{1,5},{2,6},{3,7},{4,0},{5,1},{6,2},{7,3},{8,12},{9,13},{10,... | collective-permute-start | bytes 589832 | tf_op jit(solution)/shard_map/ppermute | solution.py:338
  108.5 0.6 and_select_fusion.1.which_ref
  109.2 8.9 %collective-permute-done.5.refs_1_ = bf16[768,256]{1,0:T(8,128)(2,1)S(1)} collective-permute-done((bf16[768,256]{1,0:T(8,128)(2,1)S(1)}, bf16[768,256]{1,0:T(8,128)(2,1)S(1)}, u32[]{:S(2)}, u32[]{:S(2)}) %collective-permute-start.5) | collective-permute-done | bytes 393248 | tf_op jit(solution)/shard_map/ppermute | solution.py:338
  118.1 0.7 copy-done.10
  118.8 5.9 %shard_map.115.refs_5_ = f32[768,768]{1,0:T(8,128)} custom-call(s32[4]{0:T(128)} %and_select_fusion.1.which_ref, bf16[768,256]{1,0:T(8,128)(2,1)} %shard_map.114.refs_0_, bf16[768,256]{1,0:T(8,128)(2,1)} %copy-done.10, bf16[768,256]{1,0:T(8,128)(2,1)} %copy-done.9, bf16[768,256]{1,0:T(8,128)(2,1)} %copy-done.8, bf16[4,768,384]{2,1,0:T(8,128)(2,1)} %bitcast.29), custom_call_target="tpu_custom_call" | custom-call | flops 1207959552 | bytes 3538944 | tf_op jit(solution)/shard_map/pallas_call | solution.py:211
  124.8 0.4 collective-permute-done.refs_1_
  125.5 0.7 copy-done.7
  126.2 4.6 %shard_map.117 = bf16[768,384]{1,0:T(8,128)(2,1)} custom-call(s32[4]{0:T(128)} %and_select_fusion.1.which_ref, s32[1]{0:T(128)S(6)} %sub.31.side_ref, bf16[768,128]{1,0:T(8,128)(2,1)} %bitcast.48, bf16[768,128]{1,0:T(8,128)(2,1)} %copy-done.7, bf16[768,128]{1,0:T(8,128)(2,1)} %copy-done.6, bf16[768,128]{1,0:T(8,128)(2,1)} %copy-done.5, ...), custom_call_target="tpu_custom_call" | custom-call | flops 301989888 | bytes 1769472 | tf_op jit(solution)/shard_map/pallas_call | solution.py:242
  130.8 0.7 collective-permute-start.8
  131.5 4.7 %shard_map.116 = f32[768,384]{1,0:T(8,128)} custom-call(s32[4]{0:T(128)} %and_select_fusion.1.which_ref, s32[1]{0:T(128)} %bitcast.side_ref, bf16[768,128]{1,0:T(8,128)(2,1)} %bitcast.49, bf16[768,128]{1,0:T(8,128)(2,1)} %copy-done.7, bf16[768,128]{1,0:T(8,128)(2,1)} %copy-done.6, bf16[768,128]{1,0:T(8,128)(2,1)} %copy-done.5, ...), custom_call_target="tpu_custom_call" | custom-call | flops 301989888 | bytes 1769472 | tf_op jit(solution)/shard_map/pallas_call | solution.py:242
  136.3 2.2 %fusion.1 = bf16[1,768,384]{2,1,0:T(8,128)(2,1)} fusion(f32[768,384]{1,0:T(8,128)} %shard_map.116, bf16[768,384]{1,0:T(8,128)(2,1)S(1)} %collective-permute-done.8), kind=kLoop, calls=%fused_computation.3 | loop fusion | flops 884736 | bytes 2359296 | tf_op jit(solution)/shard_map/broadcast_in_dim | solution.py:348
  (47 shorter events, 1.2 us)
Async XLA Ops:
  6.5 36.2 %copy-start = (s32[16,12,12]{2,0,1:T(8,128)S(1)}, s32[16,12,12]{2,0,1:T(8,128)}, u32[]{:S(2)}) copy-start(s32[16,12,12]{2,0,1:T(8,128)} %param.14) | copy-start | bytes 27652
  6.5 111.5 %all-gather.3.cloned.1.call-start = ((), (), s32[]{:S(2)}) async-start(), calls=%async_computation.2 | async-start | bytes 2433024 | tf_op jit(solution)/shard_map/all_gather | solution.py:296
  11.1 1.5 %collective-permute-start.3 = (bf16[96,384]{1,0:T(8,128)(2,1)}, bf16[96,384]{1,0:T(8,128)(2,1)S(1)}, u32[]{:S(2)}, u32[]{:S(2)}) collective-permute-start(bf16[96,384]{1,0:T(8,128)(2,1)} %shard_map.111), channel_id=1, source_target_pairs={{0,0},{1,1},{2,64},{3,65},{4,128},{5,129},{6,192},{7,193},{8,8},{9... | collective-permute-start | bytes 221192 | tf_op jit(solution)/shard_map/ppermute | solution.py:295
  12.6 0.6 copy-start.12
  16.7 64.7 %all-to-all-start = ((bf16[32,24,384]{2,1,0:T(8,128)(2,1)}), bf16[32,24,384]{2,1,0:T(8,128)(2,1)S(1)}, u32[]{:S(2)}, u32[]{:S(2)}) async-start(bf16[32,24,384]{2,1,0:T(8,128)(2,1)} %bitcast.43), calls=%async_computation | async-start | bytes 1179648 | tf_op jit(solution)/shard_map/all_to_all | solution.py:304
  37.7 5.0 %copy-start.11 = (s32[12,16,16]{2,1,0:T(8,128)S(1)}, s32[12,16,16]{2,1,0:T(8,128)}, u32[]{:S(2)}) copy-start(s32[12,16,16]{2,1,0:T(8,128)} %param.15) | copy-start | bytes 36868
  37.7 5.6 %copy-start.13 = (s32[48]{0:T(128)S(1)}, s32[48]{0:T(128)}, u32[]{:S(2)}) copy-start(s32[48]{0:T(128)} %constant.98.clone) | copy-start | bytes 580
  41.5 29.9 %collective-permute-start.4 = (bf16[768,512]{1,0:T(8,128)(2,1)}, bf16[768,512]{1,0:T(8,128)(2,1)S(1)}, u32[]{:S(2)}, u32[]{:S(2)}) collective-permute-start(bf16[768,512]{1,0:T(8,128)(2,1)} %shard_map.112), channel_id=1, source_target_pairs={{0,8},{8,0},{16,24},{24,16},{32,40},{40,32},{48,56},{56,48},{64,72... | collective-permute-start | bytes 2359304 | tf_op jit(solution)/shard_map/ppermute | solution.py:300
  71.3 0.9 copy-start.1
  81.3 14.3 %copy-start.4 = (bf16[768,256]{1,0:T(8,128)(2,1)S(1)}, bf16[768,256]{1,0:T(8,128)(2,1)}, u32[]{:S(2)}) copy-start(bf16[768,256]{1,0:T(8,128)(2,1)} %shard_map.114.refs_0_) | copy-start | bytes 1179652
  81.3 27.2 %collective-permute-start.7 = (bf16[768,256]{1,0:T(8,128)(2,1)}, bf16[768,256]{1,0:T(8,128)(2,1)S(1)}, u32[]{:S(2)}, u32[]{:S(2)}) collective-permute-start(bf16[768,256]{1,0:T(8,128)(2,1)} %shard_map.114.refs_0_), channel_id=1, source_target_pairs={{0,6},{1,7},{2,0},{3,1},{4,2},{5,3},{6,4},{7,5},{8,14},{9,15},{10,... | collective-permute-start | bytes 1179656 | tf_op jit(solution)/shard_map/ppermute | solution.py:338
  81.4 0.8 copy-start.2
  86.5 18.8 %all-to-all-start.1 = ((bf16[32,24,128]{2,1,0:T(8,128)(2,1)}), bf16[32,24,128]{2,1,0:T(8,128)(2,1)S(1)}, u32[]{:S(2)}, u32[]{:S(2)}) async-start(bf16[32,24,128]{2,1,0:T(8,128)(2,1)} %bitcast.50), calls=%async_computation.1 | async-start | bytes 393216 | tf_op jit(solution)/shard_map/all_to_all | solution.py:331
  95.7 13.5 %collective-permute-start.6 = (bf16[768,256]{1,0:T(8,128)(2,1)S(1)}, bf16[768,256]{1,0:T(8,128)(2,1)S(1)}, u32[]{:S(2)}, u32[]{:S(2)}) collective-permute-start(bf16[768,256]{1,0:T(8,128)(2,1)S(1)} %copy-done.4), channel_id=1, source_target_pairs={{0,4},{1,5},{2,6},{3,7},{4,0},{5,1},{6,2},{7,3},{8,12},{9,13},{10,... | collective-permute-start | bytes 1179656 | tf_op jit(solution)/shard_map/ppermute | solution.py:338
  96.5 21.6 %collective-permute-start.5 = (bf16[768,256]{1,0:T(8,128)(2,1)S(1)}, bf16[768,256]{1,0:T(8,128)(2,1)S(1)}, u32[]{:S(2)}, u32[]{:S(2)}) collective-permute-start(bf16[768,256]{1,0:T(8,128)(2,1)S(1)} %copy-done.4), channel_id=1, source_target_pairs={{0,2},{1,3},{2,4},{3,5},{4,6},{5,7},{6,0},{7,1},{8,10},{9,11},{10,... | collective-permute-start | bytes 1179656 | tf_op jit(solution)/shard_map/ppermute | solution.py:338
  105.2 19.5 %copy-start.3 = (bf16[32,24,128]{2,1,0:T(8,128)(2,1)}, bf16[32,24,128]{2,1,0:T(8,128)(2,1)S(1)}, u32[]{:S(2)}) copy-start(bf16[32,24,128]{2,1,0:T(8,128)(2,1)S(1)} %all-to-all-done.1) | copy-start | bytes 589828
  105.2 19.5 %collective-permute-start.2 = (bf16[768,128]{1,0:T(8,128)(2,1)S(1)}, bf16[768,128]{1,0:T(8,128)(2,1)S(1)}, u32[]{:S(2)}, u32[]{:S(2)}) collective-permute-start(bf16[768,128]{1,0:T(8,128)(2,1)S(1)} %bitcast.45), channel_id=1, source_target_pairs={{0,6},{1,7},{2,0},{3,1},{4,2},{5,3},{6,4},{7,5},{8,14},{9,15},{10,... | collective-permute-start | bytes 589832 | tf_op jit(solution)/shard_map/ppermute | solution.py:338
  105.2 19.5 %collective-permute-start.1 = (bf16[768,128]{1,0:T(8,128)(2,1)S(1)}, bf16[768,128]{1,0:T(8,128)(2,1)S(1)}, u32[]{:S(2)}, u32[]{:S(2)}) collective-permute-start(bf16[768,128]{1,0:T(8,128)(2,1)S(1)} %bitcast.46), channel_id=1, source_target_pairs={{0,4},{1,5},{2,6},{3,7},{4,0},{5,1},{6,2},{7,3},{8,12},{9,13},{10,... | collective-permute-start | bytes 589832 | tf_op jit(solution)/shard_map/ppermute | solution.py:338
  108.5 9.5 %copy-start.8 = (bf16[768,256]{1,0:T(8,128)(2,1)}, bf16[768,256]{1,0:T(8,128)(2,1)S(1)}, u32[]{:S(2)}) copy-start(bf16[768,256]{1,0:T(8,128)(2,1)S(1)} %collective-permute-done.7.refs_3_) | copy-start | bytes 1179652
  108.5 16.6 %collective-permute-start = (bf16[768,128]{1,0:T(8,128)(2,1)S(1)}, bf16[768,128]{1,0:T(8,128)(2,1)S(1)}, u32[]{:S(2)}, u32[]{:S(2)}) collective-permute-start(bf16[768,128]{1,0:T(8,128)(2,1)S(1)} %bitcast.47), channel_id=1, source_target_pairs={{0,2},{1,3},{2,4},{3,5},{4,6},{5,7},{6,0},{7,1},{8,10},{9,11},{10,... | collective-permute-start | bytes 589832 | tf_op jit(solution)/shard_map/ppermute | solution.py:338
  109.2 8.9 %copy-start.9 = (bf16[768,256]{1,0:T(8,128)(2,1)}, bf16[768,256]{1,0:T(8,128)(2,1)S(1)}, u32[]{:S(2)}) copy-start(bf16[768,256]{1,0:T(8,128)(2,1)S(1)} %collective-permute-done.6.refs_2_) | copy-start | bytes 1179652
  118.1 0.7 copy-start.10
  124.8 0.7 copy-start.5
  124.8 0.7 copy-start.6
  125.5 0.7 copy-start.7
  130.8 5.5 %collective-permute-start.8 = (bf16[768,384]{1,0:T(8,128)(2,1)}, bf16[768,384]{1,0:T(8,128)(2,1)S(1)}, u32[]{:S(2)}, u32[]{:S(2)}) collective-permute-start(bf16[768,384]{1,0:T(8,128)(2,1)} %shard_map.117), channel_id=1, source_target_pairs={{0,1},{1,0},{2,3},{3,2},{4,5},{5,4},{6,7},{7,6},{8,9},{9,8},{10,11... | collective-permute-start | bytes 1769480 | tf_op jit(solution)/shard_map/ppermute | solution.py:346
Sparse Core Ops, SparseCore 0:
  13.4 86.2 all-gather.2

commit v2 on v0

v2 whole, which is shorter than its diff:
```python
import functools
import math

import jax
import jax.numpy as jnp
import numpy as np
from jax import lax
from jax.experimental import pallas as pl
from jax.experimental.pallas import tpu as pltpu
from jax.sharding import PartitionSpec as P

HD = 128
BLOCK = 128
VMEM = 24 * 1024 * 1024
ALL_VMEM = 60 * 1024 * 1024
BF16 = jnp.bfloat16
F32 = jnp.float32
CFG = {'w': 'zlast2', 'pick': 'kvt', 'order': ['kv', 'packed', 'w', 'own', 'r', 'spat', 'x', 'time', 'r', 'r', 'r'], 'after': {'w': ['kv'], 'own': ['first'], 'time': ['spat'], 'r2': ['time'], 'r3': ['x1', 'x2', 'x3'], 'r4': ['returned']}}
LOG2E = math.log2(math.e)
SCALE2 = LOG2E / math.sqrt(HD)
NT = (((1,), (1,)), ((), ()))


def dot_nt(a, b):
    return lax.dot_general(a, b, NT, preferred_element_type=F32)


def dot_nn(a, b):
    return jnp.dot(a, b, preferred_element_type=F32)


def params():
    return pltpu.CompilerParams(vmem_limit_bytes=VMEM)


def cost(flops, moved):
    return pl.CostEstimate(flops=flops // 1000, bytes_accessed=moved // 1000, transcendentals=0)


def smem():
    return pl.BlockSpec(memory_space=pltpu.SMEM)


def vmem():
    return pl.BlockSpec(memory_space=pltpu.VMEM)


def anywhere():
    return pl.BlockSpec(memory_space=pl.ANY)


def hbm():
    return pl.BlockSpec(memory_space=pltpu.HBM)


def start_all(copies):
    for copy in copies:
        copy.start()


def wait_all(copies):
    for copy in copies:
        copy.wait()


def head_lanes(heads_ref, slot):
    temp = lax.rem(heads_ref[0], 3)
    if slot == 0:
        number = jnp.where(temp == 0, 1, 0)
    elif slot == 1:
        number = jnp.where(temp == 2, 1, 2)
    else:
        number = temp
    return pl.ds(pl.multiple_of(number * HD, HD), HD)


def token(block):
    return block[:16, :HD]


def pick(heads, groups, after=()):
    arrays = []
    for array, _ in [move for group in groups for move in group]:
        if not any(array is a for a in arrays):
            arrays.append(array)
    moves = [
        (next(i for i, a in enumerate(arrays) if a is array), slot, g, n)
        for g, group in enumerate(groups)
        for n, (array, slot) in enumerate(group)
    ]

    def body(heads_ref, *refs):
        outs, sems = refs[-1 - len(groups) : -1], refs[-1]
        copies = [
            pltpu.make_async_copy(
                refs[i].at[:, head_lanes(heads_ref, slot)],
                outs[g].at[:, n * HD : (n + 1) * HD],
                sems.at[k],
            )
            for k, (i, slot, g, n) in enumerate(moves)
        ]
        start_all(copies)
        wait_all(copies)

    return pl.pallas_call(
        body,
        out_shape=tuple(
            jax.ShapeDtypeStruct((group[0][0].shape[0], len(group) * HD), BF16) for group in groups
        ),
        in_specs=[smem()] + [hbm()] * len(arrays) + [anywhere()] * len(after),
        out_specs=(vmem(),) * len(groups),
        scratch_shapes=[pltpu.SemaphoreType.DMA((len(moves),))],
        compiler_params=pltpu.CompilerParams(vmem_limit_bytes=ALL_VMEM),
        cost_estimate=cost(0, 4 * len(moves) * arrays[0].size // 3),
    )(heads, *arrays, *after)


def exp_parts(scores, floor):
    top = floor
    for s in scores:
        part = jnp.max(s, axis=0, keepdims=True)
        top = part if top is None else jnp.maximum(top, part)
    raised = [jnp.exp2(s - top) for s in scores]
    total = None
    for p in raised:
        part = jnp.sum(p, axis=0, keepdims=True)
        total = part if total is None else total + part
    weights = jnp.concatenate([p.astype(BF16) for p in raised], axis=0)
    return top, total, weights


def half_scores(keys, queries, bias_ref, base, tile, t):
    blocks = keys.shape[0] // BLOCK
    out = []
    for n in range(blocks):
        s = dot_nt(keys[n * BLOCK : (n + 1) * BLOCK, :], queries) * SCALE2
        out.append(s + bias_ref[base + n : base + n + 1, t * tile : (t + 1) * tile])
    return out


def own_half(order, q, k, v, bias, after):
    rows = q.shape[0]
    tile = 256

    def body(
        order_ref, q_ref, k_ref, v_ref, bias_ref, *refs
    ):
        o_ref, m_ref, l_ref, q_in, k_in, v_in, sems = refs[-7:]
        copies = [
            [
                pltpu.make_async_copy(
                    src.at[:, head_lanes(order_ref, h)], dst.at[h], sems.at[h, i]
                )
                for i, (src, dst) in enumerate(((q_ref, q_in), (k_ref, k_in), (v_ref, v_in)))
            ]
            for h in range(2)
        ]
        for h in range(2):
            start_all(copies[h])
        for h in range(2):
            wait_all(copies[h])
            keys = k_in[h]
            values = v_in[h].T
            for t in range(rows // tile):
                part = slice(t * tile, (t + 1) * tile)
                scores = half_scores(keys, q_in[h, part, :], bias_ref, 0, tile, t)
                top, total, weights = exp_parts(scores, None)
                o_ref[h, :, part] = dot_nn(values, weights)
                m_ref[h : h + 1, part] = top
                l_ref[h : h + 1, part] = total

    small = jax.ShapeDtypeStruct((2, rows), F32)
    held = pltpu.VMEM((2, rows, HD), BF16)
    return pl.pallas_call(
        body,
        out_shape=(jax.ShapeDtypeStruct((2, HD, rows), F32), small, small),
        in_specs=[smem()] + [hbm()] * 3 + [vmem()] + [anywhere()] * len(after),
        out_specs=(vmem(),) * 3,
        scratch_shapes=[held, held, held, pltpu.SemaphoreType.DMA((2, 3))],
        compiler_params=params(),
        cost_estimate=cost(8 * rows * rows * HD, 8 * rows * HD * 4),
    )(order, q, k, v, bias, *after)


def other_half(order, q, kv, bias, o, m, l, after):
    rows = q.shape[0]
    tile = 256

    def body(
        order_ref, q_ref, kv_ref, bias_ref, o_ref, m_ref, l_ref, *refs
    ):
        out_ref, q_in, k_in, v_in, sems = refs[-5:]
        copies = [
            [
                pltpu.make_async_copy(src, dst.at[h], sems.at[h, i])
                for i, (src, dst) in enumerate(
                    (
                        (q_ref.at[:, head_lanes(order_ref, h)], q_in),
                        (kv_ref.at[:, h * HD : (h + 1) * HD], k_in),
                        (kv_ref.at[:, (2 + h) * HD : (3 + h) * HD], v_in),
                    )
                )
            ]
            for h in range(2)
        ]
        for h in range(2):
            start_all(copies[h])
        for h in range(2):
            wait_all(copies[h])
            keys = k_in[h]
            values = v_in[h].T
            for t in range(rows // tile):
                part = slice(t * tile, (t + 1) * tile)
                scores = half_scores(
                    keys, q_in[h, part, :], bias_ref, rows // BLOCK, tile, t
                )
                before = m_ref[h : h + 1, part]
                top, total, weights = exp_parts(scores, before)
                keep = jnp.exp2(before - top)
                total = total + l_ref[h : h + 1, part] * keep
                mixed = o_ref[h, :, part] * keep + dot_nn(values, weights)
                out_ref[part, h * HD : (h + 1) * HD] = (mixed / total).T.astype(BF16)

    held = pltpu.VMEM((2, rows, HD), BF16)
    return pl.pallas_call(
        body,
        out_shape=jax.ShapeDtypeStruct((rows, 2 * HD), BF16),
        in_specs=[smem(), hbm(), anywhere()] + [vmem()] * 4 + [anywhere()] * len(after),
        out_specs=vmem(),
        scratch_shapes=[held, held, held, pltpu.SemaphoreType.DMA((2, 3))],
        compiler_params=params(),
        cost_estimate=cost(8 * rows * rows * HD, 8 * rows * HD * 4),
    )(order, q, kv, bias, o, m, l, *after)


def time_attention(owned, rule, place, after):
    rows = owned.shape[0]
    tile = 256

    def body(all_ref, rule_ref, place_ref, *refs):
        out_ref = refs[-1]
        values = all_ref[:, 2 * HD :].T
        for t in range(rows // tile):
            part = slice(t * tile, (t + 1) * tile)
            scores = []
            for n in range(rows // BLOCK):
                down = slice(n * BLOCK, (n + 1) * BLOCK)
                s = dot_nt(all_ref[down, HD : 2 * HD], all_ref[part, 0:HD]) * SCALE2
                agree = dot_nn(place_ref[down, :], rule_ref[:, part])
                scores.append(jnp.where(agree > 1.5, s, -jnp.inf))
            _, total, weights = exp_parts(scores, None)
            out_ref[part, :] = (dot_nn(values, weights) / total).T.astype(BF16)

    return pl.pallas_call(
        body,
        out_shape=jax.ShapeDtypeStruct((rows, HD), BF16),
        in_specs=[vmem()] * 3 + [anywhere()] * len(after),
        out_specs=vmem(),
        compiler_params=params(),
        cost_estimate=cost(4 * rows * rows * HD, 8 * rows * HD),
    )(owned, rule, place, *after)


def join(*blocks, after=()):
    rows = [b.shape[0] for b in blocks]
    width = blocks[0].shape[1]

    def body(*refs):
        out_ref = refs[-1]
        start = 0
        for ref, held in zip(refs, rows):
            out_ref[start : start + held, :] = ref[...]
            start += held

    return pl.pallas_call(
        body,
        out_shape=jax.ShapeDtypeStruct((sum(rows), width), BF16),
        in_specs=[vmem()] * len(blocks) + [anywhere()] * len(after),
        out_specs=vmem(),
        compiler_params=params(),
        cost_estimate=cost(0, 4 * sum(rows) * width),
    )(*blocks, *after)


def gate(blocks, after):
    def body(*refs):
        count = len(blocks)
        for n in range(count):
            refs[n - count][...] = refs[n][...]

    return pl.pallas_call(
        body,
        out_shape=tuple(jax.ShapeDtypeStruct(b.shape, b.dtype) for b in blocks),
        in_specs=[vmem()] * len(blocks) + [anywhere()] * len(after),
        out_specs=(vmem(),) * len(blocks),
        compiler_params=params(),
        cost_estimate=cost(0, 4 * sum(b.size for b in blocks)),
    )(*blocks, *after)


def gather_weight(blocks, starts, pieces, after):
    each = 96
    count = pieces[0].shape[0] // each
    width = pieces[0].shape[1]

    def body(block_ref, row_ref, *refs):
        out_ref = refs[-1]
        for n in range(len(pieces)):
            start = pl.multiple_of(row_ref[n] * each, each)
            for j in range(count):
                out_ref[block_ref[j], pl.ds(start, each), :] = refs[n][
                    j * each : (j + 1) * each, :
                ]

    return pl.pallas_call(
        body,
        out_shape=jax.ShapeDtypeStruct((count, len(pieces) * each, width), BF16),
        in_specs=[smem(), smem()] + [vmem()] * len(pieces) + [anywhere()] * len(after),
        out_specs=vmem(),
        compiler_params=params(),
        cost_estimate=cost(0, 4 * count * len(pieces) * each * width),
    )(blocks, starts, *pieces, *after)


def project_spatial(which, side, parts, weights):
    rows, width = parts[0].shape
    count, cols, _ = weights.shape
    half = cols // 2
    tile = 256

    def body(which_ref, side_ref, *refs):
        w_ref, twin_ref, own_ref = refs[-3:]
        for out_ref, place in ((twin_ref, 1 - side_ref[0]), (own_ref, side_ref[0])):
            columns = pl.ds(pl.multiple_of(place * half, half), half)
            for t in range(rows // tile):
                part = slice(t * tile, (t + 1) * tile)
                total = None
                for n in range(count):
                    term = dot_nt(refs[n][part, :], w_ref[which_ref[n], columns, 0:width])
                    total = term if total is None else total + term
                out_ref[part, :] = total

    shape = jax.ShapeDtypeStruct((rows, half), F32)
    return pl.pallas_call(
        body,
        out_shape=(shape, shape),
        in_specs=[smem(), smem()] + [vmem()] * (count + 1),
        out_specs=(vmem(), vmem()),
        compiler_params=params(),
        cost_estimate=cost(2 * rows * cols * width * count, 6 * rows * cols),
    )(which, side, *parts, weights)


def project_time(which, side, parts, weights, base, dtype):
    rows, width = parts[0].shape
    count, cols, all_rows = weights.shape
    half = cols // 2
    tile = 256

    def body(which_ref, side_ref, *refs):
        out_ref = refs[-1]
        w_ref, base_ref = refs[count], refs[count + 1]
        columns = pl.ds(pl.multiple_of(side_ref[0] * half, half), half)
        for t in range(rows // tile):
            part = slice(t * tile, (t + 1) * tile)
            total = base_ref[part, :]
            for n in range(count):
                w = w_ref[which_ref[n], columns, all_rows - width : all_rows]
                total = total + dot_nt(refs[n][part, :], w)
            out_ref[part, :] = total.astype(dtype)

    return pl.pallas_call(
        body,
        out_shape=jax.ShapeDtypeStruct((rows, half), dtype),
        in_specs=[smem(), smem()] + [vmem()] * (count + 2),
        out_specs=vmem(),
        compiler_params=params(),
        cost_estimate=cost(2 * rows * half * width * count, 6 * rows * half),
    )(which, side, *parts, weights, base)


def finish(own, other):
    rows, cols = own.shape
    tile = 256
    count = rows // tile

    def body(own_ref, other_ref, out_ref, held, sems):
        copies = []
        for t in range(count):
            part = slice(t * tile, (t + 1) * tile)
            held[part, :] = (own_ref[part, :] + other_ref[part, :].astype(F32)).astype(BF16)
            copies.append(
                pltpu.make_async_copy(held.at[part, :], out_ref.at[part, :], sems.at[t])
            )
            copies[-1].start()
        wait_all(copies)

    return pl.pallas_call(
        body,
        out_shape=jax.ShapeDtypeStruct((rows, cols), BF16),
        in_specs=[vmem(), vmem()],
        out_specs=hbm(),
        scratch_shapes=[pltpu.VMEM((rows, cols), BF16), pltpu.SemaphoreType.DMA((count,))],
        compiler_params=params(),
        cost_estimate=cost(rows * cols, 8 * rows * cols),
    )(own, other)


def shards(
    shape_yzx,
    query_states,
    key_states,
    value_states,
    spatial_mask,
    temporal_mask,
    temporal_heads,
    out_weight,
):
    ys, zs, xs, cores = shape_yzx
    _, rows, width = query_states.shape
    heads_here = width // HD
    seq_count = ys * zs
    seq_index = lax.axis_index("seq")
    head_index = lax.axis_index("head")
    frames = spatial_mask.shape[0]
    blocks = spatial_mask.shape[1]
    x_index = head_index // cores
    core = head_index % cores
    q, k, v = query_states[0], key_states[0], value_states[0]
    weight = out_weight.T

    W_MODE, T = CFG["w"], CFG
    heads = temporal_heads
    if CFG["pick"] == "all":
        kv, packed, w_own = pick(
            heads,
            [
                [(k, 0), (k, 1), (v, 0), (v, 1)],
                [(q, 2), (k, 2), (v, 2)],
                [(weight, n) for n in range(heads_here)],
            ],
        )
    elif CFG["pick"] == "kvw":
        kv, w_own = pick(
            heads,
            [[(k, 0), (k, 1), (v, 0), (v, 1)], [(weight, n) for n in range(heads_here)]],
        )
    elif CFG["pick"] == "kvt":
        kv, packed = pick(
            heads, [[(k, 0), (k, 1), (v, 0), (v, 1)], [(q, 2), (k, 2), (v, 2)]]
        )
        w_own = None
    elif CFG["pick"] == "timew":
        packed, w_own = pick(
            heads,
            [[(q, 2), (k, 2), (v, 2)], [(weight, n) for n in range(heads_here)]],
        )

    def swap(move):
        route = []
        for y in range(ys):
            for z in range(zs):
                for x in range(xs):
                    for c in range(cores):
                        here = (y * zs + z) * xs * cores + x * cores + c
                        there = (x * zs + move(z)) * xs * cores + y * cores + c
                        route.append((here, there))
        return route

    def along_y(block, step):
        route = [(s, (s + step * zs) % seq_count) for s in range(seq_count)]
        return lax.ppermute(block, "seq", route)

    def along_z(block, step):
        route = [(s, s // zs * zs + (s + step) % zs) for s in range(seq_count)]
        return lax.ppermute(block, "seq", route)

    y_index, z_index = seq_index // zs, seq_index % zs
    got = {}

    def make_w(w_own=w_own):
        if W_MODE == "pair":
            w_two = join(
                lax.ppermute(w_own, ("seq", "head"), swap(lambda z: z)),
                lax.ppermute(w_own, ("seq", "head"), swap(lambda z: z ^ 1)),
                after=toks("w_two"),
            )
            got["w_two"] = w_two
            steps = (0, 2, zs - 2, 4)
            got["z"] = [w_two, *[along_z(w_two, step) for step in steps[1:]]]
            return jnp.stack(
                [((z_index + zs - step) % zs) ^ flip for step in steps for flip in (0, 1)]
            ).astype(jnp.int32)
        if W_MODE == "direct":
            got["z"] = [
                lax.ppermute(w_own, ("seq", "head"), swap(lambda z, n=n: (z + n) % zs))
                for n in range(zs)
            ]
            return jnp.stack([(z_index + zs - n) % zs for n in range(zs)]).astype(jnp.int32)
        if w_own is None:
            (w_own,) = pick(heads, [[(weight, n) for n in range(heads_here)]], toks("w"))
        if W_MODE == "zlast2":
            first = lax.ppermute(w_own, ("seq", "head"), swap(lambda z: z))
            got["first"] = first
            got["w_two"] = join(*[first] + [along_y(first, n) for n in range(1, ys)])
            got["up"], got["down"] = [got["w_two"]], [got["w_two"]]
        if W_MODE == "zlast":
            spread = []
            for step in range(ys):
                route = []
                for y in range(ys):
                    for z in range(zs):
                        for x in range(xs):
                            for c in range(cores):
                                here = (y * zs + z) * xs * cores + x * cores + c
                                to = ((x + step) % ys * zs + z) * xs * cores + y * cores + c
                                route.append((here, to))
                spread.append(lax.ppermute(w_own, ("seq", "head"), route))
            got["w_two"] = join(*spread, after=toks("w_two"))
            got["up"], got["down"] = [got["w_two"]], [got["w_two"]]
        if W_MODE == "ring":
            first = lax.ppermute(w_own, ("seq", "head"), swap(lambda z: z))
            got["w_two"] = first
            got["up"], got["down"] = [first], [first]
            ring_step()

    def ring_step():
        n = len(got["up"])
        up, down = got["up"][-1], got["down"][-1]
        if CFG["after"].get(f"r{n}"):
            if n == 1:
                (up,) = gate([up], toks(f"r{n}"))
                down = up
            else:
                up, down = gate([up, down], toks(f"r{n}"))
        got["up"].append(along_z(up, 1))
        got[f"up{n}"] = got["up"][-1]
        if n < zs // 2:
            got["down"].append(along_z(down, -1))
        else:
            up, down = got["up"], got["down"]
            got["z"] = [up[0], up[1], down[1], *up[2:], *down[2:]]

    def w_order():
        order = [0, 1, zs - 1, *range(2, zs // 2 + 1)] + [zs - n for n in range(2, zs // 2)]
        return jnp.stack([(z_index + zs - n) % zs for n in order]).astype(jnp.int32)

    def make_wz():
        z = got["z"]
        if CFG.get("split"):
            got["w_n"] = join(*z[: CFG["split"]], after=toks("w_n"))
            got["w_z"] = join(*z[CFG["split"] :], after=toks("w_z"))
            got["groups"] = [got["w_n"], got["w_z"]]
        else:
            got["w_z"] = join(*z, after=toks("w_z"))
            got["groups"] = [got["w_z"]]

    def toks(name):
        return [got[n] if n == "kv" else token(got[n]) for n in CFG["after"].get(name, ())]

    def make_kv():
        if CFG["pick"] in ("all", "kvw", "kvt"):
            block = kv
        else:
            (block,) = pick(heads, [[(k, 0), (k, 1), (v, 0), (v, 1)]], toks("kv"))
        got["kv"] = block
        got["kv_other"] = lax.ppermute(block, "seq", [(s, s ^ 1) for s in range(seq_count)])

    positions = rows // seq_count

    def make_time():
        if CFG["pick"] in ("all", "timew", "kvt"):
            block = packed
        else:
            (block,) = pick(heads, [[(q, 2), (k, 2), (v, 2)]], toks("packed"))
        got["packed"] = block
        owned = lax.all_to_all(
            block.reshape(seq_count, positions, 3 * HD), "seq", 0, 0, tiled=True
        )
        got["owned"] = owned.reshape(rows, 3 * HD)

    parity = seq_index % 2
    mine = lax.dynamic_slice(
        spatial_mask,
        (seq_index // 2, parity * (blocks // 2), jnp.int32(0)),
        (1, blocks // 2, blocks),
    )[0]
    bias = jnp.where(mine > 0, 0.0, -jnp.inf).astype(F32)
    bias = jnp.where(parity == 0, bias, jnp.roll(bias, blocks // 2, axis=1))
    bias = jnp.repeat(bias.T, BLOCK, axis=1)

    spot = np.arange(2)[:, None] * rows + np.arange(positions)[None, :]
    spot = (jnp.asarray(spot.reshape(-1), jnp.int32) + seq_index * positions) // BLOCK
    hot = (spot[:, None] == jnp.arange(blocks, dtype=jnp.int32)[None, :]).astype(BF16)
    rule = jnp.dot(
        hot, (temporal_mask > 0).reshape(blocks, -1).astype(BF16), preferred_element_type=F32
    )
    rule = rule.reshape(2 * positions, frames, frames).transpose(2, 1, 0)
    rule = rule.reshape(frames, rows).astype(BF16)
    index = np.arange(rows)
    frame_hot = index[:, None] // (2 * positions) == np.arange(frames)[None, :]
    key_hot = index[:, None] % (2 * positions) == np.arange(2 * positions)[None, :]
    place = jnp.asarray(np.concatenate([frame_hot, key_hot], axis=1), BF16)
    rule = jnp.concatenate([rule, jnp.asarray(key_hot.T, BF16)], axis=0)
    def along_x(block):
        got = [block]
        for step in range(1, xs):
            route = [(h, (h + step * cores) % (xs * cores)) for h in range(xs * cores)]
            got.append(lax.ppermute(block, "head", route))
        return got

    def make_x():
        got["parts"] = along_x(got["spat"])
        got["x1"], got["x2"], got["x3"] = got["parts"][1:]

    def make_own():
        got["o"], got["m"], got["l"] = own_half(heads, q, k, v, bias, toks("own"))
        got["own"] = got["l"]

    def make_spat():
        got["spat"] = other_half(
            heads, q, got["kv_other"], bias, got["o"], got["m"], got["l"], toks("spat")
        )

    def make_att():
        got["time"] = time_attention(got["owned"], rule, place, toks("time"))
        back = lax.all_to_all(
            got["time"].reshape(seq_count, positions, HD), "seq", 0, 0, tiled=True
        )
        got["returned"] = back.reshape(rows, HD)

    steps = dict(
        x=make_x, wz=make_wz, kv=make_kv, packed=make_time, own=make_own, spat=make_spat, time=make_att
    )
    for name in CFG["order"]:
        if name == "w":
            make_w()
        elif name == "r":
            ring_step()
        else:
            steps[name]()
    w_blocks = jnp.stack([(y_index + ys - n) % ys for n in range(ys)]).astype(jnp.int32)
    w_all = gather_weight(w_blocks, w_order(), got["z"], toks("gather"))
    spat, returned = got["spat"], got["returned"]

    which = ((x_index + xs - jnp.arange(xs)) % xs).astype(jnp.int32)
    side = core.astype(jnp.int32).reshape(1)
    base_twin, base_own = project_spatial(which, side, got["parts"], w_all)
    time_parts = along_x(returned)
    for_twin = project_time(which, 1 - side, time_parts, w_all, base_twin, BF16)
    from_twin = lax.ppermute(for_twin, "head", [(h, h ^ 1) for h in range(xs * cores)])
    own = project_time(which, side, time_parts, w_all, base_own, F32)
    return finish(own, from_twin)[None]


def solution(mesh):
    in_specs = (
        P(None, "seq", "head"),
        P(None, "seq", "head"),
        P(None, "seq", "head"),
        P(),
        P(),
        P("head"),
        P("head", "seq"),
    )
    out_specs = P(None, "seq", "head")
    return jax.shard_map(
        functools.partial(shards, (4, 8, 4, 2)),
        mesh=mesh,
        in_specs=in_specs,
        out_specs=out_specs,
        check_vma=False,
    )
```

time: 176 us -> 96.2 us (0.55)
  waiting for transfers between devices: 90.7 us -> 17.9 us
  starting transfers between devices: 22.5 us -> 50.1 us
  Pallas kernels: 0 us -> 23.1 us
  other arithmetic: 21.2 us -> 0.21 us
  matrix products: 16 us -> 0.15 us
  between operations: 14.5 us -> 1.24 us
  local copies, waits for them, and re-layouts: 10.5 us -> 2.86 us
    reduce_scatter x1 -> x0, waiting for transfers between devices: 61 us -> none  [shards(): lax.psum_scatter(partial_sum, 'head', scatter_dimension=1, tiled=True)]
    ppermute x1 -> x19, starting transfers between devices: 1.5 us -> 28.2 us  [the longest x7 9.39 us: along_z(): return lax.ppermute(block, 'seq', route)]
    pallas_call x0 -> x14, Pallas kernels: none -> 23.1 us  [the longest x1 4.21 us: other_half(): pl.pallas_call(body, out_shape=jax.ShapeDtypeStruct((rows, 2 * HD), BF16)...]
    dot_general x15 -> x1, matrix products: 16 us -> 0.15 us  [shards(): jnp.dot(hot, (temporal_mask > 0).reshape(blocks, -1).astype(BF16), prefer...]
    select_n x2 -> x3, other arithmetic: 15 us -> 0.02 us  [the longest x1 0.01 us: shards(): (jnp.asarray(spot.reshape(-1), jnp.int32) + seq_index * positions) // BLOCK]
    ppermute x1 -> x19, waiting for transfers between devices: 28.8 us -> 15 us  [the longest x7 9.99 us: along_z(): return lax.ppermute(block, 'seq', route)]
    reshape x3 -> x1, local copies, waits for them, and re-layouts: 3.73 us -> 0.11 us  [shards(): (temporal_mask > 0).reshape(blocks, -1).astype(BF16)]
    all_to_all x2, waiting for transfers between devices: 0.19 us -> 2.83 us  [the longest x1 2.83 us: make_att(): lax.all_to_all(got['time'].reshape(seq_count, positions, HD), 'seq', 0, 0...]
  transfers between devices with their start and end apart: 5 -> 21, of which waited for: 3 -> 7; matrix products, arithmetic and copies ran while one was open for 22% -> 3% of each run, Pallas kernels for 0% -> 18%
where the time goes in v2:
time: 96.2 us; the launch traced here: 95.6 us
  starting transfers between devices  50.1 us (52%)
  Pallas kernels  23.1 us (24%)
  waiting for transfers between devices  17.9 us (19%)
  local copies, waits for them, and re-layouts  2.86 us (3%)
  between operations  1.24 us (1%)
    all_to_all x1, starting transfers between devices, make_time(): lax.all_to_all(block.reshape(seq_count, positions, 3 * HD), 'seq', 0, 0,...  13.4 us
    ppermute x7, waiting for transfers between devices, along_z(): return lax.ppermute(block, 'seq', route)  9.99 us
    ppermute x7, starting transfers between devices, along_z(): return lax.ppermute(block, 'seq', route)  9.39 us
    all_to_all x1, starting transfers between devices, make_att(): lax.all_to_all(got['time'].reshape(seq_count, positions, HD), 'seq', 0, 0...  8.54 us
    ppermute x6, starting transfers between devices, along_x(): got.append(lax.ppermute(block, 'head', route))  7.48 us
    ppermute x3, starting transfers between devices, along_y(): return lax.ppermute(block, 'seq', route)  4.82 us
    pallas_call x1, Pallas kernels, other_half(): pl.pallas_call(body, out_shape=jax.ShapeDtypeStruct((rows, 2 * HD), BF16)...  4.21 us
    pallas_call x2, Pallas kernels, pick(): pl.pallas_call(body, out_shape=tuple((jax.ShapeDtypeStruct((group[0][0].s...  3.96 us
  transfers between devices with their start and end apart: 21, of which 7 were waited for; matrix products, arithmetic and copies ran while one was open for 3% of the time, Pallas kernels for 18%

profile of v2, /device:TPU:1, one launch (start us, length us, event | category | flops | bytes accessed | tf_op | source)
XLA Modules:
  0.0 95.6 jit_solution(11086522794963286846)
XLA Ops:
  0.7 2.5 %shard_map.100 = (bf16[768,512]{1,0:T(8,128)(2,1)}, bf16[768,384]{1,0:T(8,128)(2,1)}) custom-call(s32[1]{0:T(128)S(6)} %copy.22.heads_ref.order_ref, bf16[768,384]{1,0:T(8,128)(2,1)} %bitcast.43, bf16[768,384]{1,0:T(8,128)(2,1)} %bitcast.45, bf16[768,384]{1,0:T(8,128)(2,1)} %bitcast.39), custom_call_target="tpu_custom_call" | custom-call | bytes 2752 | tf_op jit(solution)/shard_map/pallas_call | solution.py:105
  3.3 2.6 %collective-permute-start = (bf16[768,512]{1,0:T(8,128)(2,1)}, bf16[768,512]{1,0:T(8,128)(2,1)}, u32[]{:S(2)}, u32[]{:S(2)}) collective-permute-start(bf16[768,512]{1,0:T(8,128)(2,1)} %get-tuple-element.18.refs_1_), channel_id=1, source_target_pairs={{0,8},{8,0},{16,24},{24,16},{32,40},{40,32},{48,56},{56,48},{64,72... | collective-permute-start | bytes 2359304 | tf_op jit(solution)/shard_map/ppermute | solution.py:567
  5.8 1.4 %shard_map.101 = bf16[96,384]{1,0:T(8,128)(2,1)} custom-call(s32[1]{0:T(128)S(6)} %copy.22.heads_ref.order_ref, bf16[96,384]{1,0:T(8,128)(2,1)} %bitcast.58, bf16[768,512]{1,0:T(8,128)(2,1)} %get-tuple-element.18.refs_1_), custom_call_target="tpu_custom_call" | custom-call | bytes 147 | tf_op jit(solution)/shard_map/pallas_call | solution.py:105
  7.2 1.5 %collective-permute-start.1 = (bf16[96,384]{1,0:T(8,128)(2,1)}, bf16[96,384]{1,0:T(8,128)(2,1)S(1)}, u32[]{:S(2)}, u32[]{:S(2)}) collective-permute-start(bf16[96,384]{1,0:T(8,128)(2,1)} %shard_map.101), channel_id=1, source_target_pairs={{0,0},{1,1},{2,64},{3,65},{4,128},{5,129},{6,192},{7,193},{8,8},{9... | collective-permute-start | bytes 221192 | tf_op jit(solution)/shard_map/ppermute | solution.py:503
  8.8 13.4 %all-to-all-start = ((bf16[32,24,384]{2,1,0:T(8,128)(2,1)}), bf16[32,24,384]{2,1,0:T(8,128)(2,1)S(1)}, u32[]{:S(2)}, u32[]{:S(2)}) async-start(bf16[32,24,384]{2,1,0:T(8,128)(2,1)} %bitcast.55), calls=%async_computation | async-start | bytes 1179648 | tf_op jit(solution)/shard_map/all_to_all | solution.py:577
  22.4 1.2 %collective-permute-start.5 = (bf16[96,384]{1,0:T(8,128)(2,1)S(1)}, bf16[96,384]{1,0:T(8,128)(2,1)S(1)}, u32[]{:S(2)}, u32[]{:S(2)}) collective-permute-start(bf16[96,384]{1,0:T(8,128)(2,1)S(1)} %collective-permute-done.1.refs_0_), channel_id=1, source_target_pairs={{0,64},{8,72},{16,80},{24,88},{32,96},{40,104},{48,112},{56,120},{... | collective-permute-start | bytes 221192 | tf_op jit(solution)/shard_map/ppermute | solution.py:472
  23.7 2.4 %collective-permute-start.6 = (bf16[96,384]{1,0:T(8,128)(2,1)S(1)}, bf16[96,384]{1,0:T(8,128)(2,1)S(1)}, u32[]{:S(2)}, u32[]{:S(2)}) collective-permute-start(bf16[96,384]{1,0:T(8,128)(2,1)S(1)} %collective-permute-done.1.refs_0_), channel_id=1, source_target_pairs={{0,128},{8,136},{16,144},{24,152},{32,160},{40,168},{48,176},{56,1... | collective-permute-start | bytes 221192 | tf_op jit(solution)/shard_map/ppermute | solution.py:472
  26.1 1.1 %collective-permute-start.7 = (bf16[96,384]{1,0:T(8,128)(2,1)S(1)}, bf16[96,384]{1,0:T(8,128)(2,1)S(1)}, u32[]{:S(2)}, u32[]{:S(2)}) collective-permute-start(bf16[96,384]{1,0:T(8,128)(2,1)S(1)} %collective-permute-done.1.refs_0_), channel_id=1, source_target_pairs={{0,192},{8,200},{16,208},{24,216},{32,224},{40,232},{48,240},{56,2... | collective-permute-start | bytes 221192 | tf_op jit(solution)/shard_map/ppermute | solution.py:472
  27.8 2.7 %collective-permute-done.6.refs_2_ = bf16[96,384]{1,0:T(8,128)(2,1)S(1)} collective-permute-done((bf16[96,384]{1,0:T(8,128)(2,1)S(1)}, bf16[96,384]{1,0:T(8,128)(2,1)S(1)}, u32[]{:S(2)}, u32[]{:S(2)}) %collective-permute-start.6) | collective-permute-done | bytes 73760 | tf_op jit(solution)/shard_map/ppermute | solution.py:472
  30.8 2.1 %collective-permute-start.8 = (bf16[384,384]{1,0:T(8,128)(2,1)S(1)}, bf16[384,384]{1,0:T(8,128)(2,1)S(1)}, u32[]{:S(2)}, u32[]{:S(2)}) collective-permute-start(bf16[384,384]{1,0:T(8,128)(2,1)S(1)} %shard_map.105.refs_0_), channel_id=1, source_target_pairs={{0,8},{8,16},{16,24},{24,32},{32,40},{40,48},{48,56},{56,0},{64,72... | collective-permute-start | bytes 884744 | tf_op jit(solution)/shard_map/ppermute | solution.py:476
  32.9 1.9 %collective-permute-start.9 = (bf16[384,384]{1,0:T(8,128)(2,1)S(1)}, bf16[384,384]{1,0:T(8,128)(2,1)S(1)}, u32[]{:S(2)}, u32[]{:S(2)}) collective-permute-start(bf16[384,384]{1,0:T(8,128)(2,1)S(1)} %shard_map.105.refs_0_), channel_id=1, source_target_pairs={{0,56},{8,0},{16,8},{24,16},{32,24},{40,32},{48,40},{56,48},{64,12... | collective-permute-start | bytes 884744 | tf_op jit(solution)/shard_map/ppermute | solution.py:476
  35.1 3.1 %shard_map.102 = (f32[2,128,768]{2,1,0:T(8,128)S(1)}, f32[2,768]{1,0:T(2,128)S(1)}, f32[2,768]{1,0:T(2,128)S(1)}) custom-call(s32[1]{0:T(128)S(6)} %copy.22.heads_ref.order_ref, bf16[768,384]{1,0:T(8,128)(2,1)S(1)} %bitcast.40, bf16[768,384]{1,0:T(8,128)(2,1)S(1)} %bitcast.44, bf16[768,384]{1,0:T(8,128)(2,1)S(1)} %bitcast.46, f32[12,768]{1,0:T(8,128)S(1)} %bitcast.53, ...), custom_call_target="tpu_custom_call" | custom-call | flops 603979 | bytes 3145 | tf_op jit(solution)/shard_map/pallas_call | solution.py:174
  38.3 4.2 %shard_map.103.refs_0_ = bf16[768,256]{1,0:T(8,128)(2,1)S(1)} custom-call(s32[1]{0:T(128)S(6)} %copy.22.heads_ref.order_ref, bf16[768,384]{1,0:T(8,128)(2,1)S(1)} %bitcast.41, bf16[768,512]{1,0:T(8,128)(2,1)} %collective-permute-done.kv_ref, f32[12,768]{1,0:T(8,128)S(1)} %bitcast.54, f32[2,128,768]{2,1,0:T(8,128)S(1)} %get-tuple-element.19.o_ref, ...), custom_call_target="tpu_custom_call" | custom-call | flops 603979 | bytes 3145 | tf_op jit(solution)/shard_map/pallas_call | solution.py:225
  43.3 1.5 %collective-permute-start.13 = (bf16[768,256]{1,0:T(8,128)(2,1)S(1)}, bf16[768,256]{1,0:T(8,128)(2,1)}, u32[]{:S(2)}, u32[]{:S(2)}) collective-permute-start(bf16[768,256]{1,0:T(8,128)(2,1)S(1)} %shard_map.103.refs_0_), channel_id=1, source_target_pairs={{0,4},{1,5},{2,6},{3,7},{4,0},{5,1},{6,2},{7,3},{8,12},{9,13},{10,... | collective-permute-start | bytes 1179656 | tf_op jit(solution)/shard_map/ppermute | solution.py:609
  44.8 1.0 %collective-permute-start.14 = (bf16[768,256]{1,0:T(8,128)(2,1)S(1)}, bf16[768,256]{1,0:T(8,128)(2,1)}, u32[]{:S(2)}, u32[]{:S(2)}) collective-permute-start(bf16[768,256]{1,0:T(8,128)(2,1)S(1)} %shard_map.103.refs_0_), channel_id=1, source_target_pairs={{0,6},{1,7},{2,0},{3,1},{4,2},{5,3},{6,4},{7,5},{8,14},{9,15},{10,... | collective-permute-start | bytes 1179656 | tf_op jit(solution)/shard_map/ppermute | solution.py:609
  45.9 2.4 %shard_map.104 = bf16[768,128]{1,0:T(8,128)(2,1)} custom-call(bf16[768,384]{1,0:T(8,128)(2,1)S(1)} %bitcast.42, bf16[64,768]{1,0:T(8,128)(2,1)S(1)} %pad_maximum_fusion.rule_ref, bf16[768,64]{1,0:T(8,128)(2,1)S(1)} %copy-done.6, bf16[16,128]{1,0:T(8,128)(2,1)S(1)} %slice.39.refs_0_), custom_call_target="tpu_custom_call" | custom-call | flops 301989 | bytes 786 | tf_op jit(solution)/shard_map/pallas_call | solution.py:254
  49.1 2.7 %collective-permute-start.11 = (bf16[384,384]{1,0:T(8,128)(2,1)S(1)}, bf16[384,384]{1,0:T(8,128)(2,1)S(1)}, u32[]{:S(2)}, u32[]{:S(2)}) collective-permute-start(bf16[384,384]{1,0:T(8,128)(2,1)S(1)} %get-tuple-element.23), channel_id=1, source_target_pairs={{0,56},{8,0},{16,8},{24,16},{32,24},{40,32},{48,40},{56,48},{64,12... | collective-permute-start | bytes 884744 | tf_op jit(solution)/shard_map/ppermute | solution.py:476
  51.8 8.5 %all-to-all-start.1 = ((bf16[32,24,128]{2,1,0:T(8,128)(2,1)}), bf16[32,24,128]{2,1,0:T(8,128)(2,1)S(1)}, u32[]{:S(2)}, u32[]{:S(2)}) async-start(bf16[32,24,128]{2,1,0:T(8,128)(2,1)} %bitcast.13), calls=%async_computation.1 | async-start | bytes 393216 | tf_op jit(solution)/shard_map/all_to_all | solution.py:627
  61.1 1.7 %collective-permute-done.14.refs_3_ = bf16[768,256]{1,0:T(8,128)(2,1)} collective-permute-done((bf16[768,256]{1,0:T(8,128)(2,1)S(1)}, bf16[768,256]{1,0:T(8,128)(2,1)}, u32[]{:S(2)}, u32[]{:S(2)}) %collective-permute-start.14) | collective-permute-done | bytes 393248 | tf_op jit(solution)/shard_map/ppermute | solution.py:609
  64.2 2.7 %collective-permute-start.16 = (bf16[384,384]{1,0:T(8,128)(2,1)S(1)}, bf16[384,384]{1,0:T(8,128)(2,1)S(1)}, u32[]{:S(2)}, u32[]{:S(2)}) collective-permute-start(bf16[384,384]{1,0:T(8,128)(2,1)S(1)} %get-tuple-element.25), channel_id=1, source_target_pairs={{0,56},{8,0},{16,8},{24,16},{32,24},{40,32},{48,40},{56,48},{64,12... | collective-permute-start | bytes 884744 | tf_op jit(solution)/shard_map/ppermute | solution.py:476
  66.9 2.8 %all-to-all-done.1 = bf16[32,24,128]{2,1,0:T(8,128)(2,1)S(1)} async-done(((bf16[32,24,128]{2,1,0:T(8,128)(2,1)}), bf16[32,24,128]{2,1,0:T(8,128)(2,1)S(1)}, u32[]{:S(2)}, u32[]{:S(2)}) %all-to-all-start.1) | async-done | bytes 196640 | tf_op jit(solution)/shard_map/all_to_all | solution.py:627
  69.7 5.7 %collective-permute-done.15.refs_0_.refs_4_ = bf16[384,384]{1,0:T(8,128)(2,1)S(1)} collective-permute-done((bf16[384,384]{1,0:T(8,128)(2,1)}, bf16[384,384]{1,0:T(8,128)(2,1)S(1)}, u32[]{:S(2)}, u32[]{:S(2)}) %collective-permute-start.15) | collective-permute-done | bytes 294944 | tf_op jit(solution)/shard_map/ppermute | solution.py:476
  75.5 0.9 shard_map.108
  76.4 1.3 %collective-permute-start.2 = (bf16[768,128]{1,0:T(8,128)(2,1)S(1)}, bf16[768,128]{1,0:T(8,128)(2,1)S(1)}, u32[]{:S(2)}, u32[]{:S(2)}) collective-permute-start(bf16[768,128]{1,0:T(8,128)(2,1)S(1)} %bitcast.48), channel_id=1, source_target_pairs={{0,2},{1,3},{2,4},{3,5},{4,6},{5,7},{6,0},{7,1},{8,10},{9,11},{10,... | collective-permute-start | bytes 589832 | tf_op jit(solution)/shard_map/ppermute | solution.py:609
  77.8 2.8 %collective-permute-start.3 = (bf16[768,128]{1,0:T(8,128)(2,1)S(1)}, bf16[768,128]{1,0:T(8,128)(2,1)S(1)}, u32[]{:S(2)}, u32[]{:S(2)}) collective-permute-start(bf16[768,128]{1,0:T(8,128)(2,1)S(1)} %bitcast.49), channel_id=1, source_target_pairs={{0,4},{1,5},{2,6},{3,7},{4,0},{5,1},{6,2},{7,3},{8,12},{9,13},{10,... | collective-permute-start | bytes 589832 | tf_op jit(solution)/shard_map/ppermute | solution.py:609
  80.7 4.3 %collective-permute-done.17.refs_5_ = bf16[384,384]{1,0:T(8,128)(2,1)} collective-permute-done((bf16[384,384]{1,0:T(8,128)(2,1)}, bf16[384,384]{1,0:T(8,128)(2,1)}, u32[]{:S(2)}, u32[]{:S(2)}) %collective-permute-start.17) | collective-permute-done | bytes 294944 | tf_op jit(solution)/shard_map/ppermute | solution.py:476
  84.9 1.2 %shard_map.109.refs_4_ = bf16[4,768,384]{2,1,0:T(8,128)(2,1)S(1)} custom-call(s32[4]{0:T(128)S(1)} %pad_add_fusion.block_ref, s32[8]{0:T(128)S(1)} %stack.55.row_ref, bf16[384,384]{1,0:T(8,128)(2,1)S(1)} %shard_map.105.refs_0_, bf16[384,384]{1,0:T(8,128)(2,1)S(1)} %collective-permute-done.8.refs_0_.refs_1_, ...), custom_call_target="tpu_custom_call" | custom-call | bytes 4718 | tf_op jit(solution)/shard_map/pallas_call | solution.py:315
  86.1 2.9 %shard_map.110 = (f32[768,384]{1,0:T(8,128)S(1)}, f32[768,384]{1,0:T(8,128)S(1)}) custom-call(s32[4]{0:T(128)S(1)} %and_select_fusion.1.which_ref, s32[1]{0:T(128)} %bitcast.side_ref, bf16[768,256]{1,0:T(8,128)(2,1)S(1)} %shard_map.103.refs_0_, bf16[768,256]{1,0:T(8,128)(2,1)S(1)} %copy-done.5, bf16[768,256]{1,0:T(8,128)(2,1)} %collective-permute-done.13.refs_2_, ...), custom_call_target="tpu_custom_call" | custom-call | flops 1207959 | bytes 3538 | tf_op jit(solution)/shard_map/pallas_call | solution.py:344
  89.1 1.3 %shard_map.112 = bf16[768,384]{1,0:T(8,128)(2,1)S(1)} custom-call(s32[4]{0:T(128)S(1)} %and_select_fusion.1.which_ref, s32[1]{0:T(128)S(6)} %sub.71.side_ref, bf16[768,128]{1,0:T(8,128)(2,1)S(1)} %bitcast.51, bf16[768,128]{1,0:T(8,128)(2,1)S(1)} %collective-permute-done.2.refs_1_, bf16[768,128]{1,0:T(8,128)(2,1)S(1)} %collective-permute-done.3.refs_2_, ...), custom_call_target="tpu_custom_call" | custom-call | flops 301989 | bytes 1769 | tf_op jit(solution)/shard_map/pallas_call | solution.py:372
  90.5 2.4 %collective-permute-start.18 = (bf16[768,384]{1,0:T(8,128)(2,1)S(1)}, bf16[768,384]{1,0:T(8,128)(2,1)S(1)}, u32[]{:S(2)}, u32[]{:S(2)}) collective-permute-start(bf16[768,384]{1,0:T(8,128)(2,1)S(1)} %shard_map.112), channel_id=1, source_target_pairs={{0,1},{1,0},{2,3},{3,2},{4,5},{5,4},{6,7},{7,6},{8,9},{9,8},{10,11... | collective-permute-start | bytes 1769480 | tf_op jit(solution)/shard_map/ppermute | solution.py:651
  92.9 1.3 %shard_map.111.own_ref = f32[768,384]{1,0:T(8,128)S(1)} custom-call(s32[4]{0:T(128)S(1)} %and_select_fusion.1.which_ref, s32[1]{0:T(128)} %bitcast.side_ref, bf16[768,128]{1,0:T(8,128)(2,1)S(1)} %bitcast.52, bf16[768,128]{1,0:T(8,128)(2,1)S(1)} %collective-permute-done.2.refs_1_, bf16[768,128]{1,0:T(8,128)(2,1)S(1)} %collective-permute-done.3.refs_2_, ...), custom_call_target="tpu_custom_call" | custom-call | flops 301989 | bytes 1769 | tf_op jit(solution)/shard_map/pallas_call | solution.py:372
  94.6 0.9 shard_map.113
  (70 shorter events, 5.6 us)
Async XLA Ops:
  0.0 22.2 %copy-start = (s32[16,12,12]{2,0,1:T(8,128)S(1)}, s32[16,12,12]{2,0,1:T(8,128)}, u32[]{:S(2)}) copy-start(s32[16,12,12]{2,0,1:T(8,128)} %param.13) | copy-start | bytes 27652
  3.2 19.0 %copy-start.7 = (s32[12,16,16]{2,1,0:T(8,128)S(1)}, s32[12,16,16]{2,1,0:T(8,128)}, u32[]{:S(2)}) copy-start(s32[12,16,16]{2,1,0:T(8,128)} %param.14) | copy-start | bytes 36868
  3.3 24.0 %copy-start.9 = (s32[48]{0:T(128)S(1)}, s32[48]{0:T(128)}, u32[]{:S(2)}) copy-start(s32[48]{0:T(128)} %constant.184.clone) | copy-start | bytes 580
  3.3 35.0 %collective-permute-start = (bf16[768,512]{1,0:T(8,128)(2,1)}, bf16[768,512]{1,0:T(8,128)(2,1)}, u32[]{:S(2)}, u32[]{:S(2)}) collective-permute-start(bf16[768,512]{1,0:T(8,128)(2,1)} %get-tuple-element.18.refs_1_), channel_id=1, source_target_pairs={{0,8},{8,0},{16,24},{24,16},{32,40},{40,32},{48,56},{56,48},{64,72... | collective-permute-start | bytes 2359304 | tf_op jit(solution)/shard_map/ppermute | solution.py:567
  7.2 15.2 %collective-permute-start.1 = (bf16[96,384]{1,0:T(8,128)(2,1)}, bf16[96,384]{1,0:T(8,128)(2,1)S(1)}, u32[]{:S(2)}, u32[]{:S(2)}) collective-permute-start(bf16[96,384]{1,0:T(8,128)(2,1)} %shard_map.101), channel_id=1, source_target_pairs={{0,0},{1,1},{2,64},{3,65},{4,128},{5,129},{6,192},{7,193},{8,8},{9... | collective-permute-start | bytes 221192 | tf_op jit(solution)/shard_map/ppermute | solution.py:503
  8.8 26.3 %copy-start.1 = (bf16[1,768,384]{2,1,0:T(8,128)(2,1)S(1)}, bf16[1,768,384]{2,1,0:T(8,128)(2,1)}, u32[]{:S(2)}) copy-start(bf16[1,768,384]{2,1,0:T(8,128)(2,1)} %param.10) | copy-start | bytes 1769476
  8.8 26.3 %copy-start.2 = (bf16[1,768,384]{2,1,0:T(8,128)(2,1)S(1)}, bf16[1,768,384]{2,1,0:T(8,128)(2,1)}, u32[]{:S(2)}) copy-start(bf16[1,768,384]{2,1,0:T(8,128)(2,1)} %param.11) | copy-start | bytes 1769476
  8.8 26.3 %copy-start.3 = (bf16[1,768,384]{2,1,0:T(8,128)(2,1)S(1)}, bf16[1,768,384]{2,1,0:T(8,128)(2,1)}, u32[]{:S(2)}) copy-start(bf16[1,768,384]{2,1,0:T(8,128)(2,1)} %param.12) | copy-start | bytes 1769476
  8.8 37.1 %all-to-all-start = ((bf16[32,24,384]{2,1,0:T(8,128)(2,1)}), bf16[32,24,384]{2,1,0:T(8,128)(2,1)S(1)}, u32[]{:S(2)}, u32[]{:S(2)}) async-start(bf16[32,24,384]{2,1,0:T(8,128)(2,1)} %bitcast.55), calls=%async_computation | async-start | bytes 1179648 | tf_op jit(solution)/shard_map/all_to_all | solution.py:577
  22.4 5.3 %collective-permute-start.5 = (bf16[96,384]{1,0:T(8,128)(2,1)S(1)}, bf16[96,384]{1,0:T(8,128)(2,1)S(1)}, u32[]{:S(2)}, u32[]{:S(2)}) collective-permute-start(bf16[96,384]{1,0:T(8,128)(2,1)S(1)} %collective-permute-done.1.refs_0_), channel_id=1, source_target_pairs={{0,64},{8,72},{16,80},{24,88},{32,96},{40,104},{48,112},{56,120},{... | collective-permute-start | bytes 221192 | tf_op jit(solution)/shard_map/ppermute | solution.py:472
  23.7 6.8 %collective-permute-start.6 = (bf16[96,384]{1,0:T(8,128)(2,1)S(1)}, bf16[96,384]{1,0:T(8,128)(2,1)S(1)}, u32[]{:S(2)}, u32[]{:S(2)}) collective-permute-start(bf16[96,384]{1,0:T(8,128)(2,1)S(1)} %collective-permute-done.1.refs_0_), channel_id=1, source_target_pairs={{0,128},{8,136},{16,144},{24,152},{32,160},{40,168},{48,176},{56,1... | collective-permute-start | bytes 221192 | tf_op jit(solution)/shard_map/ppermute | solution.py:472
  26.1 4.6 %collective-permute-start.7 = (bf16[96,384]{1,0:T(8,128)(2,1)S(1)}, bf16[96,384]{1,0:T(8,128)(2,1)S(1)}, u32[]{:S(2)}, u32[]{:S(2)}) collective-permute-start(bf16[96,384]{1,0:T(8,128)(2,1)S(1)} %collective-permute-done.1.refs_0_), channel_id=1, source_target_pairs={{0,192},{8,200},{16,208},{24,216},{32,224},{40,232},{48,240},{56,2... | collective-permute-start | bytes 221192 | tf_op jit(solution)/shard_map/ppermute | solution.py:472
  30.8 18.2 %collective-permute-start.8 = (bf16[384,384]{1,0:T(8,128)(2,1)S(1)}, bf16[384,384]{1,0:T(8,128)(2,1)S(1)}, u32[]{:S(2)}, u32[]{:S(2)}) collective-permute-start(bf16[384,384]{1,0:T(8,128)(2,1)S(1)} %shard_map.105.refs_0_), channel_id=1, source_target_pairs={{0,8},{8,16},{16,24},{24,32},{32,40},{40,48},{48,56},{56,0},{64,72... | collective-permute-start | bytes 884744 | tf_op jit(solution)/shard_map/ppermute | solution.py:476
  32.9 16.1 %collective-permute-start.9 = (bf16[384,384]{1,0:T(8,128)(2,1)S(1)}, bf16[384,384]{1,0:T(8,128)(2,1)S(1)}, u32[]{:S(2)}, u32[]{:S(2)}) collective-permute-start(bf16[384,384]{1,0:T(8,128)(2,1)S(1)} %shard_map.105.refs_0_), channel_id=1, source_target_pairs={{0,56},{8,0},{16,8},{24,16},{32,24},{40,32},{48,40},{56,48},{64,12... | collective-permute-start | bytes 884744 | tf_op jit(solution)/shard_map/ppermute | solution.py:476
  38.2 7.6 %copy-start.8 = (bf16[48,768]{1,0:T(8,128)(2,1)S(1)}, bf16[48,768]{1,0:T(8,128)(2,1)}, u32[]{:S(2)}) copy-start(bf16[48,768]{1,0:T(8,128)(2,1)} %constant.186.clone) | copy-start | bytes 221188
  38.3 7.6 %copy-start.6 = (bf16[768,64]{1,0:T(8,128)(2,1)S(1)}, bf16[768,64]{1,0:T(8,128)(2,1)}, u32[]{:S(2)}) copy-start(bf16[768,64]{1,0:T(8,128)(2,1)} %constant.185.clone.place_ref) | copy-start | bytes 294916
  42.5 17.9 %collective-permute-start.12 = (bf16[768,256]{1,0:T(8,128)(2,1)S(1)}, bf16[768,256]{1,0:T(8,128)(2,1)S(1)}, u32[]{:S(2)}, u32[]{:S(2)}) collective-permute-start(bf16[768,256]{1,0:T(8,128)(2,1)S(1)} %shard_map.103.refs_0_), channel_id=1, source_target_pairs={{0,2},{1,3},{2,4},{3,5},{4,6},{5,7},{6,0},{7,1},{8,10},{9,11},{10,... | collective-permute-start | bytes 1179656 | tf_op jit(solution)/shard_map/ppermute | solution.py:609
  43.3 17.1 %collective-permute-start.13 = (bf16[768,256]{1,0:T(8,128)(2,1)S(1)}, bf16[768,256]{1,0:T(8,128)(2,1)}, u32[]{:S(2)}, u32[]{:S(2)}) collective-permute-start(bf16[768,256]{1,0:T(8,128)(2,1)S(1)} %shard_map.103.refs_0_), channel_id=1, source_target_pairs={{0,4},{1,5},{2,6},{3,7},{4,0},{5,1},{6,2},{7,3},{8,12},{9,13},{10,... | collective-permute-start | bytes 1179656 | tf_op jit(solution)/shard_map/ppermute | solution.py:609
  44.8 18.0 %collective-permute-start.14 = (bf16[768,256]{1,0:T(8,128)(2,1)S(1)}, bf16[768,256]{1,0:T(8,128)(2,1)}, u32[]{:S(2)}, u32[]{:S(2)}) collective-permute-start(bf16[768,256]{1,0:T(8,128)(2,1)S(1)} %shard_map.103.refs_0_), channel_id=1, source_target_pairs={{0,6},{1,7},{2,0},{3,1},{4,2},{5,3},{6,4},{7,5},{8,14},{9,15},{10,... | collective-permute-start | bytes 1179656 | tf_op jit(solution)/shard_map/ppermute | solution.py:609
  49.0 14.4 %collective-permute-start.10 = (bf16[384,384]{1,0:T(8,128)(2,1)S(1)}, bf16[384,384]{1,0:T(8,128)(2,1)S(1)}, u32[]{:S(2)}, u32[]{:S(2)}) collective-permute-start(bf16[384,384]{1,0:T(8,128)(2,1)S(1)} %get-tuple-element.22), channel_id=1, source_target_pairs={{0,8},{8,16},{16,24},{24,32},{32,40},{40,48},{48,56},{56,0},{64,72... | collective-permute-start | bytes 884744 | tf_op jit(solution)/shard_map/ppermute | solution.py:476
  49.1 14.3 %collective-permute-start.11 = (bf16[384,384]{1,0:T(8,128)(2,1)S(1)}, bf16[384,384]{1,0:T(8,128)(2,1)S(1)}, u32[]{:S(2)}, u32[]{:S(2)}) collective-permute-start(bf16[384,384]{1,0:T(8,128)(2,1)S(1)} %get-tuple-element.23), channel_id=1, source_target_pairs={{0,56},{8,0},{16,8},{24,16},{32,24},{40,32},{48,40},{56,48},{64,12... | collective-permute-start | bytes 884744 | tf_op jit(solution)/shard_map/ppermute | solution.py:476
  51.8 17.9 %all-to-all-start.1 = ((bf16[32,24,128]{2,1,0:T(8,128)(2,1)}), bf16[32,24,128]{2,1,0:T(8,128)(2,1)S(1)}, u32[]{:S(2)}, u32[]{:S(2)}) async-start(bf16[32,24,128]{2,1,0:T(8,128)(2,1)} %bitcast.13), calls=%async_computation.1 | async-start | bytes 393216 | tf_op jit(solution)/shard_map/all_to_all | solution.py:627
  60.4 3.9 %copy-start.4 = (bf16[768,256]{1,0:T(8,128)(2,1)}, bf16[768,256]{1,0:T(8,128)(2,1)S(1)}, u32[]{:S(2)}) copy-start(bf16[768,256]{1,0:T(8,128)(2,1)S(1)} %collective-permute-done.12.refs_1_) | copy-start | bytes 1179652
  64.2 11.2 %collective-permute-start.15 = (bf16[384,384]{1,0:T(8,128)(2,1)}, bf16[384,384]{1,0:T(8,128)(2,1)S(1)}, u32[]{:S(2)}, u32[]{:S(2)}) collective-permute-start(bf16[384,384]{1,0:T(8,128)(2,1)} %get-tuple-element.24), channel_id=1, source_target_pairs={{0,8},{8,16},{16,24},{24,32},{32,40},{40,48},{48,56},{56,0},{64,72... | collective-permute-start | bytes 884744 | tf_op jit(solution)/shard_map/ppermute | solution.py:476
  64.2 11.2 %collective-permute-start.16 = (bf16[384,384]{1,0:T(8,128)(2,1)S(1)}, bf16[384,384]{1,0:T(8,128)(2,1)S(1)}, u32[]{:S(2)}, u32[]{:S(2)}) collective-permute-start(bf16[384,384]{1,0:T(8,128)(2,1)S(1)} %get-tuple-element.25), channel_id=1, source_target_pairs={{0,56},{8,0},{16,8},{24,16},{32,24},{40,32},{48,40},{56,48},{64,12... | collective-permute-start | bytes 884744 | tf_op jit(solution)/shard_map/ppermute | solution.py:476
  76.4 8.6 %collective-permute-start.17 = (bf16[384,384]{1,0:T(8,128)(2,1)}, bf16[384,384]{1,0:T(8,128)(2,1)}, u32[]{:S(2)}, u32[]{:S(2)}) collective-permute-start(bf16[384,384]{1,0:T(8,128)(2,1)} %get-tuple-element.26), channel_id=1, source_target_pairs={{0,8},{8,16},{16,24},{24,32},{32,40},{40,48},{48,56},{56,0},{64,72... | collective-permute-start | bytes 884744 | tf_op jit(solution)/shard_map/ppermute | solution.py:476
  76.4 12.7 %collective-permute-start.2 = (bf16[768,128]{1,0:T(8,128)(2,1)S(1)}, bf16[768,128]{1,0:T(8,128)(2,1)S(1)}, u32[]{:S(2)}, u32[]{:S(2)}) collective-permute-start(bf16[768,128]{1,0:T(8,128)(2,1)S(1)} %bitcast.48), channel_id=1, source_target_pairs={{0,2},{1,3},{2,4},{3,5},{4,6},{5,7},{6,0},{7,1},{8,10},{9,11},{10,... | collective-permute-start | bytes 589832 | tf_op jit(solution)/shard_map/ppermute | solution.py:609
  77.8 11.3 %collective-permute-start.3 = (bf16[768,128]{1,0:T(8,128)(2,1)S(1)}, bf16[768,128]{1,0:T(8,128)(2,1)S(1)}, u32[]{:S(2)}, u32[]{:S(2)}) collective-permute-start(bf16[768,128]{1,0:T(8,128)(2,1)S(1)} %bitcast.49), channel_id=1, source_target_pairs={{0,4},{1,5},{2,6},{3,7},{4,0},{5,1},{6,2},{7,3},{8,12},{9,13},{10,... | collective-permute-start | bytes 589832 | tf_op jit(solution)/shard_map/ppermute | solution.py:609
  80.6 8.5 %collective-permute-start.4 = (bf16[768,128]{1,0:T(8,128)(2,1)S(1)}, bf16[768,128]{1,0:T(8,128)(2,1)S(1)}, u32[]{:S(2)}, u32[]{:S(2)}) collective-permute-start(bf16[768,128]{1,0:T(8,128)(2,1)S(1)} %bitcast.50), channel_id=1, source_target_pairs={{0,6},{1,7},{2,0},{3,1},{4,2},{5,3},{6,4},{7,5},{8,14},{9,15},{10,... | collective-permute-start | bytes 589832 | tf_op jit(solution)/shard_map/ppermute | solution.py:609
  80.7 5.5 %copy-start.5 = (bf16[768,256]{1,0:T(8,128)(2,1)S(1)}, bf16[768,256]{1,0:T(8,128)(2,1)}, u32[]{:S(2)}) copy-start(bf16[768,256]{1,0:T(8,128)(2,1)} %copy-done.4) | copy-start | bytes 1179652
  90.5 4.1 %collective-permute-start.18 = (bf16[768,384]{1,0:T(8,128)(2,1)S(1)}, bf16[768,384]{1,0:T(8,128)(2,1)S(1)}, u32[]{:S(2)}, u32[]{:S(2)}) collective-permute-start(bf16[768,384]{1,0:T(8,128)(2,1)S(1)} %shard_map.112), channel_id=1, source_target_pairs={{0,1},{1,0},{2,3},{3,2},{4,5},{5,4},{6,7},{7,6},{8,9},{9,8},{10,11... | collective-permute-start | bytes 1769480 | tf_op jit(solution)/shard_map/ppermute | solution.py:651

commit v3 on v2

--- a/solution.py
+++ b/solution.py
@@ -15,7 +15,7 @@
 ALL_VMEM = 60 * 1024 * 1024
 BF16 = jnp.bfloat16
 F32 = jnp.float32
-CFG = {'w': 'zlast2', 'pick': 'kvt', 'order': ['kv', 'packed', 'w', 'own', 'r', 'spat', 'x', 'time', 'r', 'r', 'r'], 'after': {'w': ['kv'], 'own': ['first'], 'time': ['spat'], 'r2': ['time'], 'r3': ['x1', 'x2', 'x3'], 'r4': ['returned']}}
+CFG = {'w': 'zlast2', 'pick': 'kvt', 'order': ['kv', 'packed', 'w', 'own', 'r', 'spat', 'x', 'time', 'r', 'r', 'r'], 'after': {'w': ['kv'], 'own': ['first'], 'time': ['spat'], 'r2': ['time'], 'r3': ['x1', 'x2', 'x3'], 'r4': ['returned']}, 'tok': ['first', 'spat', 'returned']}
 LOG2E = math.log2(math.e)
 SCALE2 = LOG2E / math.sqrt(HD)
 NT = (((1,), (1,)), ((), ()))
@@ -284,17 +284,16 @@
 
 def gate(blocks, after):
     def body(*refs):
-        count = len(blocks)
-        for n in range(count):
-            refs[n - count][...] = refs[n][...]
+        pass
 
     return pl.pallas_call(
         body,
         out_shape=tuple(jax.ShapeDtypeStruct(b.shape, b.dtype) for b in blocks),
-        in_specs=[vmem()] * len(blocks) + [anywhere()] * len(after),
-        out_specs=(vmem(),) * len(blocks),
-        compiler_params=params(),
-        cost_estimate=cost(0, 4 * sum(b.size for b in blocks)),
+        in_specs=[anywhere()] * (len(blocks) + len(after)),
+        out_specs=(anywhere(),) * len(blocks),
+        input_output_aliases={n: n for n in range(len(blocks))},
+        compiler_params=params(),
+        cost_estimate=cost(0, 0),
     )(*blocks, *after)
 
 
@@ -526,17 +525,17 @@
 
     def ring_step():
         n = len(got["up"])
-        up, down = got["up"][-1], got["down"][-1]
         if CFG["after"].get(f"r{n}"):
-            if n == 1:
-                (up,) = gate([up], toks(f"r{n}"))
-                down = up
+            if n == zs // 2:
+                (got["up"][-1],) = gate([got["up"][-1]], toks(f"r{n}"))
             else:
-                up, down = gate([up, down], toks(f"r{n}"))
-        got["up"].append(along_z(up, 1))
+                got["up"][-1], got["down"][-1] = gate(
+                    [got["up"][-1], got["down"][-1]], toks(f"r{n}")
+                )
+        got["up"].append(along_z(got["up"][-1], 1))
         got[f"up{n}"] = got["up"][-1]
         if n < zs // 2:
-            got["down"].append(along_z(down, -1))
+            got["down"].append(along_z(got["down"][-1], -1))
         else:
             up, down = got["up"], got["down"]
             got["z"] = [up[0], up[1], down[1], *up[2:], *down[2:]]
@@ -556,7 +555,7 @@
             got["groups"] = [got["w_z"]]
 
     def toks(name):
-        return [got[n] if n == "kv" else token(got[n]) for n in CFG["after"].get(name, ())]
+        return [token(got[n]) if n in CFG.get("tok", ()) else got[n] for n in CFG["after"].get(name, ())]
 
     def make_kv():
         if CFG["pick"] in ("all", "kvw", "kvt"):

time: 96.2 us -> 93.8 us (0.975)
  Pallas kernels: 23.1 us -> 21 us
  local copies, waits for them, and re-layouts: 2.86 us -> 1.73 us
    ppermute x7, waiting for transfers between devices: 9.99 us -> 6.49 us  [along_z(): return lax.ppermute(block, 'seq', route)]
    ppermute x6, waiting for transfers between devices: 1.73 us -> 3.99 us  [along_x(): got.append(lax.ppermute(block, 'head', route))]
    slice x7 -> x3, local copies, waits for them, and re-layouts: 2.04 us -> 0.01 us  [token(): return block[:16, :HD]]
    pallas_call x3, Pallas kernels: 1.7 us -> 0.01 us  [gate(): pl.pallas_call(body, out_shape=tuple((jax.ShapeDtypeStruct(b.shape, b.dty...]
    all_to_all x1, waiting for transfers between devices: 2.83 us -> 4.31 us  [make_att(): lax.all_to_all(got['time'].reshape(seq_count, positions, HD), 'seq', 0, 0...]
  transfers between devices with their start and end apart: 21 -> 21, of which waited for: 7 -> 8; matrix products, arithmetic and copies ran while one was open for 3% -> 1% of each run, Pallas kernels for 18% -> 18%
where the time goes in v3:
time: 93.8 us; the launch traced here: 92.6 us
  starting transfers between devices  50.3 us (54%)
  Pallas kernels  21 us (22%)
  waiting for transfers between devices  18.1 us (19%)
  local copies, waits for them, and re-layouts  1.73 us (2%)
  between operations  1.19 us (1%)
    all_to_all x1, starting transfers between devices, make_time(): lax.all_to_all(block.reshape(seq_count, positions, 3 * HD), 'seq', 0, 0,...  13.4 us
    ppermute x7, starting transfers between devices, along_z(): return lax.ppermute(block, 'seq', route)  9.34 us
    all_to_all x1, starting transfers between devices, make_att(): lax.all_to_all(got['time'].reshape(seq_count, positions, HD), 'seq', 0, 0...  8.45 us
    ppermute x6, starting transfers between devices, along_x(): got.append(lax.ppermute(block, 'head', route))  8.14 us
    ppermute x7, waiting for transfers between devices, along_z(): return lax.ppermute(block, 'seq', route)  6.49 us
    ppermute x3, starting transfers between devices, along_y(): return lax.ppermute(block, 'seq', route)  4.82 us
    all_to_all x1, waiting for transfers between devices, make_att(): lax.all_to_all(got['time'].reshape(seq_count, positions, HD), 'seq', 0, 0...  4.31 us
    pallas_call x1, Pallas kernels, other_half(): pl.pallas_call(body, out_shape=jax.ShapeDtypeStruct((rows, 2 * HD), BF16)...  4.15 us
  transfers between devices with their start and end apart: 21, of which 8 were waited for; matrix products, arithmetic and copies ran while one was open for 1% of the time, Pallas kernels for 18%

profile of v3, /device:TPU:1, one launch (start us, length us, event | category | flops | bytes accessed | tf_op | source)
XLA Modules:
  0.0 92.6 jit_solution(10478548081038077445)
XLA Ops:
  0.7 2.5 %shard_map.100 = (bf16[768,512]{1,0:T(8,128)(2,1)}, bf16[768,384]{1,0:T(8,128)(2,1)}) custom-call(s32[1]{0:T(128)S(6)} %copy.32.heads_ref.order_ref, bf16[768,384]{1,0:T(8,128)(2,1)} %bitcast.43, bf16[768,384]{1,0:T(8,128)(2,1)} %bitcast.45, bf16[768,384]{1,0:T(8,128)(2,1)} %bitcast.39), custom_call_target="tpu_custom_call" | custom-call | bytes 2752 | tf_op jit(solution)/shard_map/pallas_call | solution.py:105
  3.3 2.6 %collective-permute-start = (bf16[768,512]{1,0:T(8,128)(2,1)}, bf16[768,512]{1,0:T(8,128)(2,1)}, u32[]{:S(2)}, u32[]{:S(2)}) collective-permute-start(bf16[768,512]{1,0:T(8,128)(2,1)} %get-tuple-element.17.refs_1_), channel_id=1, source_target_pairs={{0,8},{8,0},{16,24},{24,16},{32,40},{40,32},{48,56},{56,48},{64,72... | collective-permute-start | bytes 2359304 | tf_op jit(solution)/shard_map/ppermute | solution.py:566
  5.8 1.4 %shard_map.101 = bf16[96,384]{1,0:T(8,128)(2,1)} custom-call(s32[1]{0:T(128)S(6)} %copy.32.heads_ref.order_ref, bf16[96,384]{1,0:T(8,128)(2,1)} %bitcast.58, bf16[768,512]{1,0:T(8,128)(2,1)} %get-tuple-element.17.refs_1_), custom_call_target="tpu_custom_call" | custom-call | bytes 147 | tf_op jit(solution)/shard_map/pallas_call | solution.py:105
  7.3 1.5 %collective-permute-start.1 = (bf16[96,384]{1,0:T(8,128)(2,1)}, bf16[96,384]{1,0:T(8,128)(2,1)S(1)}, u32[]{:S(2)}, u32[]{:S(2)}) collective-permute-start(bf16[96,384]{1,0:T(8,128)(2,1)} %shard_map.101), channel_id=1, source_target_pairs={{0,0},{1,1},{2,64},{3,65},{4,128},{5,129},{6,192},{7,193},{8,8},{9... | collective-permute-start | bytes 221192 | tf_op jit(solution)/shard_map/ppermute | solution.py:502
  8.8 13.4 %all-to-all-start = ((bf16[32,24,384]{2,1,0:T(8,128)(2,1)}), bf16[32,24,384]{2,1,0:T(8,128)(2,1)S(1)}, u32[]{:S(2)}, u32[]{:S(2)}) async-start(bf16[32,24,384]{2,1,0:T(8,128)(2,1)} %bitcast.55), calls=%async_computation | async-start | bytes 1179648 | tf_op jit(solution)/shard_map/all_to_all | solution.py:576
  22.5 1.2 %collective-permute-start.5 = (bf16[96,384]{1,0:T(8,128)(2,1)S(1)}, bf16[96,384]{1,0:T(8,128)(2,1)S(1)}, u32[]{:S(2)}, u32[]{:S(2)}) collective-permute-start(bf16[96,384]{1,0:T(8,128)(2,1)S(1)} %collective-permute-done.1.refs_0_), channel_id=1, source_target_pairs={{0,64},{8,72},{16,80},{24,88},{32,96},{40,104},{48,112},{56,120},{... | collective-permute-start | bytes 221192 | tf_op jit(solution)/shard_map/ppermute | solution.py:471
  23.7 2.4 %collective-permute-start.6 = (bf16[96,384]{1,0:T(8,128)(2,1)S(1)}, bf16[96,384]{1,0:T(8,128)(2,1)S(1)}, u32[]{:S(2)}, u32[]{:S(2)}) collective-permute-start(bf16[96,384]{1,0:T(8,128)(2,1)S(1)} %collective-permute-done.1.refs_0_), channel_id=1, source_target_pairs={{0,128},{8,136},{16,144},{24,152},{32,160},{40,168},{48,176},{56,1... | collective-permute-start | bytes 221192 | tf_op jit(solution)/shard_map/ppermute | solution.py:471
  26.1 1.1 %collective-permute-start.7 = (bf16[96,384]{1,0:T(8,128)(2,1)S(1)}, bf16[96,384]{1,0:T(8,128)(2,1)S(1)}, u32[]{:S(2)}, u32[]{:S(2)}) collective-permute-start(bf16[96,384]{1,0:T(8,128)(2,1)S(1)} %collective-permute-done.1.refs_0_), channel_id=1, source_target_pairs={{0,192},{8,200},{16,208},{24,216},{32,224},{40,232},{48,240},{56,2... | collective-permute-start | bytes 221192 | tf_op jit(solution)/shard_map/ppermute | solution.py:471
  27.8 2.7 %collective-permute-done.6.refs_2_ = bf16[96,384]{1,0:T(8,128)(2,1)S(1)} collective-permute-done((bf16[96,384]{1,0:T(8,128)(2,1)S(1)}, bf16[96,384]{1,0:T(8,128)(2,1)S(1)}, u32[]{:S(2)}, u32[]{:S(2)}) %collective-permute-start.6) | collective-permute-done | bytes 73760 | tf_op jit(solution)/shard_map/ppermute | solution.py:471
  30.8 2.1 %collective-permute-start.8 = (bf16[384,384]{1,0:T(8,128)(2,1)S(1)}, bf16[384,384]{1,0:T(8,128)(2,1)S(1)}, u32[]{:S(2)}, u32[]{:S(2)}) collective-permute-start(bf16[384,384]{1,0:T(8,128)(2,1)S(1)} %shard_map.105.refs_0_), channel_id=1, source_target_pairs={{0,8},{8,16},{16,24},{24,32},{32,40},{40,48},{48,56},{56,0},{64,72... | collective-permute-start | bytes 884744 | tf_op jit(solution)/shard_map/ppermute | solution.py:475
  32.9 1.9 %collective-permute-start.9 = (bf16[384,384]{1,0:T(8,128)(2,1)S(1)}, bf16[384,384]{1,0:T(8,128)(2,1)S(1)}, u32[]{:S(2)}, u32[]{:S(2)}) collective-permute-start(bf16[384,384]{1,0:T(8,128)(2,1)S(1)} %shard_map.105.refs_0_), channel_id=1, source_target_pairs={{0,56},{8,0},{16,8},{24,16},{32,24},{40,32},{48,40},{56,48},{64,12... | collective-permute-start | bytes 884744 | tf_op jit(solution)/shard_map/ppermute | solution.py:475
  35.1 3.1 %shard_map.102 = (f32[2,128,768]{2,1,0:T(8,128)S(1)}, f32[2,768]{1,0:T(2,128)S(1)}, f32[2,768]{1,0:T(2,128)S(1)}) custom-call(s32[1]{0:T(128)S(6)} %copy.32.heads_ref.order_ref, bf16[768,384]{1,0:T(8,128)(2,1)S(1)} %bitcast.40, bf16[768,384]{1,0:T(8,128)(2,1)S(1)} %bitcast.44, bf16[768,384]{1,0:T(8,128)(2,1)S(1)} %bitcast.46, f32[12,768]{1,0:T(8,128)S(1)} %bitcast.53, ...), custom_call_target="tpu_custom_call" | custom-call | flops 603979 | bytes 3145 | tf_op jit(solution)/shard_map/pallas_call | solution.py:174
  38.3 4.2 %shard_map.103.refs_0_ = bf16[768,256]{1,0:T(8,128)(2,1)S(1)} custom-call(s32[1]{0:T(128)S(6)} %copy.32.heads_ref.order_ref, bf16[768,384]{1,0:T(8,128)(2,1)S(1)} %bitcast.41, bf16[768,512]{1,0:T(8,128)(2,1)} %collective-permute-done.kv_ref, f32[12,768]{1,0:T(8,128)S(1)} %bitcast.54, f32[2,128,768]{2,1,0:T(8,128)S(1)} %get-tuple-element.18.o_ref, ...), custom_call_target="tpu_custom_call" | custom-call | flops 603979 | bytes 3145 | tf_op jit(solution)/shard_map/pallas_call | solution.py:225
  43.3 1.5 %collective-permute-start.13 = (bf16[768,256]{1,0:T(8,128)(2,1)S(1)}, bf16[768,256]{1,0:T(8,128)(2,1)S(1)}, u32[]{:S(2)}, u32[]{:S(2)}) collective-permute-start(bf16[768,256]{1,0:T(8,128)(2,1)S(1)} %shard_map.103.refs_0_), channel_id=1, source_target_pairs={{0,4},{1,5},{2,6},{3,7},{4,0},{5,1},{6,2},{7,3},{8,12},{9,13},{10,... | collective-permute-start | bytes 1179656 | tf_op jit(solution)/shard_map/ppermute | solution.py:608
  44.8 1.0 %collective-permute-start.14 = (bf16[768,256]{1,0:T(8,128)(2,1)S(1)}, bf16[768,256]{1,0:T(8,128)(2,1)S(1)}, u32[]{:S(2)}, u32[]{:S(2)}) collective-permute-start(bf16[768,256]{1,0:T(8,128)(2,1)S(1)} %shard_map.103.refs_0_), channel_id=1, source_target_pairs={{0,6},{1,7},{2,0},{3,1},{4,2},{5,3},{6,4},{7,5},{8,14},{9,15},{10,... | collective-permute-start | bytes 1179656 | tf_op jit(solution)/shard_map/ppermute | solution.py:608
  45.8 0.9 copy-done.4
  46.7 2.4 %shard_map.104.refs_2_ = bf16[768,128]{1,0:T(8,128)(2,1)} custom-call(bf16[768,384]{1,0:T(8,128)(2,1)S(1)} %bitcast.42, bf16[64,768]{1,0:T(8,128)(2,1)S(1)} %pad_maximum_fusion.rule_ref, bf16[768,64]{1,0:T(8,128)(2,1)S(1)} %copy-done.4, bf16[16,128]{1,0:T(8,128)(2,1)S(1)} %slice.23.refs_0_), custom_call_target="tpu_custom_call" | custom-call | flops 301989 | bytes 786 | tf_op jit(solution)/shard_map/pallas_call | solution.py:254
  49.2 2.7 %collective-permute-start.11 = (bf16[384,384]{1,0:T(8,128)(2,1)S(1)}, bf16[384,384]{1,0:T(8,128)(2,1)S(1)}, u32[]{:S(2)}, u32[]{:S(2)}) collective-permute-start(bf16[384,384]{1,0:T(8,128)(2,1)S(1)} %get-tuple-element.22.refs_2_), channel_id=1, source_target_pairs={{0,56},{8,0},{16,8},{24,16},{32,24},{40,32},{48,40},{56,48},{64,12... | collective-permute-start | bytes 884744 | tf_op jit(solution)/shard_map/ppermute | solution.py:475
  51.9 8.4 %all-to-all-start.1 = ((bf16[32,24,128]{2,1,0:T(8,128)(2,1)}), bf16[32,24,128]{2,1,0:T(8,128)(2,1)S(1)}, u32[]{:S(2)}, u32[]{:S(2)}) async-start(bf16[32,24,128]{2,1,0:T(8,128)(2,1)} %bitcast.13), calls=%async_computation.1 | async-start | bytes 393216 | tf_op jit(solution)/shard_map/all_to_all | solution.py:626
  60.4 2.4 %collective-permute-done.14.refs_4_.refs_3_ = bf16[768,256]{1,0:T(8,128)(2,1)S(1)} collective-permute-done((bf16[768,256]{1,0:T(8,128)(2,1)S(1)}, bf16[768,256]{1,0:T(8,128)(2,1)S(1)}, u32[]{:S(2)}, u32[]{:S(2)}) %collective-permute-start.14) | collective-permute-done | bytes 393248 | tf_op jit(solution)/shard_map/ppermute | solution.py:608
  62.8 2.7 %collective-permute-start.17 = (bf16[384,384]{1,0:T(8,128)(2,1)S(1)}, bf16[384,384]{1,0:T(8,128)(2,1)}, u32[]{:S(2)}, u32[]{:S(2)}) collective-permute-start(bf16[384,384]{1,0:T(8,128)(2,1)S(1)} %get-tuple-element.24.refs_6_), channel_id=1, source_target_pairs={{0,56},{8,0},{16,8},{24,16},{32,24},{40,32},{48,40},{56,48},{64,12... | collective-permute-start | bytes 884744 | tf_op jit(solution)/shard_map/ppermute | solution.py:475
  65.4 4.3 %all-to-all-done.1 = bf16[32,24,128]{2,1,0:T(8,128)(2,1)S(1)} async-done(((bf16[32,24,128]{2,1,0:T(8,128)(2,1)}), bf16[32,24,128]{2,1,0:T(8,128)(2,1)S(1)}, u32[]{:S(2)}, u32[]{:S(2)}) %all-to-all-start.1) | async-done | bytes 196640 | tf_op jit(solution)/shard_map/all_to_all | solution.py:626
  69.8 3.8 %collective-permute-done.15.refs_0_ = bf16[384,384]{1,0:T(8,128)(2,1)} collective-permute-done((bf16[384,384]{1,0:T(8,128)(2,1)S(1)}, bf16[384,384]{1,0:T(8,128)(2,1)}, u32[]{:S(2)}, u32[]{:S(2)}) %collective-permute-start.15) | collective-permute-done | bytes 294944 | tf_op jit(solution)/shard_map/ppermute | solution.py:475
  73.6 2.2 %collective-permute-start.2 = (bf16[768,128]{1,0:T(8,128)(2,1)S(1)}, bf16[768,128]{1,0:T(8,128)(2,1)S(1)}, u32[]{:S(2)}, u32[]{:S(2)}) collective-permute-start(bf16[768,128]{1,0:T(8,128)(2,1)S(1)} %bitcast.48), channel_id=1, source_target_pairs={{0,2},{1,3},{2,4},{3,5},{4,6},{5,7},{6,0},{7,1},{8,10},{9,11},{10,... | collective-permute-start | bytes 589832 | tf_op jit(solution)/shard_map/ppermute | solution.py:608
  75.8 2.6 %collective-permute-start.3 = (bf16[768,128]{1,0:T(8,128)(2,1)S(1)}, bf16[768,128]{1,0:T(8,128)(2,1)S(1)}, u32[]{:S(2)}, u32[]{:S(2)}) collective-permute-start(bf16[768,128]{1,0:T(8,128)(2,1)S(1)} %bitcast.49), channel_id=1, source_target_pairs={{0,4},{1,5},{2,6},{3,7},{4,0},{5,1},{6,2},{7,3},{8,12},{9,13},{10,... | collective-permute-start | bytes 589832 | tf_op jit(solution)/shard_map/ppermute | solution.py:608
  78.5 2.7 %collective-permute-done.16.refs_5_ = bf16[384,384]{1,0:T(8,128)(2,1)} collective-permute-done((bf16[384,384]{1,0:T(8,128)(2,1)}, bf16[384,384]{1,0:T(8,128)(2,1)}, u32[]{:S(2)}, u32[]{:S(2)}) %collective-permute-start.16) | collective-permute-done | bytes 294944 | tf_op jit(solution)/shard_map/ppermute | solution.py:475
  81.2 1.4 %shard_map.109.refs_4_ = bf16[4,768,384]{2,1,0:T(8,128)(2,1)S(1)} custom-call(s32[4]{0:T(128)S(1)} %pad_add_fusion.block_ref, s32[8]{0:T(128)S(1)} %stack.55.row_ref, bf16[384,384]{1,0:T(8,128)(2,1)S(1)} %shard_map.105.refs_0_, bf16[384,384]{1,0:T(8,128)(2,1)S(1)} %get-tuple-element.21.refs_1_, bf16[384,384]{1,0:T(8,128)(2,1)S(1)} %get-tuple-element.22.refs_2_, ...), custom_call_target="tpu_custom_call" | custom-call | bytes 4718 | tf_op jit(solution)/shard_map/pallas_call | solution.py:314
  82.6 2.4 %shard_map.110 = (f32[768,384]{1,0:T(8,128)S(1)}, f32[768,384]{1,0:T(8,128)S(1)}) custom-call(s32[4]{0:T(128)S(1)} %and_select_fusion.1.which_ref, s32[1]{0:T(128)} %bitcast.side_ref, bf16[768,256]{1,0:T(8,128)(2,1)S(1)} %shard_map.103.refs_0_, bf16[768,256]{1,0:T(8,128)(2,1)S(1)} %collective-permute-done.12.refs_2_.refs_1_, ...), custom_call_target="tpu_custom_call" | custom-call | flops 1207959 | bytes 3538 | tf_op jit(solution)/shard_map/pallas_call | solution.py:343
  85.0 1.6 %collective-permute-done.3.refs_2_ = bf16[768,128]{1,0:T(8,128)(2,1)S(1)} collective-permute-done((bf16[768,128]{1,0:T(8,128)(2,1)S(1)}, bf16[768,128]{1,0:T(8,128)(2,1)S(1)}, u32[]{:S(2)}, u32[]{:S(2)}) %collective-permute-start.3) | collective-permute-done | bytes 196640 | tf_op jit(solution)/shard_map/ppermute | solution.py:608
  86.5 1.3 %shard_map.112 = bf16[768,384]{1,0:T(8,128)(2,1)S(1)} custom-call(s32[4]{0:T(128)S(1)} %and_select_fusion.1.which_ref, s32[1]{0:T(128)S(6)} %sub.71.side_ref, bf16[768,128]{1,0:T(8,128)(2,1)S(1)} %bitcast.51, bf16[768,128]{1,0:T(8,128)(2,1)S(1)} %collective-permute-done.2.refs_1_, bf16[768,128]{1,0:T(8,128)(2,1)S(1)} %collective-permute-done.3.refs_2_, ...), custom_call_target="tpu_custom_call" | custom-call | flops 301989 | bytes 1769 | tf_op jit(solution)/shard_map/pallas_call | solution.py:371
  87.9 2.0 %collective-permute-start.18 = (bf16[768,384]{1,0:T(8,128)(2,1)S(1)}, bf16[768,384]{1,0:T(8,128)(2,1)S(1)}, u32[]{:S(2)}, u32[]{:S(2)}) collective-permute-start(bf16[768,384]{1,0:T(8,128)(2,1)S(1)} %shard_map.112), channel_id=1, source_target_pairs={{0,1},{1,0},{2,3},{3,2},{4,5},{5,4},{6,7},{7,6},{8,9},{9,8},{10,11... | collective-permute-start | bytes 1769480 | tf_op jit(solution)/shard_map/ppermute | solution.py:650
  89.9 1.3 %shard_map.111.own_ref = f32[768,384]{1,0:T(8,128)S(1)} custom-call(s32[4]{0:T(128)S(1)} %and_select_fusion.1.which_ref, s32[1]{0:T(128)} %bitcast.side_ref, bf16[768,128]{1,0:T(8,128)(2,1)S(1)} %bitcast.52, bf16[768,128]{1,0:T(8,128)(2,1)S(1)} %collective-permute-done.2.refs_1_, bf16[768,128]{1,0:T(8,128)(2,1)S(1)} %collective-permute-done.3.refs_2_, ...), custom_call_target="tpu_custom_call" | custom-call | flops 301989 | bytes 1769 | tf_op jit(solution)/shard_map/pallas_call | solution.py:371
  (62 shorter events, 3.6 us)
Async XLA Ops:
  0.0 22.3 %copy-start = (s32[16,12,12]{2,0,1:T(8,128)S(1)}, s32[16,12,12]{2,0,1:T(8,128)}, u32[]{:S(2)}) copy-start(s32[16,12,12]{2,0,1:T(8,128)} %param.13) | copy-start | bytes 27652
  3.2 19.0 %copy-start.5 = (s32[12,16,16]{2,1,0:T(8,128)S(1)}, s32[12,16,16]{2,1,0:T(8,128)}, u32[]{:S(2)}) copy-start(s32[12,16,16]{2,1,0:T(8,128)} %param.14) | copy-start | bytes 36868
  3.3 24.0 %copy-start.7 = (s32[48]{0:T(128)S(1)}, s32[48]{0:T(128)}, u32[]{:S(2)}) copy-start(s32[48]{0:T(128)} %constant.184.clone) | copy-start | bytes 580
  3.3 35.0 %collective-permute-start = (bf16[768,512]{1,0:T(8,128)(2,1)}, bf16[768,512]{1,0:T(8,128)(2,1)}, u32[]{:S(2)}, u32[]{:S(2)}) collective-permute-start(bf16[768,512]{1,0:T(8,128)(2,1)} %get-tuple-element.17.refs_1_), channel_id=1, source_target_pairs={{0,8},{8,0},{16,24},{24,16},{32,40},{40,32},{48,56},{56,48},{64,72... | collective-permute-start | bytes 2359304 | tf_op jit(solution)/shard_map/ppermute | solution.py:566
  7.3 15.2 %collective-permute-start.1 = (bf16[96,384]{1,0:T(8,128)(2,1)}, bf16[96,384]{1,0:T(8,128)(2,1)S(1)}, u32[]{:S(2)}, u32[]{:S(2)}) collective-permute-start(bf16[96,384]{1,0:T(8,128)(2,1)} %shard_map.101), channel_id=1, source_target_pairs={{0,0},{1,1},{2,64},{3,65},{4,128},{5,129},{6,192},{7,193},{8,8},{9... | collective-permute-start | bytes 221192 | tf_op jit(solution)/shard_map/ppermute | solution.py:502
  8.8 26.3 %copy-start.1 = (bf16[1,768,384]{2,1,0:T(8,128)(2,1)S(1)}, bf16[1,768,384]{2,1,0:T(8,128)(2,1)}, u32[]{:S(2)}) copy-start(bf16[1,768,384]{2,1,0:T(8,128)(2,1)} %param.10) | copy-start | bytes 1769476
  8.8 26.3 %copy-start.2 = (bf16[1,768,384]{2,1,0:T(8,128)(2,1)S(1)}, bf16[1,768,384]{2,1,0:T(8,128)(2,1)}, u32[]{:S(2)}) copy-start(bf16[1,768,384]{2,1,0:T(8,128)(2,1)} %param.11) | copy-start | bytes 1769476
  8.8 26.3 %copy-start.3 = (bf16[1,768,384]{2,1,0:T(8,128)(2,1)S(1)}, bf16[1,768,384]{2,1,0:T(8,128)(2,1)}, u32[]{:S(2)}) copy-start(bf16[1,768,384]{2,1,0:T(8,128)(2,1)} %param.12) | copy-start | bytes 1769476
  8.8 37.0 %all-to-all-start = ((bf16[32,24,384]{2,1,0:T(8,128)(2,1)}), bf16[32,24,384]{2,1,0:T(8,128)(2,1)S(1)}, u32[]{:S(2)}, u32[]{:S(2)}) async-start(bf16[32,24,384]{2,1,0:T(8,128)(2,1)} %bitcast.55), calls=%async_computation | async-start | bytes 1179648 | tf_op jit(solution)/shard_map/all_to_all | solution.py:576
  22.5 5.3 %collective-permute-start.5 = (bf16[96,384]{1,0:T(8,128)(2,1)S(1)}, bf16[96,384]{1,0:T(8,128)(2,1)S(1)}, u32[]{:S(2)}, u32[]{:S(2)}) collective-permute-start(bf16[96,384]{1,0:T(8,128)(2,1)S(1)} %collective-permute-done.1.refs_0_), channel_id=1, source_target_pairs={{0,64},{8,72},{16,80},{24,88},{32,96},{40,104},{48,112},{56,120},{... | collective-permute-start | bytes 221192 | tf_op jit(solution)/shard_map/ppermute | solution.py:471
  23.7 6.8 %collective-permute-start.6 = (bf16[96,384]{1,0:T(8,128)(2,1)S(1)}, bf16[96,384]{1,0:T(8,128)(2,1)S(1)}, u32[]{:S(2)}, u32[]{:S(2)}) collective-permute-start(bf16[96,384]{1,0:T(8,128)(2,1)S(1)} %collective-permute-done.1.refs_0_), channel_id=1, source_target_pairs={{0,128},{8,136},{16,144},{24,152},{32,160},{40,168},{48,176},{56,1... | collective-permute-start | bytes 221192 | tf_op jit(solution)/shard_map/ppermute | solution.py:471
  26.1 4.6 %collective-permute-start.7 = (bf16[96,384]{1,0:T(8,128)(2,1)S(1)}, bf16[96,384]{1,0:T(8,128)(2,1)S(1)}, u32[]{:S(2)}, u32[]{:S(2)}) collective-permute-start(bf16[96,384]{1,0:T(8,128)(2,1)S(1)} %collective-permute-done.1.refs_0_), channel_id=1, source_target_pairs={{0,192},{8,200},{16,208},{24,216},{32,224},{40,232},{48,240},{56,2... | collective-permute-start | bytes 221192 | tf_op jit(solution)/shard_map/ppermute | solution.py:471
  30.8 18.4 %collective-permute-start.8 = (bf16[384,384]{1,0:T(8,128)(2,1)S(1)}, bf16[384,384]{1,0:T(8,128)(2,1)S(1)}, u32[]{:S(2)}, u32[]{:S(2)}) collective-permute-start(bf16[384,384]{1,0:T(8,128)(2,1)S(1)} %shard_map.105.refs_0_), channel_id=1, source_target_pairs={{0,8},{8,16},{16,24},{24,32},{32,40},{40,48},{48,56},{56,0},{64,72... | collective-permute-start | bytes 884744 | tf_op jit(solution)/shard_map/ppermute | solution.py:475
  32.9 16.3 %collective-permute-start.9 = (bf16[384,384]{1,0:T(8,128)(2,1)S(1)}, bf16[384,384]{1,0:T(8,128)(2,1)S(1)}, u32[]{:S(2)}, u32[]{:S(2)}) collective-permute-start(bf16[384,384]{1,0:T(8,128)(2,1)S(1)} %shard_map.105.refs_0_), channel_id=1, source_target_pairs={{0,56},{8,0},{16,8},{24,16},{32,24},{40,32},{48,40},{56,48},{64,12... | collective-permute-start | bytes 884744 | tf_op jit(solution)/shard_map/ppermute | solution.py:475
  38.3 7.5 %copy-start.6 = (bf16[48,768]{1,0:T(8,128)(2,1)S(1)}, bf16[48,768]{1,0:T(8,128)(2,1)}, u32[]{:S(2)}) copy-start(bf16[48,768]{1,0:T(8,128)(2,1)} %constant.186.clone) | copy-start | bytes 221188
  42.4 17.9 %collective-permute-start.12 = (bf16[768,256]{1,0:T(8,128)(2,1)S(1)}, bf16[768,256]{1,0:T(8,128)(2,1)S(1)}, u32[]{:S(2)}, u32[]{:S(2)}) collective-permute-start(bf16[768,256]{1,0:T(8,128)(2,1)S(1)} %shard_map.103.refs_0_), channel_id=1, source_target_pairs={{0,2},{1,3},{2,4},{3,5},{4,6},{5,7},{6,0},{7,1},{8,10},{9,11},{10,... | collective-permute-start | bytes 1179656 | tf_op jit(solution)/shard_map/ppermute | solution.py:608
  43.3 17.1 %collective-permute-start.13 = (bf16[768,256]{1,0:T(8,128)(2,1)S(1)}, bf16[768,256]{1,0:T(8,128)(2,1)S(1)}, u32[]{:S(2)}, u32[]{:S(2)}) collective-permute-start(bf16[768,256]{1,0:T(8,128)(2,1)S(1)} %shard_map.103.refs_0_), channel_id=1, source_target_pairs={{0,4},{1,5},{2,6},{3,7},{4,0},{5,1},{6,2},{7,3},{8,12},{9,13},{10,... | collective-permute-start | bytes 1179656 | tf_op jit(solution)/shard_map/ppermute | solution.py:608
  44.8 17.9 %collective-permute-start.14 = (bf16[768,256]{1,0:T(8,128)(2,1)S(1)}, bf16[768,256]{1,0:T(8,128)(2,1)S(1)}, u32[]{:S(2)}, u32[]{:S(2)}) collective-permute-start(bf16[768,256]{1,0:T(8,128)(2,1)S(1)} %shard_map.103.refs_0_), channel_id=1, source_target_pairs={{0,6},{1,7},{2,0},{3,1},{4,2},{5,3},{6,4},{7,5},{8,14},{9,15},{10,... | collective-permute-start | bytes 1179656 | tf_op jit(solution)/shard_map/ppermute | solution.py:608
  45.8 0.9 %copy-start.4 = (bf16[768,64]{1,0:T(8,128)(2,1)S(1)}, bf16[768,64]{1,0:T(8,128)(2,1)}, u32[]{:S(2)}) copy-start(bf16[768,64]{1,0:T(8,128)(2,1)} %constant.185.clone.place_ref) | copy-start | bytes 294916
  49.2 13.5 %collective-permute-start.10 = (bf16[384,384]{1,0:T(8,128)(2,1)S(1)}, bf16[384,384]{1,0:T(8,128)(2,1)S(1)}, u32[]{:S(2)}, u32[]{:S(2)}) collective-permute-start(bf16[384,384]{1,0:T(8,128)(2,1)S(1)} %get-tuple-element.21.refs_1_), channel_id=1, source_target_pairs={{0,8},{8,16},{16,24},{24,32},{32,40},{40,48},{48,56},{56,0},{64,72... | collective-permute-start | bytes 884744 | tf_op jit(solution)/shard_map/ppermute | solution.py:475
  49.2 13.5 %collective-permute-start.11 = (bf16[384,384]{1,0:T(8,128)(2,1)S(1)}, bf16[384,384]{1,0:T(8,128)(2,1)S(1)}, u32[]{:S(2)}, u32[]{:S(2)}) collective-permute-start(bf16[384,384]{1,0:T(8,128)(2,1)S(1)} %get-tuple-element.22.refs_2_), channel_id=1, source_target_pairs={{0,56},{8,0},{16,8},{24,16},{32,24},{40,32},{48,40},{56,48},{64,12... | collective-permute-start | bytes 884744 | tf_op jit(solution)/shard_map/ppermute | solution.py:475
  51.9 17.9 %all-to-all-start.1 = ((bf16[32,24,128]{2,1,0:T(8,128)(2,1)}), bf16[32,24,128]{2,1,0:T(8,128)(2,1)S(1)}, u32[]{:S(2)}, u32[]{:S(2)}) async-start(bf16[32,24,128]{2,1,0:T(8,128)(2,1)} %bitcast.13), calls=%async_computation.1 | async-start | bytes 393216 | tf_op jit(solution)/shard_map/all_to_all | solution.py:626
  62.8 10.8 %collective-permute-start.15 = (bf16[384,384]{1,0:T(8,128)(2,1)S(1)}, bf16[384,384]{1,0:T(8,128)(2,1)}, u32[]{:S(2)}, u32[]{:S(2)}) collective-permute-start(bf16[384,384]{1,0:T(8,128)(2,1)S(1)} %get-tuple-element.23.refs_3_), channel_id=1, source_target_pairs={{0,8},{8,16},{16,24},{24,32},{32,40},{40,48},{48,56},{56,0},{64,72... | collective-permute-start | bytes 884744 | tf_op jit(solution)/shard_map/ppermute | solution.py:475
  62.8 15.8 %collective-permute-start.17 = (bf16[384,384]{1,0:T(8,128)(2,1)S(1)}, bf16[384,384]{1,0:T(8,128)(2,1)}, u32[]{:S(2)}, u32[]{:S(2)}) collective-permute-start(bf16[384,384]{1,0:T(8,128)(2,1)S(1)} %get-tuple-element.24.refs_6_), channel_id=1, source_target_pairs={{0,56},{8,0},{16,8},{24,16},{32,24},{40,32},{48,40},{56,48},{64,12... | collective-permute-start | bytes 884744 | tf_op jit(solution)/shard_map/ppermute | solution.py:475
  73.5 7.7 %collective-permute-start.16 = (bf16[384,384]{1,0:T(8,128)(2,1)}, bf16[384,384]{1,0:T(8,128)(2,1)}, u32[]{:S(2)}, u32[]{:S(2)}) collective-permute-start(bf16[384,384]{1,0:T(8,128)(2,1)} %shard_map.108.refs_4_), channel_id=1, source_target_pairs={{0,8},{8,16},{16,24},{24,32},{32,40},{40,48},{48,56},{56,0},{64,72... | collective-permute-start | bytes 884744 | tf_op jit(solution)/shard_map/ppermute | solution.py:475
  73.6 11.3 %collective-permute-start.2 = (bf16[768,128]{1,0:T(8,128)(2,1)S(1)}, bf16[768,128]{1,0:T(8,128)(2,1)S(1)}, u32[]{:S(2)}, u32[]{:S(2)}) collective-permute-start(bf16[768,128]{1,0:T(8,128)(2,1)S(1)} %bitcast.48), channel_id=1, source_target_pairs={{0,2},{1,3},{2,4},{3,5},{4,6},{5,7},{6,0},{7,1},{8,10},{9,11},{10,... | collective-permute-start | bytes 589832 | tf_op jit(solution)/shard_map/ppermute | solution.py:608
  75.8 10.7 %collective-permute-start.3 = (bf16[768,128]{1,0:T(8,128)(2,1)S(1)}, bf16[768,128]{1,0:T(8,128)(2,1)S(1)}, u32[]{:S(2)}, u32[]{:S(2)}) collective-permute-start(bf16[768,128]{1,0:T(8,128)(2,1)S(1)} %bitcast.49), channel_id=1, source_target_pairs={{0,4},{1,5},{2,6},{3,7},{4,0},{5,1},{6,2},{7,3},{8,12},{9,13},{10,... | collective-permute-start | bytes 589832 | tf_op jit(solution)/shard_map/ppermute | solution.py:608
  78.4 8.1 %collective-permute-start.4 = (bf16[768,128]{1,0:T(8,128)(2,1)S(1)}, bf16[768,128]{1,0:T(8,128)(2,1)S(1)}, u32[]{:S(2)}, u32[]{:S(2)}) collective-permute-start(bf16[768,128]{1,0:T(8,128)(2,1)S(1)} %bitcast.50), channel_id=1, source_target_pairs={{0,6},{1,7},{2,0},{3,1},{4,2},{5,3},{6,4},{7,5},{8,14},{9,15},{10,... | collective-permute-start | bytes 589832 | tf_op jit(solution)/shard_map/ppermute | solution.py:608
  87.9 3.7 %collective-permute-start.18 = (bf16[768,384]{1,0:T(8,128)(2,1)S(1)}, bf16[768,384]{1,0:T(8,128)(2,1)S(1)}, u32[]{:S(2)}, u32[]{:S(2)}) collective-permute-start(bf16[768,384]{1,0:T(8,128)(2,1)S(1)} %shard_map.112), channel_id=1, source_target_pairs={{0,1},{1,0},{2,3},{3,2},{4,5},{5,4},{6,7},{7,6},{8,9},{9,8},{10,11... | collective-permute-start | bytes 1769480 | tf_op jit(solution)/shard_map/ppermute | solution.py:650

commit v4 on v3

--- a/solution.py
+++ b/solution.py
@@ -15,7 +15,6 @@
 ALL_VMEM = 60 * 1024 * 1024
 BF16 = jnp.bfloat16
 F32 = jnp.float32
-CFG = {'w': 'zlast2', 'pick': 'kvt', 'order': ['kv', 'packed', 'w', 'own', 'r', 'spat', 'x', 'time', 'r', 'r', 'r'], 'after': {'w': ['kv'], 'own': ['first'], 'time': ['spat'], 'r2': ['time'], 'r3': ['x1', 'x2', 'x3'], 'r4': ['returned']}, 'tok': ['first', 'spat', 'returned']}
 LOG2E = math.log2(math.e)
 SCALE2 = LOG2E / math.sqrt(HD)
 NT = (((1,), (1,)), ((), ()))
@@ -138,18 +137,18 @@
     return out
 
 
-def own_half(order, q, k, v, bias, after):
+def own_half(heads, q, k, v, bias, after):
     rows = q.shape[0]
     tile = 256
 
     def body(
-        order_ref, q_ref, k_ref, v_ref, bias_ref, *refs
+        heads_ref, q_ref, k_ref, v_ref, bias_ref, *refs
     ):
         o_ref, m_ref, l_ref, q_in, k_in, v_in, sems = refs[-7:]
         copies = [
             [
                 pltpu.make_async_copy(
-                    src.at[:, head_lanes(order_ref, h)], dst.at[h], sems.at[h, i]
+                    src.at[:, head_lanes(heads_ref, h)], dst.at[h], sems.at[h, i]
                 )
                 for i, (src, dst) in enumerate(((q_ref, q_in), (k_ref, k_in), (v_ref, v_in)))
             ]
@@ -179,15 +178,15 @@
         scratch_shapes=[held, held, held, pltpu.SemaphoreType.DMA((2, 3))],
         compiler_params=params(),
         cost_estimate=cost(8 * rows * rows * HD, 8 * rows * HD * 4),
-    )(order, q, k, v, bias, *after)
-
-
-def other_half(order, q, kv, bias, o, m, l, after):
+    )(heads, q, k, v, bias, *after)
+
+
+def other_half(heads, q, kv, bias, o, m, l, after):
     rows = q.shape[0]
     tile = 256
 
     def body(
-        order_ref, q_ref, kv_ref, bias_ref, o_ref, m_ref, l_ref, *refs
+        heads_ref, q_ref, kv_ref, bias_ref, o_ref, m_ref, l_ref, *refs
     ):
         out_ref, q_in, k_in, v_in, sems = refs[-5:]
         copies = [
@@ -195,7 +194,7 @@
                 pltpu.make_async_copy(src, dst.at[h], sems.at[h, i])
                 for i, (src, dst) in enumerate(
                     (
-                        (q_ref.at[:, head_lanes(order_ref, h)], q_in),
+                        (q_ref.at[:, head_lanes(heads_ref, h)], q_in),
                         (kv_ref.at[:, h * HD : (h + 1) * HD], k_in),
                         (kv_ref.at[:, (2 + h) * HD : (3 + h) * HD], v_in),
                     )
@@ -230,7 +229,7 @@
         scratch_shapes=[held, held, held, pltpu.SemaphoreType.DMA((2, 3))],
         compiler_params=params(),
         cost_estimate=cost(8 * rows * rows * HD, 8 * rows * HD * 4),
-    )(order, q, kv, bias, o, m, l, *after)
+    )(heads, q, kv, bias, o, m, l, *after)
 
 
 def time_attention(owned, rule, place, after):
@@ -261,7 +260,7 @@
     )(owned, rule, place, *after)
 
 
-def join(*blocks, after=()):
+def join(*blocks):
     rows = [b.shape[0] for b in blocks]
     width = blocks[0].shape[1]
 
@@ -275,11 +274,11 @@
     return pl.pallas_call(
         body,
         out_shape=jax.ShapeDtypeStruct((sum(rows), width), BF16),
-        in_specs=[vmem()] * len(blocks) + [anywhere()] * len(after),
+        in_specs=[vmem()] * len(blocks),
         out_specs=vmem(),
         compiler_params=params(),
         cost_estimate=cost(0, 4 * sum(rows) * width),
-    )(*blocks, *after)
+    )(*blocks)
 
 
 def gate(blocks, after):
@@ -428,43 +427,12 @@
     q, k, v = query_states[0], key_states[0], value_states[0]
     weight = out_weight.T
 
-    W_MODE, T = CFG["w"], CFG
-    heads = temporal_heads
-    if CFG["pick"] == "all":
-        kv, packed, w_own = pick(
-            heads,
-            [
-                [(k, 0), (k, 1), (v, 0), (v, 1)],
-                [(q, 2), (k, 2), (v, 2)],
-                [(weight, n) for n in range(heads_here)],
-            ],
-        )
-    elif CFG["pick"] == "kvw":
-        kv, w_own = pick(
-            heads,
-            [[(k, 0), (k, 1), (v, 0), (v, 1)], [(weight, n) for n in range(heads_here)]],
-        )
-    elif CFG["pick"] == "kvt":
-        kv, packed = pick(
-            heads, [[(k, 0), (k, 1), (v, 0), (v, 1)], [(q, 2), (k, 2), (v, 2)]]
-        )
-        w_own = None
-    elif CFG["pick"] == "timew":
-        packed, w_own = pick(
-            heads,
-            [[(q, 2), (k, 2), (v, 2)], [(weight, n) for n in range(heads_here)]],
-        )
-
-    def swap(move):
-        route = []
-        for y in range(ys):
-            for z in range(zs):
-                for x in range(xs):
-                    for c in range(cores):
-                        here = (y * zs + z) * xs * cores + x * cores + c
-                        there = (x * zs + move(z)) * xs * cores + y * cores + c
-                        route.append((here, there))
-        return route
+    def along_x(block):
+        parts = [block]
+        for step in range(1, xs):
+            route = [(h, (h + step * cores) % (xs * cores)) for h in range(xs * cores)]
+            parts.append(lax.ppermute(block, "head", route))
+        return parts
 
     def along_y(block, step):
         route = [(s, (s + step * zs) % seq_count) for s in range(seq_count)]
@@ -474,109 +442,19 @@
         route = [(s, s // zs * zs + (s + step) % zs) for s in range(seq_count)]
         return lax.ppermute(block, "seq", route)
 
+    swap = []
+    for y in range(ys):
+        for z in range(zs):
+            for x in range(xs):
+                for c in range(cores):
+                    here = (y * zs + z) * xs * cores + x * cores + c
+                    there = (x * zs + z) * xs * cores + y * cores + c
+                    swap.append((here, there))
+
     y_index, z_index = seq_index // zs, seq_index % zs
-    got = {}
-
-    def make_w(w_own=w_own):
-        if W_MODE == "pair":
-            w_two = join(
-                lax.ppermute(w_own, ("seq", "head"), swap(lambda z: z)),
-                lax.ppermute(w_own, ("seq", "head"), swap(lambda z: z ^ 1)),
-                after=toks("w_two"),
-            )
-            got["w_two"] = w_two
-            steps = (0, 2, zs - 2, 4)
-            got["z"] = [w_two, *[along_z(w_two, step) for step in steps[1:]]]
-            return jnp.stack(
-                [((z_index + zs - step) % zs) ^ flip for step in steps for flip in (0, 1)]
-            ).astype(jnp.int32)
-        if W_MODE == "direct":
-            got["z"] = [
-                lax.ppermute(w_own, ("seq", "head"), swap(lambda z, n=n: (z + n) % zs))
-                for n in range(zs)
-            ]
-            return jnp.stack([(z_index + zs - n) % zs for n in range(zs)]).astype(jnp.int32)
-        if w_own is None:
-            (w_own,) = pick(heads, [[(weight, n) for n in range(heads_here)]], toks("w"))
-        if W_MODE == "zlast2":
-            first = lax.ppermute(w_own, ("seq", "head"), swap(lambda z: z))
-            got["first"] = first
-            got["w_two"] = join(*[first] + [along_y(first, n) for n in range(1, ys)])
-            got["up"], got["down"] = [got["w_two"]], [got["w_two"]]
-        if W_MODE == "zlast":
-            spread = []
-            for step in range(ys):
-                route = []
-                for y in range(ys):
-                    for z in range(zs):
-                        for x in range(xs):
-                            for c in range(cores):
-                                here = (y * zs + z) * xs * cores + x * cores + c
-                                to = ((x + step) % ys * zs + z) * xs * cores + y * cores + c
-                                route.append((here, to))
-                spread.append(lax.ppermute(w_own, ("seq", "head"), route))
-            got["w_two"] = join(*spread, after=toks("w_two"))
-            got["up"], got["down"] = [got["w_two"]], [got["w_two"]]
-        if W_MODE == "ring":
-            first = lax.ppermute(w_own, ("seq", "head"), swap(lambda z: z))
-            got["w_two"] = first
-            got["up"], got["down"] = [first], [first]
-            ring_step()
-
-    def ring_step():
-        n = len(got["up"])
-        if CFG["after"].get(f"r{n}"):
-            if n == zs // 2:
-                (got["up"][-1],) = gate([got["up"][-1]], toks(f"r{n}"))
-            else:
-                got["up"][-1], got["down"][-1] = gate(
-                    [got["up"][-1], got["down"][-1]], toks(f"r{n}")
-                )
-        got["up"].append(along_z(got["up"][-1], 1))
-        got[f"up{n}"] = got["up"][-1]
-        if n < zs // 2:
-            got["down"].append(along_z(got["down"][-1], -1))
-        else:
-            up, down = got["up"], got["down"]
-            got["z"] = [up[0], up[1], down[1], *up[2:], *down[2:]]
-
-    def w_order():
-        order = [0, 1, zs - 1, *range(2, zs // 2 + 1)] + [zs - n for n in range(2, zs // 2)]
-        return jnp.stack([(z_index + zs - n) % zs for n in order]).astype(jnp.int32)
-
-    def make_wz():
-        z = got["z"]
-        if CFG.get("split"):
-            got["w_n"] = join(*z[: CFG["split"]], after=toks("w_n"))
-            got["w_z"] = join(*z[CFG["split"] :], after=toks("w_z"))
-            got["groups"] = [got["w_n"], got["w_z"]]
-        else:
-            got["w_z"] = join(*z, after=toks("w_z"))
-            got["groups"] = [got["w_z"]]
-
-    def toks(name):
-        return [token(got[n]) if n in CFG.get("tok", ()) else got[n] for n in CFG["after"].get(name, ())]
-
-    def make_kv():
-        if CFG["pick"] in ("all", "kvw", "kvt"):
-            block = kv
-        else:
-            (block,) = pick(heads, [[(k, 0), (k, 1), (v, 0), (v, 1)]], toks("kv"))
-        got["kv"] = block
-        got["kv_other"] = lax.ppermute(block, "seq", [(s, s ^ 1) for s in range(seq_count)])
-
     positions = rows // seq_count
-
-    def make_time():
-        if CFG["pick"] in ("all", "timew", "kvt"):
-            block = packed
-        else:
-            (block,) = pick(heads, [[(q, 2), (k, 2), (v, 2)]], toks("packed"))
-        got["packed"] = block
-        owned = lax.all_to_all(
-            block.reshape(seq_count, positions, 3 * HD), "seq", 0, 0, tiled=True
-        )
-        got["owned"] = owned.reshape(rows, 3 * HD)
+    heads = temporal_heads
+    kv, packed = pick(heads, [[(k, 0), (k, 1), (v, 0), (v, 1)], [(q, 2), (k, 2), (v, 2)]])
 
     parity = seq_index % 2
     mine = lax.dynamic_slice(
@@ -601,50 +479,38 @@
     key_hot = index[:, None] % (2 * positions) == np.arange(2 * positions)[None, :]
     place = jnp.asarray(np.concatenate([frame_hot, key_hot], axis=1), BF16)
     rule = jnp.concatenate([rule, jnp.asarray(key_hot.T, BF16)], axis=0)
-    def along_x(block):
-        got = [block]
-        for step in range(1, xs):
-            route = [(h, (h + step * cores) % (xs * cores)) for h in range(xs * cores)]
-            got.append(lax.ppermute(block, "head", route))
-        return got
-
-    def make_x():
-        got["parts"] = along_x(got["spat"])
-        got["x1"], got["x2"], got["x3"] = got["parts"][1:]
-
-    def make_own():
-        got["o"], got["m"], got["l"] = own_half(heads, q, k, v, bias, toks("own"))
-        got["own"] = got["l"]
-
-    def make_spat():
-        got["spat"] = other_half(
-            heads, q, got["kv_other"], bias, got["o"], got["m"], got["l"], toks("spat")
-        )
-
-    def make_att():
-        got["time"] = time_attention(got["owned"], rule, place, toks("time"))
-        back = lax.all_to_all(
-            got["time"].reshape(seq_count, positions, HD), "seq", 0, 0, tiled=True
-        )
-        got["returned"] = back.reshape(rows, HD)
-
-    steps = dict(
-        x=make_x, wz=make_wz, kv=make_kv, packed=make_time, own=make_own, spat=make_spat, time=make_att
-    )
-    for name in CFG["order"]:
-        if name == "w":
-            make_w()
-        elif name == "r":
-            ring_step()
-        else:
-            steps[name]()
+
+    kv_other = lax.ppermute(kv, "seq", [(s, s ^ 1) for s in range(seq_count)])
+    owned = lax.all_to_all(packed.reshape(seq_count, positions, 3 * HD), "seq", 0, 0, tiled=True)
+    owned = owned.reshape(rows, 3 * HD)
+
+    (w_own,) = pick(heads, [[(weight, n) for n in range(heads_here)]], [kv])
+    first = lax.ppermute(w_own, ("seq", "head"), swap)
+    w_y = join(*[first] + [along_y(first, n) for n in range(1, ys)])
+    o, m, l = own_half(heads, q, k, v, bias, [token(first)])
+    up, down = [w_y, along_z(w_y, 1)], [w_y, along_z(w_y, -1)]
+
+    spat = other_half(heads, q, kv_other, bias, o, m, l, [])
+    spat_parts = along_x(spat)
+    time = time_attention(owned, rule, place, [token(spat)])
+    returned = lax.all_to_all(time.reshape(seq_count, positions, HD), "seq", 0, 0, tiled=True)
+    returned = returned.reshape(rows, HD)
+
+    for after in ([time], spat_parts[1:]):
+        up[-1], down[-1] = gate([up[-1], down[-1]], after)
+        up.append(along_z(up[-1], 1))
+        down.append(along_z(down[-1], -1))
+    (down[-1],) = gate([down[-1]], [token(returned)])
+    down.append(along_z(down[-1], -1))
+    pieces = [*up, *down[1:]]
+    moved = [*range(zs // 2), *[zs - n for n in range(1, zs // 2 + 1)]]
+    starts = jnp.stack([(z_index + zs - n) % zs for n in moved]).astype(jnp.int32)
     w_blocks = jnp.stack([(y_index + ys - n) % ys for n in range(ys)]).astype(jnp.int32)
-    w_all = gather_weight(w_blocks, w_order(), got["z"], toks("gather"))
-    spat, returned = got["spat"], got["returned"]
+    w_all = gather_weight(w_blocks, starts, pieces, [])
 
     which = ((x_index + xs - jnp.arange(xs)) % xs).astype(jnp.int32)
     side = core.astype(jnp.int32).reshape(1)
-    base_twin, base_own = project_spatial(which, side, got["parts"], w_all)
+    base_twin, base_own = project_spatial(which, side, spat_parts, w_all)
     time_parts = along_x(returned)
     for_twin = project_time(which, 1 - side, time_parts, w_all, base_twin, BF16)
     from_twin = lax.ppermute(for_twin, "head", [(h, h ^ 1) for h in range(xs * cores)])

time: 93.8 us -> 93.5 us (level)
  starting transfers between devices: 50.3 us -> 51.6 us
  waiting for transfers between devices: 18.1 us -> 17.1 us
    ppermute x7, waiting for transfers between devices: 6.49 us -> 2.3 us  [along_z(): return lax.ppermute(block, 'seq', route)]
    ppermute x8, waiting for transfers between devices: 3.99 us -> 6.02 us  [the longest x6 6.02 us: along_x(): parts.append(lax.ppermute(block, 'head', route))]
    ppermute x7, starting transfers between devices: 9.34 us -> 10.8 us  [along_z(): return lax.ppermute(block, 'seq', route)]
    all_to_all x2, waiting for transfers between devices: 4.32 us -> 5.53 us  [the longest x1 5.52 us: shards(): lax.all_to_all(time.reshape(seq_count, positions, HD), 'seq', 0, 0, tiled...]
  transfers between devices with their start and end apart: 21 -> 21, of which waited for: 8 -> 8; matrix products, arithmetic and copies ran while one was open for 1% -> 1% of each run, Pallas kernels for 18% -> 17%
where the time goes in v4:
time: 93.5 us; the launch traced here: 93 us
  starting transfers between devices  51.6 us (55%)
  Pallas kernels  21 us (22%)
  waiting for transfers between devices  17.1 us (18%)
  local copies, waits for them, and re-layouts  1.73 us (2%)
  between operations  1.19 us (1%)
    all_to_all x1, starting transfers between devices, shards(): lax.all_to_all(packed.reshape(seq_count, positions, 3 * HD), 'seq', 0, 0,...  13.4 us
    ppermute x7, starting transfers between devices, along_z(): return lax.ppermute(block, 'seq', route)  10.8 us
    all_to_all x1, starting transfers between devices, shards(): lax.all_to_all(time.reshape(seq_count, positions, HD), 'seq', 0, 0, tiled...  8.45 us
    ppermute x6, starting transfers between devices, along_x(): parts.append(lax.ppermute(block, 'head', route))  7.47 us
    ppermute x6, waiting for transfers between devices, along_x(): parts.append(lax.ppermute(block, 'head', route))  6.02 us
    all_to_all x1, waiting for transfers between devices, shards(): lax.all_to_all(time.reshape(seq_count, positions, HD), 'seq', 0, 0, tiled...  5.52 us
    ppermute x3, starting transfers between devices, along_y(): return lax.ppermute(block, 'seq', route)  4.82 us
    pallas_call x1, Pallas kernels, other_half(): pl.pallas_call(body, out_shape=jax.ShapeDtypeStruct((rows, 2 * HD), BF16)...  4.15 us
  transfers between devices with their start and end apart: 21, of which 8 were waited for; matrix products, arithmetic and copies ran while one was open for 1% of the time, Pallas kernels for 17%

profile of v4, /device:TPU:1, one launch (start us, length us, event | category | flops | bytes accessed | tf_op | source)
XLA Modules:
  0.0 93.0 jit_solution(10595696206017208254)
XLA Ops:
  0.7 2.5 %shard_map.100 = (bf16[768,512]{1,0:T(8,128)(2,1)}, bf16[768,384]{1,0:T(8,128)(2,1)}) custom-call(s32[1]{0:T(128)S(6)} %copy.32.heads_ref, bf16[768,384]{1,0:T(8,128)(2,1)} %bitcast.43, bf16[768,384]{1,0:T(8,128)(2,1)} %bitcast.45, bf16[768,384]{1,0:T(8,128)(2,1)} %bitcast.39), custom_call_target="tpu_custom_call" | custom-call | bytes 2752 | tf_op jit(solution)/shard_map/pallas_call | solution.py:104
  3.3 2.6 %collective-permute-start = (bf16[768,512]{1,0:T(8,128)(2,1)}, bf16[768,512]{1,0:T(8,128)(2,1)}, u32[]{:S(2)}, u32[]{:S(2)}) collective-permute-start(bf16[768,512]{1,0:T(8,128)(2,1)} %get-tuple-element.17.refs_1_), channel_id=1, source_target_pairs={{0,8},{8,0},{16,24},{24,16},{32,40},{40,32},{48,56},{56,48},{64,72... | collective-permute-start | bytes 2359304 | tf_op jit(solution)/shard_map/ppermute | solution.py:483
  5.8 1.4 %shard_map.101 = bf16[96,384]{1,0:T(8,128)(2,1)} custom-call(s32[1]{0:T(128)S(6)} %copy.32.heads_ref, bf16[96,384]{1,0:T(8,128)(2,1)} %bitcast.58, bf16[768,512]{1,0:T(8,128)(2,1)} %get-tuple-element.17.refs_1_), custom_call_target="tpu_custom_call" | custom-call | bytes 147 | tf_op jit(solution)/shard_map/pallas_call | solution.py:104
  7.3 1.5 %collective-permute-start.1 = (bf16[96,384]{1,0:T(8,128)(2,1)}, bf16[96,384]{1,0:T(8,128)(2,1)S(1)}, u32[]{:S(2)}, u32[]{:S(2)}) collective-permute-start(bf16[96,384]{1,0:T(8,128)(2,1)} %shard_map.101), channel_id=1, source_target_pairs={{0,0},{1,1},{2,64},{3,65},{4,128},{5,129},{6,192},{7,193},{8,8},{9... | collective-permute-start | bytes 221192 | tf_op jit(solution)/shard_map/ppermute | solution.py:488
  8.8 13.4 %all-to-all-start = ((bf16[32,24,384]{2,1,0:T(8,128)(2,1)}), bf16[32,24,384]{2,1,0:T(8,128)(2,1)S(1)}, u32[]{:S(2)}, u32[]{:S(2)}) async-start(bf16[32,24,384]{2,1,0:T(8,128)(2,1)} %bitcast.55), calls=%async_computation | async-start | bytes 1179648 | tf_op jit(solution)/shard_map/all_to_all | solution.py:484
  22.5 1.2 %collective-permute-start.5 = (bf16[96,384]{1,0:T(8,128)(2,1)S(1)}, bf16[96,384]{1,0:T(8,128)(2,1)S(1)}, u32[]{:S(2)}, u32[]{:S(2)}) collective-permute-start(bf16[96,384]{1,0:T(8,128)(2,1)S(1)} %collective-permute-done.1.refs_0_), channel_id=1, source_target_pairs={{0,64},{8,72},{16,80},{24,88},{32,96},{40,104},{48,112},{56,120},{... | collective-permute-start | bytes 221192 | tf_op jit(solution)/shard_map/ppermute | solution.py:439
  23.7 2.4 %collective-permute-start.6 = (bf16[96,384]{1,0:T(8,128)(2,1)S(1)}, bf16[96,384]{1,0:T(8,128)(2,1)S(1)}, u32[]{:S(2)}, u32[]{:S(2)}) collective-permute-start(bf16[96,384]{1,0:T(8,128)(2,1)S(1)} %collective-permute-done.1.refs_0_), channel_id=1, source_target_pairs={{0,128},{8,136},{16,144},{24,152},{32,160},{40,168},{48,176},{56,1... | collective-permute-start | bytes 221192 | tf_op jit(solution)/shard_map/ppermute | solution.py:439
  26.1 1.1 %collective-permute-start.7 = (bf16[96,384]{1,0:T(8,128)(2,1)S(1)}, bf16[96,384]{1,0:T(8,128)(2,1)S(1)}, u32[]{:S(2)}, u32[]{:S(2)}) collective-permute-start(bf16[96,384]{1,0:T(8,128)(2,1)S(1)} %collective-permute-done.1.refs_0_), channel_id=1, source_target_pairs={{0,192},{8,200},{16,208},{24,216},{32,224},{40,232},{48,240},{56,2... | collective-permute-start | bytes 221192 | tf_op jit(solution)/shard_map/ppermute | solution.py:439
  27.8 2.7 %collective-permute-done.6.refs_2_ = bf16[96,384]{1,0:T(8,128)(2,1)S(1)} collective-permute-done((bf16[96,384]{1,0:T(8,128)(2,1)S(1)}, bf16[96,384]{1,0:T(8,128)(2,1)S(1)}, u32[]{:S(2)}, u32[]{:S(2)}) %collective-permute-start.6) | collective-permute-done | bytes 73760 | tf_op jit(solution)/shard_map/ppermute | solution.py:439
  30.8 2.1 %collective-permute-start.8 = (bf16[384,384]{1,0:T(8,128)(2,1)S(1)}, bf16[384,384]{1,0:T(8,128)(2,1)S(1)}, u32[]{:S(2)}, u32[]{:S(2)}) collective-permute-start(bf16[384,384]{1,0:T(8,128)(2,1)S(1)} %shard_map.105.refs_0_), channel_id=1, source_target_pairs={{0,8},{8,16},{16,24},{24,32},{32,40},{40,48},{48,56},{56,0},{64,72... | collective-permute-start | bytes 884744 | tf_op jit(solution)/shard_map/ppermute | solution.py:443
  32.9 1.9 %collective-permute-start.9 = (bf16[384,384]{1,0:T(8,128)(2,1)S(1)}, bf16[384,384]{1,0:T(8,128)(2,1)S(1)}, u32[]{:S(2)}, u32[]{:S(2)}) collective-permute-start(bf16[384,384]{1,0:T(8,128)(2,1)S(1)} %shard_map.105.refs_0_), channel_id=1, source_target_pairs={{0,56},{8,0},{16,8},{24,16},{32,24},{40,32},{48,40},{56,48},{64,12... | collective-permute-start | bytes 884744 | tf_op jit(solution)/shard_map/ppermute | solution.py:443
  35.1 3.1 %shard_map.102 = (f32[2,128,768]{2,1,0:T(8,128)S(1)}, f32[2,768]{1,0:T(2,128)S(1)}, f32[2,768]{1,0:T(2,128)S(1)}) custom-call(s32[1]{0:T(128)S(6)} %copy.32.heads_ref, bf16[768,384]{1,0:T(8,128)(2,1)S(1)} %bitcast.40, bf16[768,384]{1,0:T(8,128)(2,1)S(1)} %bitcast.44, bf16[768,384]{1,0:T(8,128)(2,1)S(1)} %bitcast.46, f32[12,768]{1,0:T(8,128)S(1)} %bitcast.53, ...), custom_call_target="tpu_custom_call" | custom-call | flops 603979 | bytes 3145 | tf_op jit(solution)/shard_map/pallas_call | solution.py:173
  38.3 4.2 %shard_map.103.refs_0_ = bf16[768,256]{1,0:T(8,128)(2,1)S(1)} custom-call(s32[1]{0:T(128)S(6)} %copy.32.heads_ref, bf16[768,384]{1,0:T(8,128)(2,1)S(1)} %bitcast.41, bf16[768,512]{1,0:T(8,128)(2,1)} %collective-permute-done.kv_ref, f32[12,768]{1,0:T(8,128)S(1)} %bitcast.54, f32[2,128,768]{2,1,0:T(8,128)S(1)} %get-tuple-element.18.o_ref, ...), custom_call_target="tpu_custom_call" | custom-call | flops 603979 | bytes 3145 | tf_op jit(solution)/shard_map/pallas_call | solution.py:224
  43.3 1.5 %collective-permute-start.13 = (bf16[768,256]{1,0:T(8,128)(2,1)S(1)}, bf16[768,256]{1,0:T(8,128)(2,1)S(1)}, u32[]{:S(2)}, u32[]{:S(2)}) collective-permute-start(bf16[768,256]{1,0:T(8,128)(2,1)S(1)} %shard_map.103.refs_0_), channel_id=1, source_target_pairs={{0,4},{1,5},{2,6},{3,7},{4,0},{5,1},{6,2},{7,3},{8,12},{9,13},{10,... | collective-permute-start | bytes 1179656 | tf_op jit(solution)/shard_map/ppermute | solution.py:434
  44.8 1.0 %collective-permute-start.14 = (bf16[768,256]{1,0:T(8,128)(2,1)S(1)}, bf16[768,256]{1,0:T(8,128)(2,1)S(1)}, u32[]{:S(2)}, u32[]{:S(2)}) collective-permute-start(bf16[768,256]{1,0:T(8,128)(2,1)S(1)} %shard_map.103.refs_0_), channel_id=1, source_target_pairs={{0,6},{1,7},{2,0},{3,1},{4,2},{5,3},{6,4},{7,5},{8,14},{9,15},{10,... | collective-permute-start | bytes 1179656 | tf_op jit(solution)/shard_map/ppermute | solution.py:434
  45.8 0.9 copy-done.4
  46.7 2.4 %shard_map.104.refs_2_ = bf16[768,128]{1,0:T(8,128)(2,1)} custom-call(bf16[768,384]{1,0:T(8,128)(2,1)S(1)} %bitcast.42, bf16[64,768]{1,0:T(8,128)(2,1)S(1)} %pad_maximum_fusion.rule_ref, bf16[768,64]{1,0:T(8,128)(2,1)S(1)} %copy-done.4, bf16[16,128]{1,0:T(8,128)(2,1)S(1)} %slice.23.refs_0_), custom_call_target="tpu_custom_call" | custom-call | flops 301989 | bytes 786 | tf_op jit(solution)/shard_map/pallas_call | solution.py:253
  49.2 2.7 %collective-permute-start.11 = (bf16[384,384]{1,0:T(8,128)(2,1)S(1)}, bf16[384,384]{1,0:T(8,128)(2,1)S(1)}, u32[]{:S(2)}, u32[]{:S(2)}) collective-permute-start(bf16[384,384]{1,0:T(8,128)(2,1)S(1)} %get-tuple-element.22.refs_4_), channel_id=1, source_target_pairs={{0,56},{8,0},{16,8},{24,16},{32,24},{40,32},{48,40},{56,48},{64,12... | collective-permute-start | bytes 884744 | tf_op jit(solution)/shard_map/ppermute | solution.py:443
  51.9 8.4 %all-to-all-start.1 = ((bf16[32,24,128]{2,1,0:T(8,128)(2,1)}), bf16[32,24,128]{2,1,0:T(8,128)(2,1)S(1)}, u32[]{:S(2)}, u32[]{:S(2)}) async-start(bf16[32,24,128]{2,1,0:T(8,128)(2,1)} %bitcast.13), calls=%async_computation.1 | async-start | bytes 393216 | tf_op jit(solution)/shard_map/all_to_all | solution.py:496
  60.4 2.4 %collective-permute-done.14.refs_4_.refs_3_ = bf16[768,256]{1,0:T(8,128)(2,1)S(1)} collective-permute-done((bf16[768,256]{1,0:T(8,128)(2,1)S(1)}, bf16[768,256]{1,0:T(8,128)(2,1)S(1)}, u32[]{:S(2)}, u32[]{:S(2)}) %collective-permute-start.14) | collective-permute-done | bytes 393248 | tf_op jit(solution)/shard_map/ppermute | solution.py:434
  62.8 1.4 %collective-permute-start.16 = (bf16[384,384]{1,0:T(8,128)(2,1)S(1)}, bf16[384,384]{1,0:T(8,128)(2,1)}, u32[]{:S(2)}, u32[]{:S(2)}) collective-permute-start(bf16[384,384]{1,0:T(8,128)(2,1)S(1)} %get-tuple-element.24.refs_5_), channel_id=1, source_target_pairs={{0,56},{8,0},{16,8},{24,16},{32,24},{40,32},{48,40},{56,48},{64,12... | collective-permute-start | bytes 884744 | tf_op jit(solution)/shard_map/ppermute | solution.py:443
  64.2 5.5 %all-to-all-done.1 = bf16[32,24,128]{2,1,0:T(8,128)(2,1)S(1)} async-done(((bf16[32,24,128]{2,1,0:T(8,128)(2,1)}), bf16[32,24,128]{2,1,0:T(8,128)(2,1)S(1)}, u32[]{:S(2)}, u32[]{:S(2)}) %all-to-all-start.1) | async-done | bytes 196640 | tf_op jit(solution)/shard_map/all_to_all | solution.py:496
  69.8 2.2 %collective-permute-done.16.refs_0_ = bf16[384,384]{1,0:T(8,128)(2,1)} collective-permute-done((bf16[384,384]{1,0:T(8,128)(2,1)S(1)}, bf16[384,384]{1,0:T(8,128)(2,1)}, u32[]{:S(2)}, u32[]{:S(2)}) %collective-permute-start.16) | collective-permute-done | bytes 294944 | tf_op jit(solution)/shard_map/ppermute | solution.py:443
  71.9 2.7 %collective-permute-start.17 = (bf16[384,384]{1,0:T(8,128)(2,1)}, bf16[384,384]{1,0:T(8,128)(2,1)}, u32[]{:S(2)}, u32[]{:S(2)}) collective-permute-start(bf16[384,384]{1,0:T(8,128)(2,1)} %shard_map.108.refs_6_), channel_id=1, source_target_pairs={{0,56},{8,0},{16,8},{24,16},{32,24},{40,32},{48,40},{56,48},{64,12... | collective-permute-start | bytes 884744 | tf_op jit(solution)/shard_map/ppermute | solution.py:443
  74.7 1.1 %collective-permute-start.2 = (bf16[768,128]{1,0:T(8,128)(2,1)S(1)}, bf16[768,128]{1,0:T(8,128)(2,1)S(1)}, u32[]{:S(2)}, u32[]{:S(2)}) collective-permute-start(bf16[768,128]{1,0:T(8,128)(2,1)S(1)} %bitcast.48), channel_id=1, source_target_pairs={{0,2},{1,3},{2,4},{3,5},{4,6},{5,7},{6,0},{7,1},{8,10},{9,11},{10,... | collective-permute-start | bytes 589832 | tf_op jit(solution)/shard_map/ppermute | solution.py:434
  75.8 3.1 %collective-permute-start.3 = (bf16[768,128]{1,0:T(8,128)(2,1)S(1)}, bf16[768,128]{1,0:T(8,128)(2,1)S(1)}, u32[]{:S(2)}, u32[]{:S(2)}) collective-permute-start(bf16[768,128]{1,0:T(8,128)(2,1)S(1)} %bitcast.49), channel_id=1, source_target_pairs={{0,4},{1,5},{2,6},{3,7},{4,0},{5,1},{6,2},{7,3},{8,12},{9,13},{10,... | collective-permute-start | bytes 589832 | tf_op jit(solution)/shard_map/ppermute | solution.py:434
  79.0 1.4 %shard_map.109.refs_4_ = bf16[4,768,384]{2,1,0:T(8,128)(2,1)S(1)} custom-call(s32[4]{0:T(128)S(1)} %pad_add_fusion.block_ref, s32[8]{0:T(128)S(1)} %stack.55.row_ref, bf16[384,384]{1,0:T(8,128)(2,1)S(1)} %shard_map.105.refs_0_, bf16[384,384]{1,0:T(8,128)(2,1)S(1)} %get-tuple-element.21.refs_1_, bf16[384,384]{1,0:T(8,128)(2,1)S(1)} %get-tuple-element.23.refs_2_, ...), custom_call_target="tpu_custom_call" | custom-call | bytes 4718 | tf_op jit(solution)/shard_map/pallas_call | solution.py:313
  80.4 2.4 %shard_map.110 = (f32[768,384]{1,0:T(8,128)S(1)}, f32[768,384]{1,0:T(8,128)S(1)}) custom-call(s32[4]{0:T(128)S(1)} %and_select_fusion.1.which_ref, s32[1]{0:T(128)} %bitcast.side_ref, bf16[768,256]{1,0:T(8,128)(2,1)S(1)} %shard_map.103.refs_0_, bf16[768,256]{1,0:T(8,128)(2,1)S(1)} %collective-permute-done.12.refs_2_.refs_1_, ...), custom_call_target="tpu_custom_call" | custom-call | flops 1207959 | bytes 3538 | tf_op jit(solution)/shard_map/pallas_call | solution.py:342
  82.8 3.6 %collective-permute-done.3.refs_2_ = bf16[768,128]{1,0:T(8,128)(2,1)S(1)} collective-permute-done((bf16[768,128]{1,0:T(8,128)(2,1)S(1)}, bf16[768,128]{1,0:T(8,128)(2,1)S(1)}, u32[]{:S(2)}, u32[]{:S(2)}) %collective-permute-start.3) | collective-permute-done | bytes 196640 | tf_op jit(solution)/shard_map/ppermute | solution.py:434
  86.4 1.3 %shard_map.112 = bf16[768,384]{1,0:T(8,128)(2,1)S(1)} custom-call(s32[4]{0:T(128)S(1)} %and_select_fusion.1.which_ref, s32[1]{0:T(128)S(6)} %sub.71.side_ref, bf16[768,128]{1,0:T(8,128)(2,1)S(1)} %bitcast.51, bf16[768,128]{1,0:T(8,128)(2,1)S(1)} %collective-permute-done.2.refs_1_, bf16[768,128]{1,0:T(8,128)(2,1)S(1)} %collective-permute-done.3.refs_2_, ...), custom_call_target="tpu_custom_call" | custom-call | flops 301989 | bytes 1769 | tf_op jit(solution)/shard_map/pallas_call | solution.py:370
  87.7 2.6 %collective-permute-start.18 = (bf16[768,384]{1,0:T(8,128)(2,1)S(1)}, bf16[768,384]{1,0:T(8,128)(2,1)S(1)}, u32[]{:S(2)}, u32[]{:S(2)}) collective-permute-start(bf16[768,384]{1,0:T(8,128)(2,1)S(1)} %shard_map.112), channel_id=1, source_target_pairs={{0,1},{1,0},{2,3},{3,2},{4,5},{5,4},{6,7},{7,6},{8,9},{9,8},{10,11... | collective-permute-start | bytes 1769480 | tf_op jit(solution)/shard_map/ppermute | solution.py:516
  90.3 1.3 %shard_map.111.own_ref = f32[768,384]{1,0:T(8,128)S(1)} custom-call(s32[4]{0:T(128)S(1)} %and_select_fusion.1.which_ref, s32[1]{0:T(128)} %bitcast.side_ref, bf16[768,128]{1,0:T(8,128)(2,1)S(1)} %bitcast.52, bf16[768,128]{1,0:T(8,128)(2,1)S(1)} %collective-permute-done.2.refs_1_, bf16[768,128]{1,0:T(8,128)(2,1)S(1)} %collective-permute-done.3.refs_2_, ...), custom_call_target="tpu_custom_call" | custom-call | flops 301989 | bytes 1769 | tf_op jit(solution)/shard_map/pallas_call | solution.py:370
  (62 shorter events, 3.7 us)
Async XLA Ops:
  0.0 22.3 %copy-start = (s32[16,12,12]{2,0,1:T(8,128)S(1)}, s32[16,12,12]{2,0,1:T(8,128)}, u32[]{:S(2)}) copy-start(s32[16,12,12]{2,0,1:T(8,128)} %param.13) | copy-start | bytes 27652
  3.2 19.0 %copy-start.5 = (s32[12,16,16]{2,1,0:T(8,128)S(1)}, s32[12,16,16]{2,1,0:T(8,128)}, u32[]{:S(2)}) copy-start(s32[12,16,16]{2,1,0:T(8,128)} %param.14) | copy-start | bytes 36868
  3.3 24.0 %copy-start.7 = (s32[48]{0:T(128)S(1)}, s32[48]{0:T(128)}, u32[]{:S(2)}) copy-start(s32[48]{0:T(128)} %constant.184.clone) | copy-start | bytes 580
  3.3 35.0 %collective-permute-start = (bf16[768,512]{1,0:T(8,128)(2,1)}, bf16[768,512]{1,0:T(8,128)(2,1)}, u32[]{:S(2)}, u32[]{:S(2)}) collective-permute-start(bf16[768,512]{1,0:T(8,128)(2,1)} %get-tuple-element.17.refs_1_), channel_id=1, source_target_pairs={{0,8},{8,0},{16,24},{24,16},{32,40},{40,32},{48,56},{56,48},{64,72... | collective-permute-start | bytes 2359304 | tf_op jit(solution)/shard_map/ppermute | solution.py:483
  7.3 15.2 %collective-permute-start.1 = (bf16[96,384]{1,0:T(8,128)(2,1)}, bf16[96,384]{1,0:T(8,128)(2,1)S(1)}, u32[]{:S(2)}, u32[]{:S(2)}) collective-permute-start(bf16[96,384]{1,0:T(8,128)(2,1)} %shard_map.101), channel_id=1, source_target_pairs={{0,0},{1,1},{2,64},{3,65},{4,128},{5,129},{6,192},{7,193},{8,8},{9... | collective-permute-start | bytes 221192 | tf_op jit(solution)/shard_map/ppermute | solution.py:488
  8.8 26.3 %copy-start.1 = (bf16[1,768,384]{2,1,0:T(8,128)(2,1)S(1)}, bf16[1,768,384]{2,1,0:T(8,128)(2,1)}, u32[]{:S(2)}) copy-start(bf16[1,768,384]{2,1,0:T(8,128)(2,1)} %param.10) | copy-start | bytes 1769476
  8.8 26.3 %copy-start.2 = (bf16[1,768,384]{2,1,0:T(8,128)(2,1)S(1)}, bf16[1,768,384]{2,1,0:T(8,128)(2,1)}, u32[]{:S(2)}) copy-start(bf16[1,768,384]{2,1,0:T(8,128)(2,1)} %param.11) | copy-start | bytes 1769476
  8.8 26.3 %copy-start.3 = (bf16[1,768,384]{2,1,0:T(8,128)(2,1)S(1)}, bf16[1,768,384]{2,1,0:T(8,128)(2,1)}, u32[]{:S(2)}) copy-start(bf16[1,768,384]{2,1,0:T(8,128)(2,1)} %param.12) | copy-start | bytes 1769476
  8.8 37.0 %all-to-all-start = ((bf16[32,24,384]{2,1,0:T(8,128)(2,1)}), bf16[32,24,384]{2,1,0:T(8,128)(2,1)S(1)}, u32[]{:S(2)}, u32[]{:S(2)}) async-start(bf16[32,24,384]{2,1,0:T(8,128)(2,1)} %bitcast.55), calls=%async_computation | async-start | bytes 1179648 | tf_op jit(solution)/shard_map/all_to_all | solution.py:484
  22.5 5.3 %collective-permute-start.5 = (bf16[96,384]{1,0:T(8,128)(2,1)S(1)}, bf16[96,384]{1,0:T(8,128)(2,1)S(1)}, u32[]{:S(2)}, u32[]{:S(2)}) collective-permute-start(bf16[96,384]{1,0:T(8,128)(2,1)S(1)} %collective-permute-done.1.refs_0_), channel_id=1, source_target_pairs={{0,64},{8,72},{16,80},{24,88},{32,96},{40,104},{48,112},{56,120},{... | collective-permute-start | bytes 221192 | tf_op jit(solution)/shard_map/ppermute | solution.py:439
  23.7 6.8 %collective-permute-start.6 = (bf16[96,384]{1,0:T(8,128)(2,1)S(1)}, bf16[96,384]{1,0:T(8,128)(2,1)S(1)}, u32[]{:S(2)}, u32[]{:S(2)}) collective-permute-start(bf16[96,384]{1,0:T(8,128)(2,1)S(1)} %collective-permute-done.1.refs_0_), channel_id=1, source_target_pairs={{0,128},{8,136},{16,144},{24,152},{32,160},{40,168},{48,176},{56,1... | collective-permute-start | bytes 221192 | tf_op jit(solution)/shard_map/ppermute | solution.py:439
  26.1 4.6 %collective-permute-start.7 = (bf16[96,384]{1,0:T(8,128)(2,1)S(1)}, bf16[96,384]{1,0:T(8,128)(2,1)S(1)}, u32[]{:S(2)}, u32[]{:S(2)}) collective-permute-start(bf16[96,384]{1,0:T(8,128)(2,1)S(1)} %collective-permute-done.1.refs_0_), channel_id=1, source_target_pairs={{0,192},{8,200},{16,208},{24,216},{32,224},{40,232},{48,240},{56,2... | collective-permute-start | bytes 221192 | tf_op jit(solution)/shard_map/ppermute | solution.py:439
  30.8 18.4 %collective-permute-start.8 = (bf16[384,384]{1,0:T(8,128)(2,1)S(1)}, bf16[384,384]{1,0:T(8,128)(2,1)S(1)}, u32[]{:S(2)}, u32[]{:S(2)}) collective-permute-start(bf16[384,384]{1,0:T(8,128)(2,1)S(1)} %shard_map.105.refs_0_), channel_id=1, source_target_pairs={{0,8},{8,16},{16,24},{24,32},{32,40},{40,48},{48,56},{56,0},{64,72... | collective-permute-start | bytes 884744 | tf_op jit(solution)/shard_map/ppermute | solution.py:443
  32.9 16.3 %collective-permute-start.9 = (bf16[384,384]{1,0:T(8,128)(2,1)S(1)}, bf16[384,384]{1,0:T(8,128)(2,1)S(1)}, u32[]{:S(2)}, u32[]{:S(2)}) collective-permute-start(bf16[384,384]{1,0:T(8,128)(2,1)S(1)} %shard_map.105.refs_0_), channel_id=1, source_target_pairs={{0,56},{8,0},{16,8},{24,16},{32,24},{40,32},{48,40},{56,48},{64,12... | collective-permute-start | bytes 884744 | tf_op jit(solution)/shard_map/ppermute | solution.py:443
  38.3 7.5 %copy-start.6 = (bf16[48,768]{1,0:T(8,128)(2,1)S(1)}, bf16[48,768]{1,0:T(8,128)(2,1)}, u32[]{:S(2)}) copy-start(bf16[48,768]{1,0:T(8,128)(2,1)} %constant.186.clone) | copy-start | bytes 221188
  42.4 17.9 %collective-permute-start.12 = (bf16[768,256]{1,0:T(8,128)(2,1)S(1)}, bf16[768,256]{1,0:T(8,128)(2,1)S(1)}, u32[]{:S(2)}, u32[]{:S(2)}) collective-permute-start(bf16[768,256]{1,0:T(8,128)(2,1)S(1)} %shard_map.103.refs_0_), channel_id=1, source_target_pairs={{0,2},{1,3},{2,4},{3,5},{4,6},{5,7},{6,0},{7,1},{8,10},{9,11},{10,... | collective-permute-start | bytes 1179656 | tf_op jit(solution)/shard_map/ppermute | solution.py:434
  43.3 17.1 %collective-permute-start.13 = (bf16[768,256]{1,0:T(8,128)(2,1)S(1)}, bf16[768,256]{1,0:T(8,128)(2,1)S(1)}, u32[]{:S(2)}, u32[]{:S(2)}) collective-permute-start(bf16[768,256]{1,0:T(8,128)(2,1)S(1)} %shard_map.103.refs_0_), channel_id=1, source_target_pairs={{0,4},{1,5},{2,6},{3,7},{4,0},{5,1},{6,2},{7,3},{8,12},{9,13},{10,... | collective-permute-start | bytes 1179656 | tf_op jit(solution)/shard_map/ppermute | solution.py:434
  44.8 17.9 %collective-permute-start.14 = (bf16[768,256]{1,0:T(8,128)(2,1)S(1)}, bf16[768,256]{1,0:T(8,128)(2,1)S(1)}, u32[]{:S(2)}, u32[]{:S(2)}) collective-permute-start(bf16[768,256]{1,0:T(8,128)(2,1)S(1)} %shard_map.103.refs_0_), channel_id=1, source_target_pairs={{0,6},{1,7},{2,0},{3,1},{4,2},{5,3},{6,4},{7,5},{8,14},{9,15},{10,... | collective-permute-start | bytes 1179656 | tf_op jit(solution)/shard_map/ppermute | solution.py:434
  45.8 0.9 %copy-start.4 = (bf16[768,64]{1,0:T(8,128)(2,1)S(1)}, bf16[768,64]{1,0:T(8,128)(2,1)}, u32[]{:S(2)}) copy-start(bf16[768,64]{1,0:T(8,128)(2,1)} %constant.185.clone.place_ref) | copy-start | bytes 294916
  49.2 13.5 %collective-permute-start.10 = (bf16[384,384]{1,0:T(8,128)(2,1)S(1)}, bf16[384,384]{1,0:T(8,128)(2,1)S(1)}, u32[]{:S(2)}, u32[]{:S(2)}) collective-permute-start(bf16[384,384]{1,0:T(8,128)(2,1)S(1)} %get-tuple-element.21.refs_1_), channel_id=1, source_target_pairs={{0,8},{8,16},{16,24},{24,32},{32,40},{40,48},{48,56},{56,0},{64,72... | collective-permute-start | bytes 884744 | tf_op jit(solution)/shard_map/ppermute | solution.py:443
  49.2 13.5 %collective-permute-start.11 = (bf16[384,384]{1,0:T(8,128)(2,1)S(1)}, bf16[384,384]{1,0:T(8,128)(2,1)S(1)}, u32[]{:S(2)}, u32[]{:S(2)}) collective-permute-start(bf16[384,384]{1,0:T(8,128)(2,1)S(1)} %get-tuple-element.22.refs_4_), channel_id=1, source_target_pairs={{0,56},{8,0},{16,8},{24,16},{32,24},{40,32},{48,40},{56,48},{64,12... | collective-permute-start | bytes 884744 | tf_op jit(solution)/shard_map/ppermute | solution.py:443
  51.9 17.9 %all-to-all-start.1 = ((bf16[32,24,128]{2,1,0:T(8,128)(2,1)}), bf16[32,24,128]{2,1,0:T(8,128)(2,1)S(1)}, u32[]{:S(2)}, u32[]{:S(2)}) async-start(bf16[32,24,128]{2,1,0:T(8,128)(2,1)} %bitcast.13), calls=%async_computation.1 | async-start | bytes 393216 | tf_op jit(solution)/shard_map/all_to_all | solution.py:496
  62.8 9.2 %collective-permute-start.16 = (bf16[384,384]{1,0:T(8,128)(2,1)S(1)}, bf16[384,384]{1,0:T(8,128)(2,1)}, u32[]{:S(2)}, u32[]{:S(2)}) collective-permute-start(bf16[384,384]{1,0:T(8,128)(2,1)S(1)} %get-tuple-element.24.refs_5_), channel_id=1, source_target_pairs={{0,56},{8,0},{16,8},{24,16},{32,24},{40,32},{48,40},{56,48},{64,12... | collective-permute-start | bytes 884744 | tf_op jit(solution)/shard_map/ppermute | solution.py:443
  64.1 14.8 %collective-permute-start.15 = (bf16[384,384]{1,0:T(8,128)(2,1)S(1)}, bf16[384,384]{1,0:T(8,128)(2,1)}, u32[]{:S(2)}, u32[]{:S(2)}) collective-permute-start(bf16[384,384]{1,0:T(8,128)(2,1)S(1)} %get-tuple-element.23.refs_2_), channel_id=1, source_target_pairs={{0,8},{8,16},{16,24},{24,32},{32,40},{40,48},{48,56},{56,0},{64,72... | collective-permute-start | bytes 884744 | tf_op jit(solution)/shard_map/ppermute | solution.py:443
  71.9 7.1 %collective-permute-start.17 = (bf16[384,384]{1,0:T(8,128)(2,1)}, bf16[384,384]{1,0:T(8,128)(2,1)}, u32[]{:S(2)}, u32[]{:S(2)}) collective-permute-start(bf16[384,384]{1,0:T(8,128)(2,1)} %shard_map.108.refs_6_), channel_id=1, source_target_pairs={{0,56},{8,0},{16,8},{24,16},{32,24},{40,32},{48,40},{56,48},{64,12... | collective-permute-start | bytes 884744 | tf_op jit(solution)/shard_map/ppermute | solution.py:443
  74.7 8.1 %collective-permute-start.2 = (bf16[768,128]{1,0:T(8,128)(2,1)S(1)}, bf16[768,128]{1,0:T(8,128)(2,1)S(1)}, u32[]{:S(2)}, u32[]{:S(2)}) collective-permute-start(bf16[768,128]{1,0:T(8,128)(2,1)S(1)} %bitcast.48), channel_id=1, source_target_pairs={{0,2},{1,3},{2,4},{3,5},{4,6},{5,7},{6,0},{7,1},{8,10},{9,11},{10,... | collective-permute-start | bytes 589832 | tf_op jit(solution)/shard_map/ppermute | solution.py:434
  75.8 10.6 %collective-permute-start.3 = (bf16[768,128]{1,0:T(8,128)(2,1)S(1)}, bf16[768,128]{1,0:T(8,128)(2,1)S(1)}, u32[]{:S(2)}, u32[]{:S(2)}) collective-permute-start(bf16[768,128]{1,0:T(8,128)(2,1)S(1)} %bitcast.49), channel_id=1, source_target_pairs={{0,4},{1,5},{2,6},{3,7},{4,0},{5,1},{6,2},{7,3},{8,12},{9,13},{10,... | collective-permute-start | bytes 589832 | tf_op jit(solution)/shard_map/ppermute | solution.py:434
  78.8 7.6 %collective-permute-start.4 = (bf16[768,128]{1,0:T(8,128)(2,1)S(1)}, bf16[768,128]{1,0:T(8,128)(2,1)S(1)}, u32[]{:S(2)}, u32[]{:S(2)}) collective-permute-start(bf16[768,128]{1,0:T(8,128)(2,1)S(1)} %bitcast.50), channel_id=1, source_target_pairs={{0,6},{1,7},{2,0},{3,1},{4,2},{5,3},{6,4},{7,5},{8,14},{9,15},{10,... | collective-permute-start | bytes 589832 | tf_op jit(solution)/shard_map/ppermute | solution.py:434
  87.7 4.2 %collective-permute-start.18 = (bf16[768,384]{1,0:T(8,128)(2,1)S(1)}, bf16[768,384]{1,0:T(8,128)(2,1)S(1)}, u32[]{:S(2)}, u32[]{:S(2)}) collective-permute-start(bf16[768,384]{1,0:T(8,128)(2,1)S(1)} %shard_map.112), channel_id=1, source_target_pairs={{0,1},{1,0},{2,3},{3,2},{4,5},{5,4},{6,7},{7,6},{8,9},{9,8},{10,11... | collective-permute-start | bytes 1769480 | tf_op jit(solution)/shard_map/ppermute | solution.py:516

commit v5 on v4

--- a/solution.py
+++ b/solution.py
@@ -236,8 +236,18 @@
     rows = owned.shape[0]
     tile = 256
 
-    def body(all_ref, rule_ref, place_ref, *refs):
-        out_ref = refs[-1]
+    def body(owned_ref, rule_ref, place_ref, *refs):
+        out_ref, all_ref, sems = refs[-3:]
+        copies = [
+            pltpu.make_async_copy(
+                owned_ref.at[:, n * HD : (n + 1) * HD],
+                all_ref.at[:, n * HD : (n + 1) * HD],
+                sems.at[n],
+            )
+            for n in range(3)
+        ]
+        start_all(copies)
+        wait_all(copies)
         values = all_ref[:, 2 * HD :].T
         for t in range(rows // tile):
             part = slice(t * tile, (t + 1) * tile)
@@ -253,8 +263,9 @@
     return pl.pallas_call(
         body,
         out_shape=jax.ShapeDtypeStruct((rows, HD), BF16),
-        in_specs=[vmem()] * 3 + [anywhere()] * len(after),
+        in_specs=[anywhere()] + [vmem()] * 2 + [anywhere()] * len(after),
         out_specs=vmem(),
+        scratch_shapes=[pltpu.VMEM((rows, 3 * HD), BF16), pltpu.SemaphoreType.DMA((3,))],
         compiler_params=params(),
         cost_estimate=cost(4 * rows * rows * HD, 8 * rows * HD),
     )(owned, rule, place, *after)

time: 93.5 us -> 93.7 us (level)
  transfers between devices with their start and end apart: 21 -> 21, of which waited for: 8 -> 7; matrix products, arithmetic and copies ran while one was open for 1% -> 1% of each run, Pallas kernels for 17% -> 18%
where the time goes in v5:
time: 93.7 us; the launch traced here: 93.3 us
  starting transfers between devices  51.8 us (55%)
  Pallas kernels  21.1 us (23%)
  waiting for transfers between devices  17.1 us (18%)
  local copies, waits for them, and re-layouts  1.73 us (2%)
  between operations  1.22 us (1%)
    all_to_all x1, starting transfers between devices, shards(): lax.all_to_all(packed.reshape(seq_count, positions, 3 * HD), 'seq', 0, 0,...  13.4 us
    ppermute x7, starting transfers between devices, along_z(): return lax.ppermute(block, 'seq', route)  11 us
    all_to_all x1, starting transfers between devices, shards(): lax.all_to_all(time.reshape(seq_count, positions, HD), 'seq', 0, 0, tiled...  8.45 us
    ppermute x6, starting transfers between devices, along_x(): parts.append(lax.ppermute(block, 'head', route))  7.59 us
    ppermute x6, waiting for transfers between devices, along_x(): parts.append(lax.ppermute(block, 'head', route))  5.99 us
    all_to_all x1, waiting for transfers between devices, shards(): lax.all_to_all(time.reshape(seq_count, positions, HD), 'seq', 0, 0, tiled...  5.85 us
    ppermute x3, starting transfers between devices, along_y(): return lax.ppermute(block, 'seq', route)  4.82 us
    pallas_call x1, Pallas kernels, other_half(): pl.pallas_call(body, out_shape=jax.ShapeDtypeStruct((rows, 2 * HD), BF16)...  4.15 us
  transfers between devices with their start and end apart: 21, of which 7 were waited for; matrix products, arithmetic and copies ran while one was open for 1% of the time, Pallas kernels for 18%

profile of v5, /device:TPU:1, one launch (start us, length us, event | category | flops | bytes accessed | tf_op | source)
XLA Modules:
  0.0 93.3 jit_solution(3737271930910794589)
XLA Ops:
  0.7 2.5 %shard_map.100 = (bf16[768,512]{1,0:T(8,128)(2,1)}, bf16[768,384]{1,0:T(8,128)(2,1)}) custom-call(s32[1]{0:T(128)S(6)} %copy.32.heads_ref, bf16[768,384]{1,0:T(8,128)(2,1)} %bitcast.43, bf16[768,384]{1,0:T(8,128)(2,1)} %bitcast.45, bf16[768,384]{1,0:T(8,128)(2,1)} %bitcast.39), custom_call_target="tpu_custom_call" | custom-call | bytes 2752 | tf_op jit(solution)/shard_map/pallas_call | solution.py:104
  3.3 2.6 %collective-permute-start = (bf16[768,512]{1,0:T(8,128)(2,1)}, bf16[768,512]{1,0:T(8,128)(2,1)}, u32[]{:S(2)}, u32[]{:S(2)}) collective-permute-start(bf16[768,512]{1,0:T(8,128)(2,1)} %get-tuple-element.17.refs_1_), channel_id=1, source_target_pairs={{0,8},{8,0},{16,24},{24,16},{32,40},{40,32},{48,56},{56,48},{64,72... | collective-permute-start | bytes 2359304 | tf_op jit(solution)/shard_map/ppermute | solution.py:494
  5.8 1.4 %shard_map.101 = bf16[96,384]{1,0:T(8,128)(2,1)} custom-call(s32[1]{0:T(128)S(6)} %copy.32.heads_ref, bf16[96,384]{1,0:T(8,128)(2,1)} %bitcast.58, bf16[768,512]{1,0:T(8,128)(2,1)} %get-tuple-element.17.refs_1_), custom_call_target="tpu_custom_call" | custom-call | bytes 147 | tf_op jit(solution)/shard_map/pallas_call | solution.py:104
  7.3 1.5 %collective-permute-start.1 = (bf16[96,384]{1,0:T(8,128)(2,1)}, bf16[96,384]{1,0:T(8,128)(2,1)S(1)}, u32[]{:S(2)}, u32[]{:S(2)}) collective-permute-start(bf16[96,384]{1,0:T(8,128)(2,1)} %shard_map.101), channel_id=1, source_target_pairs={{0,0},{1,1},{2,64},{3,65},{4,128},{5,129},{6,192},{7,193},{8,8},{9... | collective-permute-start | bytes 221192 | tf_op jit(solution)/shard_map/ppermute | solution.py:499
  8.8 13.4 %all-to-all-start = ((bf16[32,24,384]{2,1,0:T(8,128)(2,1)}), bf16[32,24,384]{2,1,0:T(8,128)(2,1)S(1)}, u32[]{:S(2)}, u32[]{:S(2)}) async-start(bf16[32,24,384]{2,1,0:T(8,128)(2,1)} %bitcast.55), calls=%async_computation | async-start | bytes 1179648 | tf_op jit(solution)/shard_map/all_to_all | solution.py:495
  22.5 1.2 %collective-permute-start.5 = (bf16[96,384]{1,0:T(8,128)(2,1)S(1)}, bf16[96,384]{1,0:T(8,128)(2,1)S(1)}, u32[]{:S(2)}, u32[]{:S(2)}) collective-permute-start(bf16[96,384]{1,0:T(8,128)(2,1)S(1)} %collective-permute-done.1.refs_0_), channel_id=1, source_target_pairs={{0,64},{8,72},{16,80},{24,88},{32,96},{40,104},{48,112},{56,120},{... | collective-permute-start | bytes 221192 | tf_op jit(solution)/shard_map/ppermute | solution.py:450
  23.7 2.4 %collective-permute-start.6 = (bf16[96,384]{1,0:T(8,128)(2,1)S(1)}, bf16[96,384]{1,0:T(8,128)(2,1)S(1)}, u32[]{:S(2)}, u32[]{:S(2)}) collective-permute-start(bf16[96,384]{1,0:T(8,128)(2,1)S(1)} %collective-permute-done.1.refs_0_), channel_id=1, source_target_pairs={{0,128},{8,136},{16,144},{24,152},{32,160},{40,168},{48,176},{56,1... | collective-permute-start | bytes 221192 | tf_op jit(solution)/shard_map/ppermute | solution.py:450
  26.1 1.1 %collective-permute-start.7 = (bf16[96,384]{1,0:T(8,128)(2,1)S(1)}, bf16[96,384]{1,0:T(8,128)(2,1)S(1)}, u32[]{:S(2)}, u32[]{:S(2)}) collective-permute-start(bf16[96,384]{1,0:T(8,128)(2,1)S(1)} %collective-permute-done.1.refs_0_), channel_id=1, source_target_pairs={{0,192},{8,200},{16,208},{24,216},{32,224},{40,232},{48,240},{56,2... | collective-permute-start | bytes 221192 | tf_op jit(solution)/shard_map/ppermute | solution.py:450
  27.8 2.7 %collective-permute-done.6.refs_2_ = bf16[96,384]{1,0:T(8,128)(2,1)S(1)} collective-permute-done((bf16[96,384]{1,0:T(8,128)(2,1)S(1)}, bf16[96,384]{1,0:T(8,128)(2,1)S(1)}, u32[]{:S(2)}, u32[]{:S(2)}) %collective-permute-start.6) | collective-permute-done | bytes 73760 | tf_op jit(solution)/shard_map/ppermute | solution.py:450
  30.8 2.1 %collective-permute-start.8 = (bf16[384,384]{1,0:T(8,128)(2,1)S(1)}, bf16[384,384]{1,0:T(8,128)(2,1)S(1)}, u32[]{:S(2)}, u32[]{:S(2)}) collective-permute-start(bf16[384,384]{1,0:T(8,128)(2,1)S(1)} %shard_map.105.refs_0_), channel_id=1, source_target_pairs={{0,8},{8,16},{16,24},{24,32},{32,40},{40,48},{48,56},{56,0},{64,72... | collective-permute-start | bytes 884744 | tf_op jit(solution)/shard_map/ppermute | solution.py:454
  32.9 1.9 %collective-permute-start.9 = (bf16[384,384]{1,0:T(8,128)(2,1)S(1)}, bf16[384,384]{1,0:T(8,128)(2,1)S(1)}, u32[]{:S(2)}, u32[]{:S(2)}) collective-permute-start(bf16[384,384]{1,0:T(8,128)(2,1)S(1)} %shard_map.105.refs_0_), channel_id=1, source_target_pairs={{0,56},{8,0},{16,8},{24,16},{32,24},{40,32},{48,40},{56,48},{64,12... | collective-permute-start | bytes 884744 | tf_op jit(solution)/shard_map/ppermute | solution.py:454
  35.1 3.1 %shard_map.102 = (f32[2,128,768]{2,1,0:T(8,128)S(1)}, f32[2,768]{1,0:T(2,128)S(1)}, f32[2,768]{1,0:T(2,128)S(1)}) custom-call(s32[1]{0:T(128)S(6)} %copy.32.heads_ref, bf16[768,384]{1,0:T(8,128)(2,1)S(1)} %bitcast.40, bf16[768,384]{1,0:T(8,128)(2,1)S(1)} %bitcast.44, bf16[768,384]{1,0:T(8,128)(2,1)S(1)} %bitcast.46, f32[12,768]{1,0:T(8,128)S(1)} %bitcast.53, ...), custom_call_target="tpu_custom_call" | custom-call | flops 603979 | bytes 3145 | tf_op jit(solution)/shard_map/pallas_call | solution.py:173
  38.3 4.2 %shard_map.103.refs_0_ = bf16[768,256]{1,0:T(8,128)(2,1)S(1)} custom-call(s32[1]{0:T(128)S(6)} %copy.32.heads_ref, bf16[768,384]{1,0:T(8,128)(2,1)S(1)} %bitcast.41, bf16[768,512]{1,0:T(8,128)(2,1)} %collective-permute-done.kv_ref, f32[12,768]{1,0:T(8,128)S(1)} %bitcast.54, f32[2,128,768]{2,1,0:T(8,128)S(1)} %get-tuple-element.18.o_ref, ...), custom_call_target="tpu_custom_call" | custom-call | flops 603979 | bytes 3145 | tf_op jit(solution)/shard_map/pallas_call | solution.py:224
  43.3 1.5 %collective-permute-start.13 = (bf16[768,256]{1,0:T(8,128)(2,1)S(1)}, bf16[768,256]{1,0:T(8,128)(2,1)S(1)}, u32[]{:S(2)}, u32[]{:S(2)}) collective-permute-start(bf16[768,256]{1,0:T(8,128)(2,1)S(1)} %shard_map.103.refs_0_), channel_id=1, source_target_pairs={{0,4},{1,5},{2,6},{3,7},{4,0},{5,1},{6,2},{7,3},{8,12},{9,13},{10,... | collective-permute-start | bytes 1179656 | tf_op jit(solution)/shard_map/ppermute | solution.py:445
  44.8 1.0 %collective-permute-start.14 = (bf16[768,256]{1,0:T(8,128)(2,1)S(1)}, bf16[768,256]{1,0:T(8,128)(2,1)S(1)}, u32[]{:S(2)}, u32[]{:S(2)}) collective-permute-start(bf16[768,256]{1,0:T(8,128)(2,1)S(1)} %shard_map.103.refs_0_), channel_id=1, source_target_pairs={{0,6},{1,7},{2,0},{3,1},{4,2},{5,3},{6,4},{7,5},{8,14},{9,15},{10,... | collective-permute-start | bytes 1179656 | tf_op jit(solution)/shard_map/ppermute | solution.py:445
  45.8 0.9 copy-done.4
  46.7 2.6 %shard_map.104.refs_2_ = bf16[768,128]{1,0:T(8,128)(2,1)} custom-call(bf16[768,384]{1,0:T(8,128)(2,1)S(1)} %bitcast.42, bf16[64,768]{1,0:T(8,128)(2,1)S(1)} %pad_maximum_fusion.rule_ref, bf16[768,64]{1,0:T(8,128)(2,1)S(1)} %copy-done.4, bf16[16,128]{1,0:T(8,128)(2,1)S(1)} %slice.23.refs_0_), custom_call_target="tpu_custom_call" | custom-call | flops 301989 | bytes 786 | tf_op jit(solution)/shard_map/pallas_call | solution.py:263
  49.5 2.7 %collective-permute-start.11 = (bf16[384,384]{1,0:T(8,128)(2,1)S(1)}, bf16[384,384]{1,0:T(8,128)(2,1)S(1)}, u32[]{:S(2)}, u32[]{:S(2)}) collective-permute-start(bf16[384,384]{1,0:T(8,128)(2,1)S(1)} %get-tuple-element.22.refs_4_), channel_id=1, source_target_pairs={{0,56},{8,0},{16,8},{24,16},{32,24},{40,32},{48,40},{56,48},{64,12... | collective-permute-start | bytes 884744 | tf_op jit(solution)/shard_map/ppermute | solution.py:454
  52.1 8.4 %all-to-all-start.1 = ((bf16[32,24,128]{2,1,0:T(8,128)(2,1)}), bf16[32,24,128]{2,1,0:T(8,128)(2,1)S(1)}, u32[]{:S(2)}, u32[]{:S(2)}) async-start(bf16[32,24,128]{2,1,0:T(8,128)(2,1)} %bitcast.13), calls=%async_computation.1 | async-start | bytes 393216 | tf_op jit(solution)/shard_map/all_to_all | solution.py:507
  60.6 2.2 %collective-permute-done.14.refs_4_.refs_3_ = bf16[768,256]{1,0:T(8,128)(2,1)S(1)} collective-permute-done((bf16[768,256]{1,0:T(8,128)(2,1)S(1)}, bf16[768,256]{1,0:T(8,128)(2,1)S(1)}, u32[]{:S(2)}, u32[]{:S(2)}) %collective-permute-start.14) | collective-permute-done | bytes 393248 | tf_op jit(solution)/shard_map/ppermute | solution.py:445
  62.8 1.4 %collective-permute-start.16 = (bf16[384,384]{1,0:T(8,128)(2,1)S(1)}, bf16[384,384]{1,0:T(8,128)(2,1)}, u32[]{:S(2)}, u32[]{:S(2)}) collective-permute-start(bf16[384,384]{1,0:T(8,128)(2,1)S(1)} %get-tuple-element.24.refs_5_), channel_id=1, source_target_pairs={{0,56},{8,0},{16,8},{24,16},{32,24},{40,32},{48,40},{56,48},{64,12... | collective-permute-start | bytes 884744 | tf_op jit(solution)/shard_map/ppermute | solution.py:454
  64.2 5.8 %all-to-all-done.1 = bf16[32,24,128]{2,1,0:T(8,128)(2,1)S(1)} async-done(((bf16[32,24,128]{2,1,0:T(8,128)(2,1)}), bf16[32,24,128]{2,1,0:T(8,128)(2,1)S(1)}, u32[]{:S(2)}, u32[]{:S(2)}) %all-to-all-start.1) | async-done | bytes 196640 | tf_op jit(solution)/shard_map/all_to_all | solution.py:507
  70.1 1.9 %collective-permute-done.16.refs_0_ = bf16[384,384]{1,0:T(8,128)(2,1)} collective-permute-done((bf16[384,384]{1,0:T(8,128)(2,1)S(1)}, bf16[384,384]{1,0:T(8,128)(2,1)}, u32[]{:S(2)}, u32[]{:S(2)}) %collective-permute-start.16) | collective-permute-done | bytes 294944 | tf_op jit(solution)/shard_map/ppermute | solution.py:454
  72.0 2.8 %collective-permute-start.17 = (bf16[384,384]{1,0:T(8,128)(2,1)}, bf16[384,384]{1,0:T(8,128)(2,1)}, u32[]{:S(2)}, u32[]{:S(2)}) collective-permute-start(bf16[384,384]{1,0:T(8,128)(2,1)} %shard_map.108.refs_6_), channel_id=1, source_target_pairs={{0,56},{8,0},{16,8},{24,16},{32,24},{40,32},{48,40},{56,48},{64,12... | collective-permute-start | bytes 884744 | tf_op jit(solution)/shard_map/ppermute | solution.py:454
  75.7 3.4 %collective-permute-start.3 = (bf16[768,128]{1,0:T(8,128)(2,1)S(1)}, bf16[768,128]{1,0:T(8,128)(2,1)S(1)}, u32[]{:S(2)}, u32[]{:S(2)}) collective-permute-start(bf16[768,128]{1,0:T(8,128)(2,1)S(1)} %bitcast.49), channel_id=1, source_target_pairs={{0,4},{1,5},{2,6},{3,7},{4,0},{5,1},{6,2},{7,3},{8,12},{9,13},{10,... | collective-permute-start | bytes 589832 | tf_op jit(solution)/shard_map/ppermute | solution.py:445
  79.2 1.4 %shard_map.109.refs_4_ = bf16[4,768,384]{2,1,0:T(8,128)(2,1)S(1)} custom-call(s32[4]{0:T(128)S(1)} %pad_add_fusion.block_ref, s32[8]{0:T(128)S(1)} %stack.55.row_ref, bf16[384,384]{1,0:T(8,128)(2,1)S(1)} %shard_map.105.refs_0_, bf16[384,384]{1,0:T(8,128)(2,1)S(1)} %get-tuple-element.21.refs_1_, bf16[384,384]{1,0:T(8,128)(2,1)S(1)} %get-tuple-element.23.refs_2_, ...), custom_call_target="tpu_custom_call" | custom-call | bytes 4718 | tf_op jit(solution)/shard_map/pallas_call | solution.py:324
  80.6 2.4 %shard_map.110 = (f32[768,384]{1,0:T(8,128)S(1)}, f32[768,384]{1,0:T(8,128)S(1)}) custom-call(s32[4]{0:T(128)S(1)} %and_select_fusion.1.which_ref, s32[1]{0:T(128)} %bitcast.side_ref, bf16[768,256]{1,0:T(8,128)(2,1)S(1)} %shard_map.103.refs_0_, bf16[768,256]{1,0:T(8,128)(2,1)S(1)} %collective-permute-done.12.refs_2_.refs_1_, ...), custom_call_target="tpu_custom_call" | custom-call | flops 1207959 | bytes 3538 | tf_op jit(solution)/shard_map/pallas_call | solution.py:353
  82.9 3.8 %collective-permute-done.3.refs_2_ = bf16[768,128]{1,0:T(8,128)(2,1)S(1)} collective-permute-done((bf16[768,128]{1,0:T(8,128)(2,1)S(1)}, bf16[768,128]{1,0:T(8,128)(2,1)S(1)}, u32[]{:S(2)}, u32[]{:S(2)}) %collective-permute-start.3) | collective-permute-done | bytes 196640 | tf_op jit(solution)/shard_map/ppermute | solution.py:445
  86.8 1.3 %shard_map.112 = bf16[768,384]{1,0:T(8,128)(2,1)S(1)} custom-call(s32[4]{0:T(128)S(1)} %and_select_fusion.1.which_ref, s32[1]{0:T(128)S(6)} %sub.71.side_ref, bf16[768,128]{1,0:T(8,128)(2,1)S(1)} %bitcast.51, bf16[768,128]{1,0:T(8,128)(2,1)S(1)} %collective-permute-done.2.refs_1_, bf16[768,128]{1,0:T(8,128)(2,1)S(1)} %collective-permute-done.3.refs_2_, ...), custom_call_target="tpu_custom_call" | custom-call | flops 301989 | bytes 1769 | tf_op jit(solution)/shard_map/pallas_call | solution.py:381
  88.1 2.5 %collective-permute-start.18 = (bf16[768,384]{1,0:T(8,128)(2,1)S(1)}, bf16[768,384]{1,0:T(8,128)(2,1)S(1)}, u32[]{:S(2)}, u32[]{:S(2)}) collective-permute-start(bf16[768,384]{1,0:T(8,128)(2,1)S(1)} %shard_map.112), channel_id=1, source_target_pairs={{0,1},{1,0},{2,3},{3,2},{4,5},{5,4},{6,7},{7,6},{8,9},{9,8},{10,11... | collective-permute-start | bytes 1769480 | tf_op jit(solution)/shard_map/ppermute | solution.py:527
  90.6 1.3 %shard_map.111.own_ref = f32[768,384]{1,0:T(8,128)S(1)} custom-call(s32[4]{0:T(128)S(1)} %and_select_fusion.1.which_ref, s32[1]{0:T(128)} %bitcast.side_ref, bf16[768,128]{1,0:T(8,128)(2,1)S(1)} %bitcast.52, bf16[768,128]{1,0:T(8,128)(2,1)S(1)} %collective-permute-done.2.refs_1_, bf16[768,128]{1,0:T(8,128)(2,1)S(1)} %collective-permute-done.3.refs_2_, ...), custom_call_target="tpu_custom_call" | custom-call | flops 301989 | bytes 1769 | tf_op jit(solution)/shard_map/pallas_call | solution.py:381
  92.2 0.9 shard_map.113
  (62 shorter events, 3.7 us)
Async XLA Ops:
  0.0 22.3 %copy-start = (s32[16,12,12]{2,0,1:T(8,128)S(1)}, s32[16,12,12]{2,0,1:T(8,128)}, u32[]{:S(2)}) copy-start(s32[16,12,12]{2,0,1:T(8,128)} %param.13) | copy-start | bytes 27652
  3.2 19.0 %copy-start.5 = (s32[12,16,16]{2,1,0:T(8,128)S(1)}, s32[12,16,16]{2,1,0:T(8,128)}, u32[]{:S(2)}) copy-start(s32[12,16,16]{2,1,0:T(8,128)} %param.14) | copy-start | bytes 36868
  3.3 24.0 %copy-start.7 = (s32[48]{0:T(128)S(1)}, s32[48]{0:T(128)}, u32[]{:S(2)}) copy-start(s32[48]{0:T(128)} %constant.184.clone) | copy-start | bytes 580
  3.3 35.0 %collective-permute-start = (bf16[768,512]{1,0:T(8,128)(2,1)}, bf16[768,512]{1,0:T(8,128)(2,1)}, u32[]{:S(2)}, u32[]{:S(2)}) collective-permute-start(bf16[768,512]{1,0:T(8,128)(2,1)} %get-tuple-element.17.refs_1_), channel_id=1, source_target_pairs={{0,8},{8,0},{16,24},{24,16},{32,40},{40,32},{48,56},{56,48},{64,72... | collective-permute-start | bytes 2359304 | tf_op jit(solution)/shard_map/ppermute | solution.py:494
  7.3 15.2 %collective-permute-start.1 = (bf16[96,384]{1,0:T(8,128)(2,1)}, bf16[96,384]{1,0:T(8,128)(2,1)S(1)}, u32[]{:S(2)}, u32[]{:S(2)}) collective-permute-start(bf16[96,384]{1,0:T(8,128)(2,1)} %shard_map.101), channel_id=1, source_target_pairs={{0,0},{1,1},{2,64},{3,65},{4,128},{5,129},{6,192},{7,193},{8,8},{9... | collective-permute-start | bytes 221192 | tf_op jit(solution)/shard_map/ppermute | solution.py:499
  8.8 26.3 %copy-start.1 = (bf16[1,768,384]{2,1,0:T(8,128)(2,1)S(1)}, bf16[1,768,384]{2,1,0:T(8,128)(2,1)}, u32[]{:S(2)}) copy-start(bf16[1,768,384]{2,1,0:T(8,128)(2,1)} %param.10) | copy-start | bytes 1769476
  8.8 26.3 %copy-start.2 = (bf16[1,768,384]{2,1,0:T(8,128)(2,1)S(1)}, bf16[1,768,384]{2,1,0:T(8,128)(2,1)}, u32[]{:S(2)}) copy-start(bf16[1,768,384]{2,1,0:T(8,128)(2,1)} %param.11) | copy-start | bytes 1769476
  8.8 26.3 %copy-start.3 = (bf16[1,768,384]{2,1,0:T(8,128)(2,1)S(1)}, bf16[1,768,384]{2,1,0:T(8,128)(2,1)}, u32[]{:S(2)}) copy-start(bf16[1,768,384]{2,1,0:T(8,128)(2,1)} %param.12) | copy-start | bytes 1769476
  8.8 37.0 %all-to-all-start = ((bf16[32,24,384]{2,1,0:T(8,128)(2,1)}), bf16[32,24,384]{2,1,0:T(8,128)(2,1)S(1)}, u32[]{:S(2)}, u32[]{:S(2)}) async-start(bf16[32,24,384]{2,1,0:T(8,128)(2,1)} %bitcast.55), calls=%async_computation | async-start | bytes 1179648 | tf_op jit(solution)/shard_map/all_to_all | solution.py:495
  22.5 5.3 %collective-permute-start.5 = (bf16[96,384]{1,0:T(8,128)(2,1)S(1)}, bf16[96,384]{1,0:T(8,128)(2,1)S(1)}, u32[]{:S(2)}, u32[]{:S(2)}) collective-permute-start(bf16[96,384]{1,0:T(8,128)(2,1)S(1)} %collective-permute-done.1.refs_0_), channel_id=1, source_target_pairs={{0,64},{8,72},{16,80},{24,88},{32,96},{40,104},{48,112},{56,120},{... | collective-permute-start | bytes 221192 | tf_op jit(solution)/shard_map/ppermute | solution.py:450
  23.7 6.8 %collective-permute-start.6 = (bf16[96,384]{1,0:T(8,128)(2,1)S(1)}, bf16[96,384]{1,0:T(8,128)(2,1)S(1)}, u32[]{:S(2)}, u32[]{:S(2)}) collective-permute-start(bf16[96,384]{1,0:T(8,128)(2,1)S(1)} %collective-permute-done.1.refs_0_), channel_id=1, source_target_pairs={{0,128},{8,136},{16,144},{24,152},{32,160},{40,168},{48,176},{56,1... | collective-permute-start | bytes 221192 | tf_op jit(solution)/shard_map/ppermute | solution.py:450
  26.1 4.6 %collective-permute-start.7 = (bf16[96,384]{1,0:T(8,128)(2,1)S(1)}, bf16[96,384]{1,0:T(8,128)(2,1)S(1)}, u32[]{:S(2)}, u32[]{:S(2)}) collective-permute-start(bf16[96,384]{1,0:T(8,128)(2,1)S(1)} %collective-permute-done.1.refs_0_), channel_id=1, source_target_pairs={{0,192},{8,200},{16,208},{24,216},{32,224},{40,232},{48,240},{56,2... | collective-permute-start | bytes 221192 | tf_op jit(solution)/shard_map/ppermute | solution.py:450
  30.8 18.6 %collective-permute-start.8 = (bf16[384,384]{1,0:T(8,128)(2,1)S(1)}, bf16[384,384]{1,0:T(8,128)(2,1)S(1)}, u32[]{:S(2)}, u32[]{:S(2)}) collective-permute-start(bf16[384,384]{1,0:T(8,128)(2,1)S(1)} %shard_map.105.refs_0_), channel_id=1, source_target_pairs={{0,8},{8,16},{16,24},{24,32},{32,40},{40,48},{48,56},{56,0},{64,72... | collective-permute-start | bytes 884744 | tf_op jit(solution)/shard_map/ppermute | solution.py:454
  32.9 16.4 %collective-permute-start.9 = (bf16[384,384]{1,0:T(8,128)(2,1)S(1)}, bf16[384,384]{1,0:T(8,128)(2,1)S(1)}, u32[]{:S(2)}, u32[]{:S(2)}) collective-permute-start(bf16[384,384]{1,0:T(8,128)(2,1)S(1)} %shard_map.105.refs_0_), channel_id=1, source_target_pairs={{0,56},{8,0},{16,8},{24,16},{32,24},{40,32},{48,40},{56,48},{64,12... | collective-permute-start | bytes 884744 | tf_op jit(solution)/shard_map/ppermute | solution.py:454
  38.3 7.5 %copy-start.6 = (bf16[48,768]{1,0:T(8,128)(2,1)S(1)}, bf16[48,768]{1,0:T(8,128)(2,1)}, u32[]{:S(2)}) copy-start(bf16[48,768]{1,0:T(8,128)(2,1)} %constant.186.clone) | copy-start | bytes 221188
  42.4 18.1 %collective-permute-start.12 = (bf16[768,256]{1,0:T(8,128)(2,1)S(1)}, bf16[768,256]{1,0:T(8,128)(2,1)S(1)}, u32[]{:S(2)}, u32[]{:S(2)}) collective-permute-start(bf16[768,256]{1,0:T(8,128)(2,1)S(1)} %shard_map.103.refs_0_), channel_id=1, source_target_pairs={{0,2},{1,3},{2,4},{3,5},{4,6},{5,7},{6,0},{7,1},{8,10},{9,11},{10,... | collective-permute-start | bytes 1179656 | tf_op jit(solution)/shard_map/ppermute | solution.py:445
  43.3 17.3 %collective-permute-start.13 = (bf16[768,256]{1,0:T(8,128)(2,1)S(1)}, bf16[768,256]{1,0:T(8,128)(2,1)S(1)}, u32[]{:S(2)}, u32[]{:S(2)}) collective-permute-start(bf16[768,256]{1,0:T(8,128)(2,1)S(1)} %shard_map.103.refs_0_), channel_id=1, source_target_pairs={{0,4},{1,5},{2,6},{3,7},{4,0},{5,1},{6,2},{7,3},{8,12},{9,13},{10,... | collective-permute-start | bytes 1179656 | tf_op jit(solution)/shard_map/ppermute | solution.py:445
  44.8 17.9 %collective-permute-start.14 = (bf16[768,256]{1,0:T(8,128)(2,1)S(1)}, bf16[768,256]{1,0:T(8,128)(2,1)S(1)}, u32[]{:S(2)}, u32[]{:S(2)}) collective-permute-start(bf16[768,256]{1,0:T(8,128)(2,1)S(1)} %shard_map.103.refs_0_), channel_id=1, source_target_pairs={{0,6},{1,7},{2,0},{3,1},{4,2},{5,3},{6,4},{7,5},{8,14},{9,15},{10,... | collective-permute-start | bytes 1179656 | tf_op jit(solution)/shard_map/ppermute | solution.py:445
  45.8 0.9 copy-start.4
  49.4 13.4 %collective-permute-start.10 = (bf16[384,384]{1,0:T(8,128)(2,1)S(1)}, bf16[384,384]{1,0:T(8,128)(2,1)S(1)}, u32[]{:S(2)}, u32[]{:S(2)}) collective-permute-start(bf16[384,384]{1,0:T(8,128)(2,1)S(1)} %get-tuple-element.21.refs_1_), channel_id=1, source_target_pairs={{0,8},{8,16},{16,24},{24,32},{32,40},{40,48},{48,56},{56,0},{64,72... | collective-permute-start | bytes 884744 | tf_op jit(solution)/shard_map/ppermute | solution.py:454
  49.5 13.3 %collective-permute-start.11 = (bf16[384,384]{1,0:T(8,128)(2,1)S(1)}, bf16[384,384]{1,0:T(8,128)(2,1)S(1)}, u32[]{:S(2)}, u32[]{:S(2)}) collective-permute-start(bf16[384,384]{1,0:T(8,128)(2,1)S(1)} %get-tuple-element.22.refs_4_), channel_id=1, source_target_pairs={{0,56},{8,0},{16,8},{24,16},{32,24},{40,32},{48,40},{56,48},{64,12... | collective-permute-start | bytes 884744 | tf_op jit(solution)/shard_map/ppermute | solution.py:454
  52.1 17.9 %all-to-all-start.1 = ((bf16[32,24,128]{2,1,0:T(8,128)(2,1)}), bf16[32,24,128]{2,1,0:T(8,128)(2,1)S(1)}, u32[]{:S(2)}, u32[]{:S(2)}) async-start(bf16[32,24,128]{2,1,0:T(8,128)(2,1)} %bitcast.13), calls=%async_computation.1 | async-start | bytes 393216 | tf_op jit(solution)/shard_map/all_to_all | solution.py:507
  62.8 9.2 %collective-permute-start.16 = (bf16[384,384]{1,0:T(8,128)(2,1)S(1)}, bf16[384,384]{1,0:T(8,128)(2,1)}, u32[]{:S(2)}, u32[]{:S(2)}) collective-permute-start(bf16[384,384]{1,0:T(8,128)(2,1)S(1)} %get-tuple-element.24.refs_5_), channel_id=1, source_target_pairs={{0,56},{8,0},{16,8},{24,16},{32,24},{40,32},{48,40},{56,48},{64,12... | collective-permute-start | bytes 884744 | tf_op jit(solution)/shard_map/ppermute | solution.py:454
  64.1 15.0 %collective-permute-start.15 = (bf16[384,384]{1,0:T(8,128)(2,1)S(1)}, bf16[384,384]{1,0:T(8,128)(2,1)}, u32[]{:S(2)}, u32[]{:S(2)}) collective-permute-start(bf16[384,384]{1,0:T(8,128)(2,1)S(1)} %get-tuple-element.23.refs_2_), channel_id=1, source_target_pairs={{0,8},{8,16},{16,24},{24,32},{32,40},{40,48},{48,56},{56,0},{64,72... | collective-permute-start | bytes 884744 | tf_op jit(solution)/shard_map/ppermute | solution.py:454
  72.0 7.2 %collective-permute-start.17 = (bf16[384,384]{1,0:T(8,128)(2,1)}, bf16[384,384]{1,0:T(8,128)(2,1)}, u32[]{:S(2)}, u32[]{:S(2)}) collective-permute-start(bf16[384,384]{1,0:T(8,128)(2,1)} %shard_map.108.refs_6_), channel_id=1, source_target_pairs={{0,56},{8,0},{16,8},{24,16},{32,24},{40,32},{48,40},{56,48},{64,12... | collective-permute-start | bytes 884744 | tf_op jit(solution)/shard_map/ppermute | solution.py:454
  74.8 8.1 %collective-permute-start.2 = (bf16[768,128]{1,0:T(8,128)(2,1)S(1)}, bf16[768,128]{1,0:T(8,128)(2,1)S(1)}, u32[]{:S(2)}, u32[]{:S(2)}) collective-permute-start(bf16[768,128]{1,0:T(8,128)(2,1)S(1)} %bitcast.48), channel_id=1, source_target_pairs={{0,2},{1,3},{2,4},{3,5},{4,6},{5,7},{6,0},{7,1},{8,10},{9,11},{10,... | collective-permute-start | bytes 589832 | tf_op jit(solution)/shard_map/ppermute | solution.py:445
  75.7 11.1 %collective-permute-start.3 = (bf16[768,128]{1,0:T(8,128)(2,1)S(1)}, bf16[768,128]{1,0:T(8,128)(2,1)S(1)}, u32[]{:S(2)}, u32[]{:S(2)}) collective-permute-start(bf16[768,128]{1,0:T(8,128)(2,1)S(1)} %bitcast.49), channel_id=1, source_target_pairs={{0,4},{1,5},{2,6},{3,7},{4,0},{5,1},{6,2},{7,3},{8,12},{9,13},{10,... | collective-permute-start | bytes 589832 | tf_op jit(solution)/shard_map/ppermute | solution.py:445
  79.1 7.7 %collective-permute-start.4 = (bf16[768,128]{1,0:T(8,128)(2,1)S(1)}, bf16[768,128]{1,0:T(8,128)(2,1)S(1)}, u32[]{:S(2)}, u32[]{:S(2)}) collective-permute-start(bf16[768,128]{1,0:T(8,128)(2,1)S(1)} %bitcast.50), channel_id=1, source_target_pairs={{0,6},{1,7},{2,0},{3,1},{4,2},{5,3},{6,4},{7,5},{8,14},{9,15},{10,... | collective-permute-start | bytes 589832 | tf_op jit(solution)/shard_map/ppermute | solution.py:445
  88.1 4.1 %collective-permute-start.18 = (bf16[768,384]{1,0:T(8,128)(2,1)S(1)}, bf16[768,384]{1,0:T(8,128)(2,1)S(1)}, u32[]{:S(2)}, u32[]{:S(2)}) collective-permute-start(bf16[768,384]{1,0:T(8,128)(2,1)S(1)} %shard_map.112), channel_id=1, source_target_pairs={{0,1},{1,0},{2,3},{3,2},{4,5},{5,4},{6,7},{7,6},{8,9},{9,8},{10,11... | collective-permute-start | bytes 1769480 | tf_op jit(solution)/shard_map/ppermute | solution.py:527
